TPU v7x, 32 devices: a whole 2x2x4 slice. The times are simulated.
32 devices in a mesh: wide: 8 (over y, x, core), narrow: 4 (over z).
Axes of the slice: x: 2, y: 2, z: 4, core: 2. Of those that a mesh axis runs over, the one named last changes fastest.
Arguments:
- tokens: bfloat16 [4096, 1280], P(('wide', 'narrow')), may hold values from -6 to 6
- seq_ids: int32 [4096], P(('wide', 'narrow')), may hold values from 0 to 4, as said below
- routes: int32 [4096, 7], P(('wide', 'narrow')), may hold values from 0 to 14, all different within a row; in each aligned block of 128 rows (0 to 127, 128 to 255, ...) at most 72 rows name the same one
- cotangent: bfloat16 [4096, 1280], P(('wide', 'narrow')), may hold values from -6 to 6
- gain_attn: bfloat16 [1280], P(('wide', 'narrow')), may hold values from 0.5 to 1.5
- w_qkv: bfloat16 [1280, 3840], P(('wide', 'narrow')), may hold values from -0.15625 to 0.15625
- w_out: bfloat16 [1280, 1280], P(('wide', 'narrow')), may hold values from -2.5 to 2.5
- gain_ffn: bfloat16 [1280], P(('wide', 'narrow')), may hold values from 0.5 to 1.5
- w_router: bfloat16 [1280, 15], P(('wide', 'narrow')), may hold values from -0.078125 to 0.078125
- w_up: bfloat16 [1280, 16, 1792], P(('wide', 'narrow')), may hold values from -0.15625 to 0.15625
- w_down: bfloat16 [1280, 16, 896], P(('wide', 'narrow')), may hold values from -0.75 to 0.75
Outputs:
- output: bfloat16 [4096, 1280], P(('wide', 'narrow'))
- grad_tokens: bfloat16 [4096, 1280], P(('wide', 'narrow'))
- grad_gain_attn: float32 [1280], P('narrow')
- grad_qkv: float32 [1280, 3840], P('narrow')
- grad_out: float32 [1280, 1280], P('narrow')
- grad_gain_ffn: float32 [1280], P('narrow')
- grad_router: float32 [1280, 15], P('narrow')
- grad_up: float32 [1280, 16, 1792], P('narrow')
- grad_down: float32 [1280, 16, 896], P('narrow')
Inputs may be any that keep to these rules, and one draw needn't show every extreme that they name: `seq_ids`: within each sequence of 512 rows the document numbers start at 0, never fall and rise by at most one from row to row. `routes`: each row names 7 different routed experts; among the rows of one device no expert is named more than 72 times.
All inputs are finite; a program needn't handle non-finite values.
Results may differ from a plain program's by a relative error of at most 0.02.
Values may be sent and summed in bfloat16 or wider, within the bound.
A program may use at most 448 MiB of HBM per device.

v0:
```python
import jax
import jax.numpy as jnp
from jax import lax
from jax.sharding import PartitionSpec as P

HEADS = 10
HEAD_DIM = 128
FF = 896
CAP = 72


epsilon = 1e-06


def shortened(x):
    return jax.tree.map(lambda a: a.astype(jnp.bfloat16) if a.dtype == jnp.float32 else a, x)


def rms_inverse(values):
    return lax.rsqrt(jnp.mean(values * values, axis=-1, keepdims=True) + epsilon)


def rotary(positions, head_size):
    half_dim = head_size // 2
    frequency = 10000.0 ** (-jnp.arange(half_dim, dtype=jnp.float32) / half_dim)
    angles = positions[:, None] * frequency[None, :]
    cosine = jnp.concatenate([jnp.cos(angles), jnp.cos(angles)], axis=1)[:, None, :]
    sine_table = jnp.concatenate([jnp.sin(angles), jnp.sin(angles)], axis=1)[:, None, :]
    return (cosine, sine_table)


def rotate(values, cosine, sine_table):
    half_dim = values.shape[-1] // 2
    turned = jnp.concatenate([-values[..., half_dim:], values[..., :half_dim]], axis=-1)
    return values * cosine + turned * sine_table


def rotate_back(grads, cosine, sine_table):
    half_dim = grads.shape[-1] // 2
    scaled = grads * sine_table
    turned = jnp.concatenate([scaled[..., half_dim:], -scaled[..., :half_dim]], axis=-1)
    return grads * cosine + turned


def expert_weight_terms(
    routed_in, routed_grad, shared_in, shared_grad, slot_grads, slot_acts, shared_grads, shared_acts
):
    up_routed = jnp.einsum(
        "ecd,ecf->def", routed_in, slot_grads, preferred_element_type=jnp.float32
    )
    up_shared = jnp.einsum("td,tf->df", shared_in, shared_grads, preferred_element_type=jnp.float32)
    down_routed = jnp.einsum(
        "ecd,ecf->def", routed_grad, slot_acts, preferred_element_type=jnp.float32
    )
    down_shared = jnp.einsum(
        "td,tf->df", shared_grad, shared_acts, preferred_element_type=jnp.float32
    )
    up_all = jnp.concatenate([up_shared[:, None], up_routed], axis=1)
    down_all = jnp.concatenate([down_shared[:, None], down_routed], axis=1)
    combined = jnp.concatenate([up_all, down_all], axis=2)
    return combined.reshape(combined.shape[0], -1)


def local(
    tokens, seq_ids, routes, cotangent, gain_attn, w_qkv, w_out, gain_ffn, w_router, w_up, w_down
):
    row_count = tokens.shape[0]
    model_width = tokens.shape[1]
    query_scale = HEAD_DIM ** (-0.5)
    hidden = FF
    capacity = CAP
    inputs = tokens.astype(jnp.float32)
    gain_one, qkv_weight, out_weight = (
        lax.all_gather(gain_attn, ("wide", "narrow"), axis=0, tiled=True),
        lax.all_gather(w_qkv, ("wide", "narrow"), axis=0, tiled=True),
        lax.all_gather(w_out, ("wide", "narrow"), axis=0, tiled=True),
    )
    inverse_one = rms_inverse(inputs)
    normed_one = inputs * inverse_one
    first_in = (normed_one * gain_one.astype(jnp.float32)).astype(jnp.bfloat16)
    projected = jnp.dot(first_in, qkv_weight, preferred_element_type=jnp.float32)
    offset = lax.axis_index("narrow") * row_count
    query_pos = offset + jnp.arange(row_count, dtype=jnp.int32)
    cosine, sine_table = rotary(query_pos.astype(jnp.float32), HEAD_DIM)
    query_rows = (
        rotate(projected[:, :model_width].reshape(row_count, HEADS, HEAD_DIM), cosine, sine_table)
        * query_scale
    ).astype(jnp.bfloat16)
    key_rows = (
        rotate(
            projected[:, model_width : 2 * model_width].reshape(row_count, HEADS, HEAD_DIM),
            cosine,
            sine_table,
        )
        .astype(jnp.bfloat16)
        .reshape(row_count, model_width)
    )
    value_rows = projected[:, 2 * model_width :].astype(jnp.bfloat16)
    all_keys, all_values, all_ids = (
        lax.all_gather(key_rows, "narrow", axis=0, tiled=True),
        lax.all_gather(value_rows, "narrow", axis=0, tiled=True),
        lax.all_gather(seq_ids.astype(jnp.bfloat16), "narrow", axis=0, tiled=True),
    )
    seqlen = all_keys.shape[0]
    block_len = min(512, seqlen)
    num_blocks = seqlen // block_len
    own_ids = seq_ids.astype(jnp.float32)

    def block_parts(block_index):
        first_row = block_index * block_len
        key_pos = first_row + jnp.arange(block_len, dtype=jnp.int32)
        key_ids = lax.dynamic_slice_in_dim(all_ids, first_row, block_len, 0).astype(jnp.float32)
        allowed = (key_pos[None, :] <= query_pos[:, None]) & (key_ids[None, :] == own_ids[:, None])
        key_block = lax.dynamic_slice_in_dim(all_keys, first_row, block_len, 0).reshape(
            block_len, HEADS, HEAD_DIM
        )
        value_block = lax.dynamic_slice_in_dim(all_values, first_row, block_len, 0).reshape(
            block_len, HEADS, HEAD_DIM
        )
        scores = jnp.einsum(
            "qhd,khd->hqk", query_rows, key_block, preferred_element_type=jnp.float32
        )
        return (allowed[None], key_block, value_block, scores)

    def max_step(state_pair, block_index):
        running_max, running_sum = state_pair
        allowed, key_block, value_block, scores = block_parts(block_index)
        masked = jnp.where(allowed, scores, -1e30)
        new_max = jnp.maximum(running_max, jnp.max(masked, axis=2))
        added = jnp.sum(jnp.where(allowed, jnp.exp(masked - new_max[..., None]), 0.0), axis=2)
        return ((new_max, running_sum * jnp.exp(running_max - new_max) + added), None)

    start_max = jnp.full((HEADS, row_count), -1e30, jnp.float32)
    start_sum = jnp.zeros((HEADS, row_count), jnp.float32)
    (top_score, exp_total), unused = lax.scan(
        max_step, (start_max, start_sum), jnp.arange(num_blocks)
    )
    log_total = top_score + jnp.log(exp_total)

    def out_step(accum, block_index):
        allowed, key_block, value_block, scores = block_parts(block_index)
        weights_low = jnp.where(allowed, jnp.exp(scores - log_total[..., None]), 0.0).astype(
            jnp.bfloat16
        )
        return (
            accum
            + jnp.einsum(
                "hqk,khd->hqd", weights_low, value_block, preferred_element_type=jnp.float32
            ),
            None,
        )

    accum_start = jnp.zeros((HEADS, row_count, HEAD_DIM), jnp.float32)
    mixed_heads, unused = lax.scan(out_step, accum_start, jnp.arange(num_blocks))
    mixed_exact = jnp.transpose(mixed_heads, (1, 0, 2))
    mixed = mixed_exact.reshape(row_count, model_width).astype(jnp.bfloat16)
    middle = inputs + jnp.dot(mixed, out_weight, preferred_element_type=jnp.float32)
    gain_two, router_weight, up_weight, down_weight = (
        lax.all_gather(gain_ffn, ("wide", "narrow"), axis=0, tiled=True),
        lax.all_gather(w_router, ("wide", "narrow"), axis=0, tiled=True),
        lax.all_gather(w_up, ("wide", "narrow"), axis=0, tiled=True),
        lax.all_gather(w_down, ("wide", "narrow"), axis=0, tiled=True),
    )
    inverse_two = rms_inverse(middle)
    normed_two = middle * inverse_two
    second_in = (normed_two * gain_two.astype(jnp.float32)).astype(jnp.bfloat16)
    logits = jnp.dot(second_in, router_weight, preferred_element_type=jnp.float32)
    router_probs = jax.nn.softmax(logits, axis=-1)
    experts = logits.shape[1]
    choose = routes[:, :, None] == jnp.arange(experts, dtype=jnp.int32)[None, None, :]
    member = jnp.sum(choose.astype(jnp.float32), axis=1)
    earlier = (jnp.arange(row_count)[:, None] > jnp.arange(row_count)[None, :]).astype(jnp.bfloat16)
    before = jnp.dot(earlier, member.astype(jnp.bfloat16), preferred_element_type=jnp.float32)
    slot_hit = (member.T[:, None, :] > 0.5) & (
        before.T[:, None, :] == jnp.arange(capacity, dtype=jnp.float32)[None, :, None]
    )
    dispatch = slot_hit.astype(jnp.bfloat16)
    gathered_in = jnp.einsum(
        "ect,td->ecd", dispatch, second_in, preferred_element_type=jnp.float32
    ).astype(jnp.bfloat16)
    gate_weights = router_probs * member
    gate_up = jnp.einsum(
        "ecd,def->ecf", gathered_in, up_weight[:, 1:], preferred_element_type=jnp.float32
    )
    gate_part = gate_up[..., :hidden]
    up_part = gate_up[..., hidden:]
    activated = (jax.nn.silu(gate_part) * up_part).astype(jnp.bfloat16)
    expert_rows = jnp.einsum(
        "ecf,def->ecd", activated, down_weight[:, 1:], preferred_element_type=jnp.float32
    ).astype(jnp.bfloat16)
    selected = jnp.einsum("ect,ecd->etd", dispatch, expert_rows, preferred_element_type=jnp.float32)
    routed = jnp.sum(gate_weights.T[:, :, None] * selected, axis=0)
    shared_up = jnp.dot(second_in, up_weight[:, 0], preferred_element_type=jnp.float32)
    shared_gate = shared_up[:, :hidden]
    shared_lin = shared_up[:, hidden:]
    shared_act = (jax.nn.silu(shared_gate) * shared_lin).astype(jnp.bfloat16)
    shared_out = jnp.einsum(
        "tf,df->td", shared_act, down_weight[:, 0], preferred_element_type=jnp.float32
    )
    output = (middle + shared_out + routed).astype(jnp.bfloat16)
    gain_two, router_weight, up_weight, down_weight = (
        lax.all_gather(gain_ffn, ("wide", "narrow"), axis=0, tiled=True),
        lax.all_gather(w_router, ("wide", "narrow"), axis=0, tiled=True),
        lax.all_gather(w_up, ("wide", "narrow"), axis=0, tiled=True),
        lax.all_gather(w_down, ("wide", "narrow"), axis=0, tiled=True),
    )
    grad_output = cotangent.astype(jnp.float32)
    slot_token = jnp.sum(
        jnp.where(slot_hit, jnp.arange(row_count, dtype=jnp.int32)[None, None, :], 0), axis=2
    )
    slot_gate = jnp.sum(jnp.where(slot_hit, gate_weights.T[:, None, :], 0.0), axis=2)
    grad_rows = (slot_gate[..., None] * grad_output[slot_token]).astype(jnp.bfloat16)
    grad_probs = jnp.sum(selected * grad_output[None], axis=2).T * member
    grad_logits = (
        router_probs * (grad_probs - jnp.sum(router_probs * grad_probs, axis=1, keepdims=True))
    ).astype(jnp.bfloat16)
    grad_act = jnp.einsum(
        "ecd,def->ecf", grad_rows, down_weight[:, 1:], preferred_element_type=jnp.float32
    )
    sigmoid_gate = jax.nn.sigmoid(gate_part)
    grad_gate_up = jnp.concatenate(
        [
            grad_act * up_part * sigmoid_gate * (1.0 + gate_part * (1.0 - sigmoid_gate)),
            grad_act * jax.nn.silu(gate_part),
        ],
        axis=-1,
    ).astype(jnp.bfloat16)
    grad_gathered = jnp.einsum(
        "ecf,def->ecd", grad_gate_up, up_weight[:, 1:], preferred_element_type=jnp.float32
    )
    slot_index = jnp.sum(jnp.where(choose, before[:, None, :], 0.0), axis=2).astype(jnp.int32)
    flat_index = routes * capacity + slot_index
    grad_second = jnp.sum(grad_gathered.reshape(-1, model_width)[flat_index], axis=1)
    grad_shared_act = jnp.einsum(
        "td,df->tf", cotangent, down_weight[:, 0], preferred_element_type=jnp.float32
    )
    sigmoid_shared = jax.nn.sigmoid(shared_gate)
    grad_shared_up = jnp.concatenate(
        [
            grad_shared_act
            * shared_lin
            * sigmoid_shared
            * (1.0 + shared_gate * (1.0 - sigmoid_shared)),
            grad_shared_act * jax.nn.silu(shared_gate),
        ],
        axis=-1,
    ).astype(jnp.bfloat16)
    grad_second = grad_second + jnp.einsum(
        "tf,df->td", grad_shared_up, up_weight[:, 0], preferred_element_type=jnp.float32
    )
    grad_second = grad_second + jnp.einsum(
        "te,de->td", grad_logits, router_weight, preferred_element_type=jnp.float32
    )
    grad_normed_two = grad_second * gain_two.astype(jnp.float32)
    grad_gain_two = jnp.sum(grad_second * normed_two, axis=0)
    grad_middle = grad_output + inverse_two * (
        grad_normed_two
        - normed_two * jnp.mean(grad_normed_two * normed_two, axis=-1, keepdims=True)
    )
    grad_router = jnp.einsum(
        "td,te->de", second_in, grad_logits, preferred_element_type=jnp.float32
    )
    narrow_rows = model_width // lax.axis_size("narrow")
    routed_cols, grad_cols, shared_cols, cotangent_cols = (
        lax.all_to_all(gathered_in, "narrow", split_axis=2, concat_axis=1, tiled=True),
        lax.all_to_all(grad_rows, "narrow", split_axis=2, concat_axis=1, tiled=True),
        lax.all_to_all(second_in[None], "narrow", split_axis=2, concat_axis=1, tiled=True),
        lax.all_to_all(cotangent[None], "narrow", split_axis=2, concat_axis=1, tiled=True),
    )
    slot_grads, slot_acts, shared_grads, shared_acts = (
        lax.all_gather(grad_gate_up, "narrow", axis=1, tiled=True),
        lax.all_gather(activated, "narrow", axis=1, tiled=True),
        lax.all_gather(grad_shared_up[None], "narrow", axis=1, tiled=True),
        lax.all_gather(shared_act[None], "narrow", axis=1, tiled=True),
    )
    expert_grads = expert_weight_terms(
        routed_cols,
        grad_cols,
        shared_cols[0],
        cotangent_cols[0],
        slot_grads,
        slot_acts,
        shared_grads[0],
        shared_acts[0],
    )
    gain_one, qkv_weight, out_weight = (
        lax.all_gather(gain_attn, ("wide", "narrow"), axis=0, tiled=True),
        lax.all_gather(w_qkv, ("wide", "narrow"), axis=0, tiled=True),
        lax.all_gather(w_out, ("wide", "narrow"), axis=0, tiled=True),
    )
    grad_attention = grad_middle.astype(jnp.bfloat16)
    grad_out_weight = jnp.einsum(
        "td,te->de", mixed, grad_attention, preferred_element_type=jnp.float32
    )
    grad_mixed = jnp.einsum(
        "te,de->td", grad_attention, out_weight, preferred_element_type=jnp.float32
    ).astype(jnp.bfloat16)
    grad_heads = grad_mixed.reshape(row_count, HEADS, HEAD_DIM)
    row_delta = jnp.sum(grad_heads.astype(jnp.float32) * mixed_exact, axis=2).T

    def back_step(grad_query, block_index):
        allowed, key_block, value_block, scores = block_parts(block_index)
        weights_exact = jnp.where(allowed, jnp.exp(scores - log_total[..., None]), 0.0)
        weights_low = weights_exact.astype(jnp.bfloat16)
        grad_value = jnp.einsum(
            "hqk,qhd->khd", weights_low, grad_heads, preferred_element_type=jnp.float32
        )
        grad_weights = jnp.einsum(
            "qhd,khd->hqk", grad_heads, value_block, preferred_element_type=jnp.float32
        )
        grad_scores = (weights_exact * (grad_weights - row_delta[..., None])).astype(jnp.bfloat16)
        grad_query = grad_query + jnp.einsum(
            "hqk,khd->qhd", grad_scores, key_block, preferred_element_type=jnp.float32
        )
        grad_key = jnp.einsum(
            "hqk,qhd->khd", grad_scores, query_rows, preferred_element_type=jnp.float32
        )
        return (
            grad_query,
            (grad_key.reshape(block_len, model_width), grad_value.reshape(block_len, model_width)),
        )

    query_start = jnp.zeros((row_count, HEADS, HEAD_DIM), jnp.float32)
    grad_query, (key_blocks, value_blocks) = lax.scan(
        back_step, query_start, jnp.arange(num_blocks)
    )
    key_partial = key_blocks.reshape(seqlen, model_width)
    value_partial = value_blocks.reshape(seqlen, model_width)
    grad_keys, grad_values = (
        lax.psum_scatter(
            key_partial.astype(jnp.bfloat16), "narrow", scatter_dimension=0, tiled=True
        ).astype(jnp.float32),
        lax.psum_scatter(
            value_partial.astype(jnp.bfloat16), "narrow", scatter_dimension=0, tiled=True
        ).astype(jnp.float32),
    )
    grad_query_raw = rotate_back(grad_query, cosine, sine_table) * query_scale
    grad_key_raw = rotate_back(grad_keys.reshape(row_count, HEADS, HEAD_DIM), cosine, sine_table)
    grad_projected = jnp.concatenate(
        [
            grad_query_raw.reshape(row_count, model_width),
            grad_key_raw.reshape(row_count, model_width),
            grad_values,
        ],
        axis=1,
    ).astype(jnp.bfloat16)
    grad_qkv_weight = jnp.einsum(
        "td,tf->df", first_in, grad_projected, preferred_element_type=jnp.float32
    )
    grad_first = jnp.einsum(
        "tf,df->td", grad_projected, qkv_weight, preferred_element_type=jnp.float32
    )
    grad_normed_one = grad_first * gain_one.astype(jnp.float32)
    grad_gain_one = jnp.sum(grad_first * normed_one, axis=0)
    grad_inputs = grad_middle + inverse_one * (
        grad_normed_one
        - normed_one * jnp.mean(grad_normed_one * normed_one, axis=-1, keepdims=True)
    )
    dense_parts = (
        lax.psum_scatter(
            grad_gain_one.astype(jnp.bfloat16), "narrow", scatter_dimension=0, tiled=True
        ).astype(jnp.float32),
        lax.psum_scatter(
            grad_qkv_weight.astype(jnp.bfloat16), "narrow", scatter_dimension=0, tiled=True
        ).astype(jnp.float32),
        lax.psum_scatter(
            grad_out_weight.astype(jnp.bfloat16), "narrow", scatter_dimension=0, tiled=True
        ).astype(jnp.float32),
        lax.psum_scatter(
            grad_gain_two.astype(jnp.bfloat16), "narrow", scatter_dimension=0, tiled=True
        ).astype(jnp.float32),
        lax.psum_scatter(
            grad_router.astype(jnp.bfloat16), "narrow", scatter_dimension=0, tiled=True
        ).astype(jnp.float32),
    )
    summed = jax.tree.map(
        lambda part: part.astype(jnp.float32),
        lax.psum(shortened((expert_grads,) + tuple(dense_parts)), "wide"),
    )
    expert_grads = summed[0]
    dense_parts = summed[1:]
    gain_one_sum, qkv_sum, out_sum, gain_two_sum, router_sum = dense_parts
    expert_table = expert_grads.reshape(narrow_rows, up_weight.shape[1], 3 * hidden)
    up_sum = expert_table[:, :, : 2 * hidden]
    down_sum = expert_table[:, :, 2 * hidden :]
    return (
        output,
        grad_inputs.astype(jnp.bfloat16),
        gain_one_sum,
        qkv_sum,
        out_sum,
        gain_two_sum,
        router_sum,
        up_sum,
        down_sum,
    )


def solution(mesh):
    return jax.shard_map(
        local,
        mesh=mesh,
        in_specs=(
            P(("wide", "narrow"), None),
            P(("wide", "narrow")),
            P(("wide", "narrow"), None),
            P(("wide", "narrow"), None),
            P(("wide", "narrow")),
            P(("wide", "narrow"), None),
            P(("wide", "narrow"), None),
            P(("wide", "narrow")),
            P(("wide", "narrow"), None),
            P(("wide", "narrow"), None, None),
            P(("wide", "narrow"), None, None),
        ),
        out_specs=(
            P(("wide", "narrow"), None),
            P(("wide", "narrow"), None),
            P("narrow"),
            P("narrow", None),
            P("narrow", None),
            P("narrow"),
            P("narrow", None),
            P("narrow", None, None),
            P("narrow", None, None),
        ),
        check_vma=False,
    )
```

profile of v0, /device:TPU:29, one launch (start us, length us, event | category | flops | bytes accessed | tf_op | source)
XLA Modules:
  0.0 2419.5 jit_solution(9995215593863136823)
XLA Ops:
  9.7 39.0 %all-reduce.4 = (bf16[1280]{0:T(1024)(128)(2,1)S(1)}, bf16[1280]{0:T(1024)(128)(2,1)S(1)}) all-reduce(bf16[1280]{0:T(1024)(128)(2,1)S(1)} %dynamic-update-slice, bf16[1280]{0:T(1024)(128)(2,1)S(1)} %dynamic-update-slice.1), channel_id=1, replica_groups=mesh['wide'=8,'narrow'=4] {'wide','narrow'}, use_global_device_ids=true, to_apply=%add | all-reduce | flops 2560 | bytes 10240
  49.8 45.5 %all-gather.13.cloned.1.call-done = bf16[1280,3840]{1,0:T(8,128)(2,1)} async-done(((bf16[40,3840]{1,0:T(8,128)(2,1)}), bf16[1280,3840]{1,0:T(8,128)(2,1)}) %all-gather.13.cloned.1.call-update) | async-done | bytes 9830416 | tf_op jit(solution)/shard_map/all_gather | solution.py:75
  95.4 5.4 fusion.66
  108.2 3.8 copy.162
  112.1 2.6 copy.163
  114.8 6.1 all-gather.1
  121.0 59.6 %all-gather.2 = bf16[32,40,15]{1,2,0:T(8,128)(2,1)S(1)} all-gather(bf16[1,40,15]{1,2,0:T(8,128)(2,1)S(1)} %bitcast.194), channel_id=1, replica_groups=mesh['wide'=8,'narrow'=4] {'wide','narrow'}, dimensions={0}, use_global_device_ids=true | all-gather | bytes 39600 | tf_op jit(solution)/shard_map/all_gather | solution.py:160
  181.9 5.3 gather_fusion
  188.5 2.4 copy.161
  191.0 2.5 copy.158
  198.0 31.7 %all-gather.19.cloned.1.call-done = bf16[1280,1280]{1,0:T(8,128)(2,1)} async-done(((bf16[40,1280]{1,0:T(8,128)(2,1)}), bf16[1280,1280]{1,0:T(8,128)(2,1)}) %all-gather.19.cloned.1.call-update) | async-done | bytes 3276816 | tf_op jit(solution)/shard_map/all_gather | solution.py:76
  229.7 2.8 multiply_reduce_fusion.5
  238.2 4.5 multiply_convert_fusion
  242.7 374.6 %all-gather.21.cloned.1.call-done = bf16[1280,16,1792]{2,0,1:T(8,128)(2,1)} async-done(((bf16[40,16,1792]{2,0,1:T(8,128)(2,1)}), bf16[1280,16,1792]{2,0,1:T(8,128)(2,1)}) %all-gather.21.cloned.1.call-update) | async-done | bytes 73400336 | tf_op jit(solution)/shard_map/all_gather | solution.py:161
  617.3 29.1 %fusion.2 = f32[15,72,1792]{2,1,0:T(8,128)} fusion(bf16[15,72,1280]{2,1,0:T(8,128)(2,1)} %convolution_convert_fusion.2, bf16[1280,16,1792]{2,0,1:T(8,128)(2,1)} %all-gather.21.cloned.1.call-done), kind=kOutput, calls=%fused_computation.4 | convolution fusion | flops 4954521600 | bytes 79319040 | tf_op jit(solution)/shard_map/ecd,def->ecf/dot_general | solution.py:182
  646.4 181.0 %all-gather.23.cloned.1.call-done = bf16[1280,16,896]{2,0,1:T(8,128)(2,1)} async-done(((bf16[40,16,896]{2,0,1:T(8,128)(2,1)}), bf16[1280,16,896]{2,0,1:T(8,128)(2,1)}) %all-gather.23.cloned.1.call-update) | async-done | bytes 36700176 | tf_op jit(solution)/shard_map/all_gather | solution.py:162
  827.3 18.7 multiply_convert_fusion.2
  846.0 30.4 %fusion = f32[15,72,1280]{2,1,0:T(8,128)} fusion(bf16[1280,16,1792]{2,0,1:T(8,128)(2,1)} %all-gather.21.cloned.1.call-done, bf16[15,72,896]{2,1,0:T(8,128)(2,1)} %get-tuple-element.170, bf16[15,72,896]{2,1,0:T(8,128)(2,1)} %get-tuple-element.169), kind=kOutput, calls=%fused_computation.2 | convolution fusion | flops 4962263040 | bytes 78213120 | tf_op jit(solution)/shard_map/ecf,def->ecd/dot_general | solution.py:228
  876.5 8.9 gather_fusion.1
  885.3 5.2 reshape.268
  890.6 19.4 multiply_reduce_fusion
  911.5 4.9 reduce_sum.166
  916.4 3.1 fusion.9
  919.5 3.0 multiply_convert_fusion.7
  922.6 4.1 fusion.19
  938.9 2.4 copy.183
  941.4 2.7 convolution_convert_fusion.6
  944.1 2.6 copy.185
  948.2 3.8 pad_maximum_fusion
  952.1 4.1 convolution_convert_fusion.1
  956.3 15.0 reduce-scatter.16.cloned.1.call-done
  975.9 28.3 %reduce-scatter.18.cloned.1.call-done = bf16[128,1280]{1,0:T(8,128)(2,1)} async-done(((bf16[512,1280]{1,0:T(8,128)(2,1)}), bf16[128,1280]{1,0:T(8,128)(2,1)}) %reduce-scatter.18.cloned.1.call-update) | async-done | bytes 327696
  1005.5 5.5 convolution_convert_fusion
  1013.7 9.5 reduce.1
  1025.0 6.3 all-to-all-start.2
  1034.2 9.1 reduce.2
  1045.1 3.1 all-to-all-done.2
  1048.2 6.6 all-to-all-start
  1054.8 9.1 copy.175
  1063.9 5.4 all-to-all-start.3
  1069.3 9.1 copy.171
  1078.4 218.6 %all-to-all-done.3 = bf16[15,72,1280]{1,0,2:T(8,128)(2,1)} async-done(((bf16[15,72,1280]{1,0,2:T(8,128)(2,1)}), bf16[15,72,1280]{1,0,2:T(8,128)(2,1)}, u32[]{:S(2)}, u32[]{:S(2)}) %all-to-all-start.3) | async-done | bytes 2764832 | tf_op jit(solution)/shard_map/all_to_all | solution.py:266
  1297.0 8.5 all-to-all-start.1
  1309.4 7.9 copy.176
  1317.3 215.2 %all-to-all-done.1 = bf16[15,72,1280]{1,0,2:T(8,128)(2,1)} async-done(((bf16[15,72,1280]{1,0,2:T(8,128)(2,1)}), bf16[15,72,1280]{1,0,2:T(8,128)(2,1)}, u32[]{:S(2)}, u32[]{:S(2)}) %all-to-all-start.1) | async-done | bytes 2764832 | tf_op jit(solution)/shard_map/all_to_all | solution.py:265
  1532.5 7.8 copy.172
  1541.4 52.7 %all-gather = bf16[512,896]{1,0:T(8,128)(2,1)S(1)} all-gather(bf16[128,896]{1,0:T(8,128)(2,1)S(1)} %copy-done.30), channel_id=2, replica_groups=mesh['wide'=8,'narrow'=4] {'narrow'}, dimensions={0}, use_global_device_ids=true | all-gather | bytes 1146880 | tf_op jit(solution)/shard_map/all_gather | solution.py:274
  1597.4 10.7 convert_bitcast_fusion.1
  1608.1 75.6 %all-gather.27.cloned.1.call-done = bf16[15,288,1792]{2,1,0:T(8,128)(2,1)} async-done(((bf16[15,72,1792]{2,1,0:T(8,128)(2,1)}), bf16[15,288,1792]{2,1,0:T(8,128)(2,1)}) %all-gather.27.cloned.1.call-update) | async-done | bytes 15482896 | tf_op jit(solution)/shard_map/all_gather | solution.py:271
  1683.7 17.8 convert_bitcast_fusion
  1701.6 18.6 maximum_maximum_fusion
  1720.1 27.9 %reduce-scatter.14.cloned.1.call-done = bf16[320,1280]{1,0:T(8,128)(2,1)} async-done(((bf16[1280,1280]{1,0:T(8,128)(2,1)}), bf16[320,1280]{1,0:T(8,128)(2,1)}) %reduce-scatter.14.cloned.1.call-update) | async-done | bytes 819216 | tf_op jit(solution)/shard_map/reduce_scatter | solution.py:366
  1748.0 170.9 %reduce-scatter.12.cloned.1.call-done = bf16[320,3840]{1,0:T(8,128)(2,1)} async-done(((bf16[1280,3840]{1,0:T(8,128)(2,1)}), bf16[320,3840]{1,0:T(8,128)(2,1)}) %reduce-scatter.12.cloned.1.call-update) | async-done | bytes 2457616 | tf_op jit(solution)/shard_map/reduce_scatter | solution.py:363
  1920.8 3.1 fusion.20
  1924.0 15.2 reduce-scatter.20.cloned.1.call-done
  1940.2 7.3 fusion.35
  1947.4 7.6 all-reduce.7
  1955.2 24.9 %all-reduce.5 = (bf16[320]{0:T(512)(128)(2,1)S(1)}, bf16[320]{0:T(512)(128)(2,1)S(1)}, bf16[320,15]{0,1:T(8,128)(2,1)S(1)}) all-reduce(bf16[320]{0:T(512)(128)(2,1)S(1)} %dynamic-slice.1, bf16[320]{0:T(512)(128)(2,1)S(1)} %dynamic-slice.3, bf16[320,15]{0,1:T(8,128)(2,1)S(1)} %copy.188), channel_id=1, replica_groups=mesh['wide'=8,'narrow'=4] {'wide'}, use_global_device_ids=true, to_apply=%region_21.22 | all-reduce | flops 5440 | bytes 21760 | tf_op jit(solution)/shard_map/psum | solution.py:378
  1982.9 334.4 %all-reduce.10.cloned.1.call-done = (bf16[320,16,2688]{2,0,1:T(8,128)(2,1)}, bf16[320,3840]{1,0:T(8,128)(2,1)}, bf16[320,1280]{1,0:T(8,128)(2,1)}) async-done(((bf16[320,16,2688]{2,0,1:T(8,128)(2,1)}, bf16[320,3840]{1,0:T(8,128)(2,1)}, bf16[320,1280]{1,0:T(8,128)(2,1)}), (bf16[320,16,2688]{2,0,1:T(8,128)(2,1)}, bf16[320,3840]{1,0:T(8,128)(2,1)}, bf16[320,1280]{1,0:T(8,128)(2,1)})) %all-reduce.10.cloned.1.call-update) | async-done | bytes 30801936 | tf_op jit(solution)/shard_map/psum | solution.py:378
  2317.3 19.9 slice.112
  2337.2 12.3 slice.113
  2349.5 2.6 convert_element_type.226
  2353.4 37.1 %copy.177 = f32[320,16,1792]{2,1,0:T(8,128)} copy(f32[320,16,1792]{2,0,1:T(8,128)} %slice.112) | data formatting | bytes 73400320
  2390.5 22.0 copy.178
  (260 shorter events, 68.7 us)
Async XLA Ops:
  7.2 88.2 %all-gather.13.cloned.1.call-start = ((), (), s32[]{:S(2)}) async-start(), calls=%async_computation.9 | async-start | bytes 10137600 | tf_op jit(solution)/shard_map/all_gather | solution.py:75
  7.9 180.6 %all-gather.17.cloned.1.call-start = ((), (), s32[]{:S(2)}) async-start(), calls=%async_computation.11 | async-start | bytes 1638400 | tf_op jit(solution)/shard_map/all_gather | solution.py:101
  48.7 52.1 %copy-start.34 = (f32[1280]{0:T(1024)}, f32[1280]{0:T(1024)S(1)}, u32[]{:S(2)}) copy-start(f32[1280]{0:T(1024)S(1)} %convert_element_type.190) | copy-start | bytes 15364
  49.8 51.0 %copy-start.49 = (f32[128]{0:T(128)}, f32[128]{0:T(128)S(1)}, u32[]{:S(2)}) copy-start(f32[128]{0:T(128)S(1)} %add_rsqrt_fusion.1) | copy-start | bytes 1540
  101.6 89.3 %all-gather.15.cloned.1.call-start = ((), (), s32[]{:S(2)}) async-start(), calls=%async_computation.10 | async-start | bytes 1638400 | tf_op jit(solution)/shard_map/all_gather | solution.py:100
  107.6 122.1 %all-gather.19.cloned.1.call-start = ((), (), s32[]{:S(2)}) async-start(), calls=%async_computation.12 | async-start | bytes 3379200 | tf_op jit(solution)/shard_map/all_gather | solution.py:76
  108.2 509.2 %all-gather.21.cloned.1.call-start = ((), (), s32[]{:S(2)}) async-start(), calls=%async_computation.13 | async-start | bytes 75694080 | tf_op jit(solution)/shard_map/all_gather | solution.py:161
  112.0 2.7 copy-start.18
  112.0 2.8 copy-start.55
  112.0 9.0 copy-start.54
  112.0 68.8 %copy-start.44 = (s32[128,7]{0,1:T(8,128)S(1)}, s32[128,7]{0,1:T(8,128)}, u32[]{:S(2)}) copy-start(s32[128,7]{0,1:T(8,128)} %param.13) | copy-start | bytes 10756
  112.0 715.3 %all-gather.23.cloned.1.call-start = ((), (), s32[]{:S(2)}) async-start(), calls=%async_computation.14 | async-start | bytes 37847040 | tf_op jit(solution)/shard_map/all_gather | solution.py:162
  114.7 856.5 %reduce-scatter.16.cloned.1.call-start = ((), (), s32[]{:S(2)}) async-start(), calls=%async_computation.20 | async-start | bytes 1638400
  193.4 3.0 copy-start.4
  229.7 5.7 copy-start.41
  890.6 19.4 copy-start.48
  910.0 6.4 copy-start.14
  911.5 15.2 copy-start.42
  916.4 3.1 copy-start.19
  919.5 3.0 copy-start.33
  922.6 4.1 copy-start.36
  922.6 4.1 copy-start.38
  922.6 4.1 copy-start.1
  922.6 4.1 copy-start.52
  932.6 4.7 copy-start.17
  941.3 62.8 %reduce-scatter.18.cloned.1.call-start = ((), (), s32[]{:S(2)}) async-start(), calls=%async_computation.21 | async-start | bytes 1638400
  944.1 4.2 copy-start.23
  946.6 648.3 %all-gather.25.cloned.1.call-start = ((), (), s32[]{:S(2)}) async-start(), calls=%async_computation.17 | async-start | bytes 2293760 | tf_op jit(solution)/shard_map/all_gather | solution.py:273
  947.6 649.8 %all-gather.29.cloned.1.call-start = ((), (), s32[]{:S(2)}) async-start(), calls=%async_computation.19 | async-start | bytes 9676800 | tf_op jit(solution)/shard_map/all_gather | solution.py:272
  948.2 735.6 %all-gather.27.cloned.1.call-start = ((), (), s32[]{:S(2)}) async-start(), calls=%async_computation.18 | async-start | bytes 19353600 | tf_op jit(solution)/shard_map/all_gather | solution.py:271
  952.1 21.0 copy-start.3
  952.1 21.0 copy-start.6
  952.1 796.0 %reduce-scatter.14.cloned.1.call-start = ((), (), s32[]{:S(2)}) async-start(), calls=%async_computation.16 | async-start | bytes 4096000 | tf_op jit(solution)/shard_map/reduce_scatter | solution.py:366
  956.2 962.7 %reduce-scatter.12.cloned.1.call-start = ((), (), s32[]{:S(2)}) async-start(), calls=%async_computation.15 | async-start | bytes 12288000 | tf_op jit(solution)/shard_map/reduce_scatter | solution.py:363
  975.5 29.8 %copy-start.21 = (f32[128,10,128]{0,2,1:T(8,128)S(1)}, f32[128,10,128]{0,2,1:T(8,128)}, u32[]{:S(2)}) copy-start(f32[128,10,128]{0,2,1:T(8,128)} %get-tuple-element.200) | copy-start | bytes 1966084
  975.5 30.0 %copy-start.11 = (bf16[128,1280]{1,0:T(8,128)(2,1)S(1)}, bf16[128,1280]{1,0:T(8,128)(2,1)}, u32[]{:S(2)}) copy-start(bf16[128,1280]{1,0:T(8,128)(2,1)} %param.11) | copy-start | bytes 983044
  975.5 30.0 %copy-start.35 = (f32[1280]{0:T(1024)S(1)}, f32[1280]{0:T(1024)}, u32[]{:S(2)}) copy-start(f32[1280]{0:T(1024)} %copy-done.34) | copy-start | bytes 15364
  975.5 30.0 %copy-start.50 = (f32[128]{0:T(128)S(1)}, f32[128]{0:T(128)}, u32[]{:S(2)}) copy-start(f32[128]{0:T(128)} %copy-done.49) | copy-start | bytes 1540
  975.8 35.2 %copy-start.26 = (bf16[128,1280]{0,1:T(8,128)(2,1)}, bf16[128,1280]{0,1:T(8,128)(2,1)S(1)}, u32[]{:S(2)}) copy-start(bf16[128,1280]{0,1:T(8,128)(2,1)S(1)} %fusion.42) | copy-start | bytes 983044
  1005.3 5.7 copy-start.24
  1005.5 5.6 copy-start.28
  1013.2 41.6 %copy-start.7 = (bf16[15,72,1280]{2,1,0:T(8,128)(2,1)S(1)}, bf16[15,72,1280]{2,1,0:T(8,128)(2,1)}, u32[]{:S(2)}) copy-start(bf16[15,72,1280]{2,1,0:T(8,128)(2,1)} %multiply_convert_fusion) | copy-start | bytes 8294404
  1025.0 23.2 all-to-all-start.2
  1048.2 15.7 all-to-all-start
  1063.9 5.4 copy-start.8
  1063.9 233.1 %all-to-all-start.3 = ((bf16[15,72,1280]{1,0,2:T(8,128)(2,1)}), bf16[15,72,1280]{1,0,2:T(8,128)(2,1)}, u32[]{:S(2)}, u32[]{:S(2)}) async-start(bf16[15,72,1280]{1,0,2:T(8,128)(2,1)} %copy.175), calls=%async_computation.5 | async-start | bytes 10485760 | tf_op jit(solution)/shard_map/all_to_all | solution.py:266
  1297.0 235.5 %all-to-all-start.1 = ((bf16[15,72,1280]{1,0,2:T(8,128)(2,1)}), bf16[15,72,1280]{1,0,2:T(8,128)(2,1)}, u32[]{:S(2)}, u32[]{:S(2)}) async-start(bf16[15,72,1280]{1,0,2:T(8,128)(2,1)} %copy.171), calls=%async_computation.3 | async-start | bytes 10485760 | tf_op jit(solution)/shard_map/all_to_all | solution.py:265
  1305.5 633.7 %reduce-scatter.20.cloned.1.call-start = ((), (), s32[]{:S(2)}) async-start(), calls=%async_computation.22 | async-start | bytes 409600
  1532.5 7.8 copy-start.15
  1532.5 7.8 copy-start.43
  1532.5 8.9 copy-start.30
  1594.2 723.2 %all-reduce.10.cloned.1.call-start = ((), (), s32[]{:S(2)}) async-start(), calls=%async_computation.23 | async-start | bytes 61603840 | tf_op jit(solution)/shard_map/psum | solution.py:378
  1919.0 21.2 copy-start.12
  1919.0 21.2 copy-start.25
  1919.0 21.2 copy-start.27
  1919.0 21.2 copy-start.29
  1940.2 7.3 copy-start.46
  1940.2 41.7 %copy-start.10 = (f32[128,1280]{1,0:T(8,128)S(1)}, f32[128,1280]{1,0:T(8,128)}, u32[]{:S(2)}) copy-start(f32[128,1280]{1,0:T(8,128)} %copy-done.9) | copy-start | bytes 1966084
  2337.2 12.3 copy-start.22
  2352.1 38.4 %slice-start = ((s8[18350080]{0:T(1024)(128)(4,1)}), s8[4194304]{0:T(1024)(128)(4,1)S(1)}, s32[]{:S(2)}) async-start(s8[18350080]{0:T(1024)(128)(4,1)} %bitcast.153), calls=%async_computation.24 | async-start | bytes 8388608
  2353.4 37.1 %slice-start.1 = ((s8[18350080]{0:T(1024)(128)(4,1)}), s8[4194304]{0:T(1024)(128)(4,1)S(1)}, s32[]{:S(2)}) async-start(s8[18350080]{0:T(1024)(128)(4,1)} %bitcast.153), calls=%async_computation.25 | async-start | bytes 8388608
  2353.4 37.1 %slice-start.2 = ((s8[18350080]{0:T(1024)(128)(4,1)}), s8[4194304]{0:T(1024)(128)(4,1)S(1)}, s32[]{:S(2)}) async-start(s8[18350080]{0:T(1024)(128)(4,1)} %bitcast.153), calls=%async_computation.26 | async-start | bytes 8388608
  2353.4 37.1 %slice-start.3 = ((s8[18350080]{0:T(1024)(128)(4,1)}), s8[4194304]{0:T(1024)(128)(4,1)S(1)}, s32[]{:S(2)}) async-start(s8[18350080]{0:T(1024)(128)(4,1)} %bitcast.153), calls=%async_computation.27 | async-start | bytes 8388608
  2353.4 37.1 %slice-start.4 = ((s8[18350080]{0:T(1024)(128)(4,1)}), s8[1572864]{0:T(1024)(128)(4,1)S(1)}, s32[]{:S(2)}) async-start(s8[18350080]{0:T(1024)(128)(4,1)} %bitcast.153), calls=%async_computation.28 | async-start | bytes 3145728
  (17 other events, 24.4 us)
Sparse Core Ops, SparseCore 0:
  10.8 84.5 all-gather.12
  101.8 30.8 all-gather.16
  134.8 32.6 all-gather.14
  170.2 59.4 all-gather.18
  233.0 384.2 all-gather.20
  620.1 207.1 all-gather.22
  941.5 29.7 reduce-scatter.15
  974.1 30.0 reduce-scatter.17
  1005.7 47.3 all-gather.24
  1054.6 248.9 all-gather.28
  1305.8 377.8 all-gather.26
  1685.9 62.1 reduce-scatter.13
  1750.4 168.4 reduce-scatter.11
  1921.7 17.3 reduce-scatter.19
  1944.5 372.8 all-reduce.9
where the time goes:
time: 2430 us; the launch traced here: 2420 us
  waiting for transfers between devices  1740 us (72%)
  local copies, waits for them, and re-layouts  193 us (8%)
  blocking collectives  190 us (8%)
  matrix products  186 us (8%)
  other arithmetic  68.4 us (3%)
  starting transfers between devices  27.6 us (1%)
    all_gather x1, waiting for transfers between devices, local(): lax.all_gather(w_up, ('wide', 'narrow'), axis=0, tiled=True)  375 us
    psum x1, waiting for transfers between devices, local(): lax.psum(shortened((expert_grads,) + tuple(dense_parts)), 'wide')  334 us
    all_to_all x1, waiting for transfers between devices, local(): lax.all_to_all(grad_rows, 'narrow', split_axis=2, concat_axis=1, tiled=True)  219 us
    all_to_all x1, waiting for transfers between devices, local(): lax.all_to_all(gathered_in, 'narrow', split_axis=2, concat_axis=1, tiled=...  215 us
    all_gather x1, waiting for transfers between devices, local(): lax.all_gather(w_down, ('wide', 'narrow'), axis=0, tiled=True)  181 us
    reduce_scatter x1, waiting for transfers between devices, local(): lax.psum_scatter(grad_qkv_weight.astype(jnp.bfloat16), 'narrow', scatter_...  171 us
    unnamed x149, local copies, waits for them, and re-layouts  91 us
    all_gather x1, waiting for transfers between devices, local(): lax.all_gather(grad_gate_up, 'narrow', axis=1, tiled=True)  75.6 us
  transfers between devices with their start and end apart: 19, of which 14 were waited for; matrix products, arithmetic and copies ran while one was open for 9% of the time, Pallas kernels for 0%

commit v1 on v0

--- a/solution.py
+++ b/solution.py
@@ -1,6 +1,8 @@
 import jax
 import jax.numpy as jnp
 from jax import lax
+from jax.experimental import pallas as pl
+from jax.experimental.pallas import tpu as pltpu
 from jax.sharding import PartitionSpec as P
 
 HEADS = 10
@@ -396,9 +398,771 @@
     )
 
 
+PLANES = 4
+WINDOW = 3
+STARTS = (0, 3, 6, 7)
+KEEP = ((0, 3), (0, 3), (0, 2), (1, 3))
+MESH_IDS = pl.DeviceIdType.MESH
+BF16 = jnp.bfloat16
+F32 = jnp.float32
+
+
+def place():
+    w = lax.axis_index("wide")
+    z = lax.axis_index("narrow")
+    return w, z
+
+
+def other_plane(z, step):
+    return lax.rem(z + step, PLANES), lax.rem(z + PLANES - step, PLANES)
+
+
+class Net:
+    def __init__(self, send_sems, recv_sems):
+        self.send_sems, self.recv_sems, self.used, self.started = send_sems, recv_sems, 0, []
+
+    def send(self, src, dst, device):
+        copy = pltpu.make_async_remote_copy(
+            src_ref=src,
+            dst_ref=dst,
+            send_sem=self.send_sems.at[self.used],
+            recv_sem=self.recv_sems.at[self.used],
+            device_id=device,
+            device_id_type=MESH_IDS,
+        )
+        self.used += 1
+        copy.start()
+        self.started.append(copy)
+        return copy
+
+    def keep(self, src, dst):
+        copy = pltpu.make_async_copy(src, dst, self.send_sems.at[self.used])
+        self.used += 1
+        copy.start()
+        return copy
+
+    def finish(self):
+        for copy in self.started:
+            copy.wait_send()
+
+
+def greet(w, z):
+    barrier = pltpu.get_barrier_semaphore()
+    peers = [(w, lax.rem(z + step, PLANES)) for step in (1, 2, 3)]
+    peers += [(w ^ flip, z) for flip in (1, 2, 4, 6)]
+    for peer in peers:
+        pl.semaphore_signal(barrier, inc=1, device_id=peer, device_id_type=MESH_IDS)
+    pl.semaphore_wait(barrier, len(peers))
+
+
+class PlaneGather:
+    def __init__(self, net, w, z, slot, number, cores):
+        self.net, self.w, self.z, self.slot, self.cores = net, w, z, slot, cores
+        self.first, self.second = (2, 4) if number % 2 == 0 else (4, 2)
+
+    def push(self, slot_of, flip):
+        ref = self.slot(slot_of)
+        return self.net.send(ref, ref, (self.w ^ flip, self.z))
+
+    def begin(self):
+        self.direct = {flip: self.push(self.w, flip) for flip in (2, 4)}
+        self.core = [self.push(self.w, 1)] if self.cores else []
+
+    def relay(self):
+        self.direct[self.first].wait_recv()
+        self.across = self.push(self.w ^ self.first, self.second)
+        if self.cores:
+            self.core.append(self.push(self.w ^ self.first, 1))
+        self.direct[self.second].wait_recv()
+        if self.cores:
+            self.core.append(self.push(self.w ^ self.second, 1))
+
+    def end(self):
+        self.across.wait_recv()
+        if self.cores:
+            self.core.append(self.push(self.w ^ 6, 1))
+
+    def settle(self):
+        for copy in self.core:
+            copy.wait_recv()
+
+
+def comm_call(kernel, name, collective, out_shape, in_spaces, out_spaces, sems, scratch=(), moved=0):
+    return pl.pallas_call(
+        kernel,
+        out_shape=out_shape,
+        in_specs=[pl.BlockSpec(memory_space=space) for space in in_spaces],
+        out_specs=[pl.BlockSpec(memory_space=space) for space in out_spaces],
+        scratch_shapes=[
+            *scratch,
+            pltpu.SemaphoreType.DMA((sems,)),
+            pltpu.SemaphoreType.DMA((sems,)),
+        ],
+        compiler_params=pltpu.CompilerParams(
+            collective_id=collective, has_side_effects=True, vmem_limit_bytes=56 * 2**20
+        ),
+        name=name,
+    )
+
+
+def spread_inputs_kernel(
+    tok, ids, wq, wo, we, cot, tok_o, ids_o, wq_o, wo_o, we_o, cot_o, hop, send_sems, recv_sems
+):
+    w, z = place()
+    chip = w // 2
+    greet(w, z)
+    net = Net(send_sems, recv_sems)
+    own = [
+        net.keep(tok, tok_o.at[z]),
+        net.keep(ids, ids_o.at[z]),
+        net.keep(wq.at[z], wq_o.at[w, z]),
+        net.keep(wo, wo_o.at[w, z]),
+        net.keep(we.at[z, chip], we_o.at[w, z]),
+        net.keep(cot, cot_o.at[chip, z]),
+    ]
+    ring, gathers = {}, {}
+    for step in (1, 2, 3):
+        to, _ = other_plane(z, step)
+        ring["tok", step] = net.send(tok, tok_o.at[z], (w, to))
+        ring["ids", step] = net.send(ids, ids_o.at[z], (w, to))
+        ring["wq", step] = net.send(wq.at[to], wq_o.at[w, z], (w, to))
+    for step in (1, 2, 3):
+        to, _ = other_plane(z, step)
+        for flip in (1, 2, 3):
+            ring["we", step, flip] = net.send(
+                we.at[to, chip ^ flip], hop.at[step - 1, flip - 1], (w, to)
+            )
+        ring["we", step, 0] = net.send(we.at[to, chip], we_o.at[w, z], (w, to))
+        ring["cot", step] = net.send(cot, cot_o.at[chip, z], (w, to))
+        ring["wo", step] = net.send(wo, wo_o.at[w, z], (w, to))
+    for copy in own:
+        copy.wait()
+    weights = {}
+    for flip in (1, 2, 3):
+        weights[0, flip] = net.send(
+            we.at[z, chip ^ flip], we_o.at[w, z], (w ^ (2 * flip), z)
+        )
+    core = [net.send(we_o.at[w, z], we_o.at[w, z], (w ^ 1, z))]
+
+    def start_gather(kind, step):
+        _, source = other_plane(z, step)
+        slot = {
+            "wq": lambda i: wq_o.at[i, source],
+            "wo": lambda i: wo_o.at[i, source],
+            "cot": lambda i: cot_o.at[i // 2, source],
+        }[kind]
+        gathers[kind, step] = PlaneGather(net, w, z, slot, step, kind != "cot")
+        gathers[kind, step].begin()
+
+    start_gather("wq", 0)
+    start_gather("wo", 0)
+    start_gather("cot", 0)
+    for step in (1, 2, 3):
+        ring["wq", step].wait_recv()
+        start_gather("wq", step)
+    for step in (0, 1, 2, 3):
+        gathers["wq", step].relay()
+    gathers["wo", 0].relay()
+    gathers["cot", 0].relay()
+    for step in (0, 1, 2, 3):
+        gathers["wq", step].end()
+    gathers["wo", 0].end()
+    gathers["cot", 0].end()
+    for step in (1, 2, 3):
+        _, source = other_plane(z, step)
+        for flip in (1, 2, 3):
+            ring["we", step, flip].wait_recv()
+            weights[step, flip] = net.send(
+                hop.at[step - 1, flip - 1], we_o.at[w, source], (w ^ (2 * flip), z)
+            )
+        ring["we", step, 0].wait_recv()
+        core.append(net.send(we_o.at[w, source], we_o.at[w, source], (w ^ 1, z)))
+        for kind in ("cot", "wo"):
+            ring[kind, step].wait_recv()
+            start_gather(kind, step)
+        ring["tok", step].wait_recv()
+        ring["ids", step].wait_recv()
+    for step in (0, 1, 2, 3):
+        _, source = other_plane(z, step)
+        for flip in (1, 2, 3):
+            weights[step, flip].wait_recv()
+            peer = w ^ (2 * flip)
+            core.append(net.send(we_o.at[peer, source], we_o.at[peer, source], (w ^ 1, z)))
+        if step:
+            for kind in ("cot", "wo"):
+                gathers[kind, step].relay()
+    for step in (1, 2, 3):
+        for kind in ("cot", "wo"):
+            gathers[kind, step].end()
+    for gather in gathers.values():
+        gather.settle()
+    for copy in core:
+        copy.wait_recv()
+    net.finish()
+
+
+def spread_inputs(tok, ids, wq, wo, we, cot):
+    rows, width = tok.shape
+    own = wo.shape[0]
+    hidden3 = we.shape[-1]
+    shapes = [
+        (PLANES, rows, width),
+        (PLANES,) + ids.shape,
+        (8, PLANES) + wq.shape[1:],
+        (8, PLANES) + wo.shape,
+        (8, PLANES, own, hidden3),
+        (4, PLANES) + cot.shape,
+        (3, 3, own, hidden3),
+    ]
+    out = comm_call(
+        spread_inputs_kernel,
+        "spread_inputs",
+        1,
+        [jax.ShapeDtypeStruct(shape, BF16) for shape in shapes],
+        [pl.ANY] * 6,
+        [pl.ANY] * 7,
+        160,
+    )(tok, ids, wq, wo, we, cot)
+    return out[:6]
+
+
+def swap_planes_kernel(x, out, send_sems, recv_sems):
+    w, z = place()
+    greet(w, z)
+    net = Net(send_sems, recv_sems)
+    own = net.keep(x.at[z], out.at[z])
+    copies = []
+    for step in (1, 2, 3):
+        to, _ = other_plane(z, step)
+        copies.append(net.send(x.at[to], out.at[z], (w, to)))
+    own.wait()
+    for copy in copies:
+        copy.wait_recv()
+    net.finish()
+
+
+def swap_planes(x, collective):
+    return comm_call(
+        swap_planes_kernel,
+        "swap_planes",
+        collective,
+        [jax.ShapeDtypeStruct(x.shape, x.dtype)],
+        [pl.ANY],
+        [pl.ANY],
+        8,
+    )(x)[0]
+
+
+def gather_rows_kernel(x, out, send_sems, recv_sems):
+    w, z = place()
+    chip = w // 2
+    greet(w, z)
+    net = Net(send_sems, recv_sems)
+    own = net.keep(x, out.at[chip, z])
+    ring = {}
+    for step in (1, 2, 3):
+        to, _ = other_plane(z, step)
+        ring[step] = net.send(x, out.at[chip, z], (w, to))
+    own.wait()
+    gathers = []
+    for step in (0, 1, 2, 3):
+        _, source = other_plane(z, step)
+        if step:
+            ring[step].wait_recv()
+        gather = PlaneGather(
+            net, w, z, lambda i, source=source: out.at[i // 2, source], step, False
+        )
+        gather.begin()
+        gathers.append(gather)
+    for gather in gathers:
+        gather.relay()
+    for gather in gathers:
+        gather.end()
+    net.finish()
+
+
+def gather_rows(x, collective):
+    return comm_call(
+        gather_rows_kernel,
+        "gather_rows",
+        collective,
+        [jax.ShapeDtypeStruct((4, PLANES) + x.shape, x.dtype)],
+        [pl.ANY],
+        [pl.ANY],
+        40,
+    )(x)[0]
+
+
+def add_blocks(out, *terms):
+    rows = out.shape[0]
+
+    def body(i, carry):
+        part = pl.ds(pl.multiple_of(i * 16, 16), 16)
+        total = terms[0][part, :].astype(F32)
+        for term in terms[1:]:
+            total = total + term[part, :].astype(F32)
+        out[part, :] = total.astype(out.dtype)
+        return carry
+
+    lax.fori_loop(0, rows // 16, body, 0)
+
+
+def sum_rows_kernel(x, out, got_one, got_two, got_far, part, ready, send_sems, recv_sems):
+    w, z = place()
+    chip = w // 2
+    greet(w, z)
+    net = Net(send_sems, recv_sems)
+    steps = (1, 2, 3, 0)
+    near, cross, far = {}, {}, []
+    for step in steps:
+        to, _ = other_plane(z, step)
+        first = 1 if step % 2 == 0 else 2
+        peer = (w ^ (2 * first), z)
+        near[step] = (
+            net.send(x.at[chip ^ 3, to], got_one.at[step, 1], peer),
+            net.send(x.at[chip ^ first, to], got_one.at[step, 0], peer),
+        )
+    for step in steps:
+        to, _ = other_plane(z, step)
+        first = 1 if step % 2 == 0 else 2
+        second = 3 - first
+        near[step][0].wait_recv()
+        add_blocks(part.at[step], x.at[chip ^ second, to], got_one.at[step, 1])
+        cross[step] = net.send(part.at[step], got_two.at[step], (w ^ (2 * second), z))
+    for step in steps:
+        to, _ = other_plane(z, step)
+        near[step][1].wait_recv()
+        cross[step].wait_recv()
+        if step:
+            add_blocks(ready.at[step - 1], x.at[chip, to], got_one.at[step, 0], got_two.at[step])
+            far.append(net.send(ready.at[step - 1], got_far.at[step - 1], (w, to)))
+    for copy in far:
+        copy.wait_recv()
+    add_blocks(
+        out,
+        x.at[chip, z],
+        got_one.at[0, 0],
+        got_two.at[0],
+        got_far.at[0],
+        got_far.at[1],
+        got_far.at[2],
+    )
+    net.finish()
+
+
+def sum_rows(x, collective):
+    rows, width = x.shape[2:]
+    return comm_call(
+        sum_rows_kernel,
+        "sum_rows",
+        collective,
+        [jax.ShapeDtypeStruct((rows, width), F32)],
+        [pltpu.VMEM],
+        [pltpu.VMEM],
+        24,
+        [
+            pltpu.VMEM((4, 2, rows, width), BF16),
+            pltpu.VMEM((4, rows, width), BF16),
+            pltpu.VMEM((3, rows, width), BF16),
+            pltpu.VMEM((4, rows, width), BF16),
+            pltpu.VMEM((3, rows, width), BF16),
+        ],
+    )(x)[0]
+
+
+def spread_grads_kernel(x, out, got, mine, total, send_sems, recv_sems):
+    w, z = place()
+    chip, core = w // 2, w % 2
+    greet(w, z)
+    net = Net(send_sems, recv_sems)
+    steps = (1, 2, 3, 0)
+    swap, load, ring, gathers = {}, {}, {}, []
+    for step in steps:
+        to, _ = other_plane(z, step)
+        swap[step] = net.send(x.at[to, 1 - core], got.at[step], (w ^ 1, z))
+        load[step] = net.keep(x.at[to, core], mine.at[step])
+    for step in steps:
+        to, _ = other_plane(z, step)
+        load[step].wait()
+        swap[step].wait_recv()
+        add_blocks(total.at[step], mine.at[step], got.at[step])
+        if step:
+            ring[step] = net.send(total.at[step], out.at[chip, z, core], (w, to))
+        else:
+            own = net.keep(total.at[step], out.at[chip, z, core])
+    own.wait()
+    for step in (0, 1, 2, 3):
+        _, source = other_plane(z, step)
+        if step:
+            ring[step].wait_recv()
+        gather = PlaneGather(
+            net, w, z, lambda i, source=source: out.at[i // 2, source, i % 2], step, True
+        )
+        gather.begin()
+        gathers.append(gather)
+    for gather in gathers:
+        gather.relay()
+    for gather in gathers:
+        gather.end()
+    for gather in gathers:
+        gather.settle()
+    net.finish()
+
+
+def spread_grads(x, collective):
+    rows, width = x.shape[2:]
+    block = (4, rows, width)
+    return comm_call(
+        spread_grads_kernel,
+        "spread_grads",
+        collective,
+        [jax.ShapeDtypeStruct((4, PLANES, 2, rows, width), BF16)],
+        [pl.ANY],
+        [pl.ANY],
+        64,
+        [pltpu.VMEM(block, BF16), pltpu.VMEM(block, BF16), pltpu.VMEM(block, BF16)],
+    )(x)[0]
+
+
+def sum_dense_kernel(
+    first, x, first_o, q_o, o_o, got, mine, part, got_one, got_two, sent, ready, got_far, send_sems, recv_sems
+):
+    w, z = place()
+    chip, core = w // 2, w % 2
+    greet(w, z)
+    net = Net(send_sems, recv_sems)
+    steps = (1, 2, 3, 0)
+    own = net.keep(first.at[z], first_o.at[z])
+    swap, load, flow, near, cross, far, gathers = {}, {}, [], {}, {}, {}, []
+    for step in steps:
+        to, _ = other_plane(z, step)
+        for kind in (0, 1):
+            swap[step, kind] = net.send(x.at[kind, 1 - core, to], got.at[kind, step], (w ^ 1, z))
+            load[step, kind] = net.keep(x.at[kind, core, to], mine.at[kind, step])
+    for step in (1, 2, 3):
+        to, _ = other_plane(z, step)
+        flow.append(net.send(first.at[to], first_o.at[z], (w, to)))
+    for step in steps:
+        for kind in (0, 1):
+            load[step, kind].wait()
+            swap[step, kind].wait_recv()
+            for block in range(4):
+                add_blocks(
+                    part.at[kind, step, block], mine.at[kind, step, block], got.at[kind, step, block]
+                )
+            first_flip = 1 + kind
+            peer = (w ^ (2 * first_flip), z)
+            near[step, kind] = (
+                net.send(part.at[kind, step, chip ^ 3], got_one.at[kind, step, 1], peer),
+                net.send(part.at[kind, step, chip ^ first_flip], got_one.at[kind, step, 0], peer),
+            )
+    for step in steps:
+        for kind in (0, 1):
+            second = 2 - kind
+            near[step, kind][0].wait_recv()
+            add_blocks(
+                sent.at[kind, step], part.at[kind, step, chip ^ second], got_one.at[kind, step, 1]
+            )
+            cross[step, kind] = net.send(
+                sent.at[kind, step], got_two.at[kind, step], (w ^ (2 * second), z)
+            )
+    for step in steps:
+        to, _ = other_plane(z, step)
+        for kind in (0, 1):
+            near[step, kind][1].wait_recv()
+            cross[step, kind].wait_recv()
+            add_blocks(
+                ready.at[kind, step],
+                part.at[kind, step, chip],
+                got_one.at[kind, step, 0],
+                got_two.at[kind, step],
+            )
+        if step:
+            far[step, 0] = net.send(ready.at[0, step], q_o.at[w, z], (w, to))
+            far[step, 1] = net.send(ready.at[1, step], got_far.at[step - 1], (w, to))
+        else:
+            kept = net.keep(ready.at[0, 0], q_o.at[w, z])
+    kept.wait()
+    for step in (0, 1, 2, 3):
+        _, source = other_plane(z, step)
+        if step:
+            far[step, 0].wait_recv()
+        gather = PlaneGather(net, w, z, lambda i, source=source: q_o.at[i, source], step, True)
+        gather.begin()
+        gathers.append(gather)
+    for step in (1, 2, 3):
+        far[step, 1].wait_recv()
+    add_blocks(mine.at[1, 0, 0], ready.at[1, 0], got_far.at[0], got_far.at[1], got_far.at[2])
+    last = net.keep(mine.at[1, 0, 0], o_o.at[w])
+    last.wait()
+    gather = PlaneGather(net, w, z, lambda i: o_o.at[i], 0, True)
+    gather.begin()
+    gathers.append(gather)
+    for gather in gathers:
+        gather.relay()
+    for gather in gathers:
+        gather.end()
+    for gather in gathers:
+        gather.settle()
+    own.wait()
+    for copy in flow:
+        copy.wait_recv()
+    net.finish()
+
+
+def sum_dense(first, x, collective):
+    rows, width = x.shape[4:]
+    block = (rows, width)
+    return comm_call(
+        sum_dense_kernel,
+        "sum_dense",
+        collective,
+        [
+            jax.ShapeDtypeStruct(first.shape, BF16),
+            jax.ShapeDtypeStruct((8, PLANES) + block, BF16),
+            jax.ShapeDtypeStruct((8,) + block, BF16),
+        ],
+        [pl.ANY, pl.ANY],
+        [pl.ANY, pl.ANY, pl.ANY],
+        140,
+        [
+            pltpu.VMEM((2, 4, 4) + block, BF16),
+            pltpu.VMEM((2, 4, 4) + block, BF16),
+            pltpu.VMEM((2, 4, 4) + block, BF16),
+            pltpu.VMEM((2, 4, 2) + block, BF16),
+            pltpu.VMEM((2, 4) + block, BF16),
+            pltpu.VMEM((2, 4) + block, BF16),
+            pltpu.VMEM((2, 4) + block, BF16),
+            pltpu.VMEM((3,) + block, BF16),
+        ],
+    )(first, x)
+
+
+def windows(x):
+    size = WINDOW * HEAD_DIM
+    return jnp.stack([x[:, s * HEAD_DIM : s * HEAD_DIM + size] for s in STARTS])
+
+
+def from_windows(x):
+    return jnp.concatenate(
+        [x[p, :, a * HEAD_DIM : b * HEAD_DIM] for p, (a, b) in enumerate(KEEP)], axis=1
+    )
+
+
+def dot(a, b, dims, out=F32):
+    return lax.dot_general(a, b, ((dims[0], dims[1]), ((), ())), preferred_element_type=F32).astype(out)
+
+
+def expert_local(
+    tokens, seq_ids, routes, cotangent, gain_attn, w_qkv, w_out, gain_ffn, w_router, w_up, w_down
+):
+    rows, width = tokens.shape
+    own = w_out.shape[0]
+    experts = w_router.shape[1]
+    seqlen = PLANES * rows
+    size = WINDOW * HEAD_DIM
+    scale = HEAD_DIM ** (-0.5)
+    w, z = place()
+    expert = (w // 2) * PLANES + z
+
+    misc = jnp.concatenate(
+        [w_router, gain_attn[:, None], gain_ffn[:, None], jnp.zeros((own, 128 - experts - 2), BF16)],
+        axis=1,
+    )
+    wq_send = jnp.concatenate(
+        [windows(w_qkv[:, i * width : (i + 1) * width]) for i in range(3)]
+        + [jnp.broadcast_to(misc[None], (PLANES, own, 128))],
+        axis=2,
+    )
+    we_send = jnp.concatenate([w_up, w_down], axis=2).reshape(own, 4, PLANES, 3 * FF)
+    we_send = jnp.transpose(we_send, (2, 1, 0, 3))
+    choose = routes[:, :, None] == jnp.arange(experts, dtype=jnp.int32)[None, None, :]
+    member = jnp.any(choose, axis=1)
+    member_cols = jnp.concatenate(
+        [jnp.ones((rows, 1), BF16), member.astype(BF16), jnp.zeros((rows, 127 - experts), BF16)],
+        axis=1,
+    )
+    cot_send = jnp.concatenate([cotangent, member_cols], axis=1)
+    ids_send = jnp.broadcast_to(seq_ids.astype(BF16)[None, :], (16, rows))
+    tok_all, ids_all, wq_all, wo_all, we_all, cot_all = spread_inputs(
+        tokens, ids_send, wq_send, w_out, we_send, cot_send
+    )
+    wq_all = wq_all.reshape(width, 3 * size + 128)
+    misc_all = wq_all[:, 3 * size :]
+    wq = wq_all[:, : 3 * size]
+    router = misc_all[:, :experts]
+    gain_one = misc_all[:, experts].astype(F32)
+    gain_two = misc_all[:, experts + 1].astype(F32)
+    out_weight = wo_all.reshape(width, width)
+
+    seq_in = tok_all.reshape(seqlen, width).astype(F32)
+    seq_normed = seq_in * rms_inverse(seq_in)
+    first_in = (seq_normed * gain_one).astype(BF16)
+    projected = dot(first_in, wq, ((1,), (0,)))
+    cosine, sine_table = rotary(jnp.arange(seqlen, dtype=F32), HEAD_DIM)
+    pq, pk, pv = (
+        projected[:, i * size : (i + 1) * size].reshape(seqlen, WINDOW, HEAD_DIM) for i in range(3)
+    )
+    query_rows = (rotate(pq, cosine, sine_table) * scale).astype(BF16)
+    key_rows = rotate(pk, cosine, sine_table).astype(BF16)
+    value_rows = pv.astype(BF16)
+    ids = ids_all[:, 0, :].reshape(seqlen)
+    at = jnp.arange(seqlen, dtype=jnp.int32)
+    allowed = ((at[None, :] <= at[:, None]) & (ids[None, :] == ids[:, None]))[None]
+    scores = jnp.einsum("qhd,khd->hqk", query_rows, key_rows, preferred_element_type=F32)
+    masked = jnp.where(allowed, scores, -1e30)
+    top = jnp.max(masked, axis=2, keepdims=True)
+    powers = jnp.where(allowed, jnp.exp(masked - top), 0.0)
+    weights_exact = powers * (1.0 / jnp.sum(powers, axis=2, keepdims=True))
+    weights_low = weights_exact.astype(BF16)
+    mixed_exact = jnp.einsum("hqk,khd->qhd", weights_low, value_rows, preferred_element_type=F32)
+    mixed_send = mixed_exact.astype(BF16).reshape(PLANES, rows, size)
+    mixed = from_windows(swap_planes(mixed_send, 2))
+    middle = tokens.astype(F32) + dot(mixed, out_weight, ((1,), (0,)))
+    inverse_two = rms_inverse(middle)
+    normed_two = middle * inverse_two
+    second_in = (normed_two * gain_two).astype(BF16)
+
+    x_all = gather_rows(second_in, 3).reshape(-1, width)
+    cot_all = cot_all.reshape(-1, width + 128)
+    cot_rows = cot_all[:, :width]
+    members = cot_all[:, width : width + experts + 1].astype(F32)
+    weights = we_all.reshape(width, 3 * FF)
+    up, down = weights[:, : 2 * FF], weights[:, 2 * FF :]
+    probs_all = jax.nn.softmax(dot(x_all, router, ((1,), (0,))), axis=-1)
+    mine = (jnp.arange(experts + 1) == expert).astype(F32)[None, :]
+    shared_one = jnp.ones((x_all.shape[0], 1), F32)
+    member_own = jnp.sum(members * mine, axis=1, keepdims=True)
+    gate = jnp.sum(
+        jnp.concatenate([shared_one, probs_all], axis=1) * members * mine, axis=1, keepdims=True
+    )
+    gate_up = dot(x_all, up, ((1,), (0,)))
+    gate_part, up_part = gate_up[:, :FF], gate_up[:, FF:]
+    sigmoid = jax.nn.sigmoid(gate_part)
+    activated = (gate_part * sigmoid * up_part).astype(BF16)
+    expert_rows = dot(activated, down, ((1,), (1,)), BF16).astype(F32)
+    cot_f = cot_rows.astype(F32)
+    out_part = (gate * expert_rows).astype(BF16)
+    grad_prob = jnp.sum(expert_rows * cot_f, axis=1, keepdims=True) * member_own
+    prob_hi = grad_prob.astype(BF16)
+    prob_lo = (grad_prob - prob_hi.astype(F32)).astype(BF16)
+    lane = jnp.arange(128)[None, :]
+    prob_cols = jnp.where(lane == expert, prob_hi, 0) + jnp.where(lane == expert + 32, prob_lo, 0)
+    grad_rows = (gate * cot_f).astype(BF16)
+    grad_act = dot(grad_rows, down, ((1,), (0,)))
+    grad_gate_up = jnp.concatenate(
+        [
+            grad_act * up_part * sigmoid * (1.0 + gate_part * (1.0 - sigmoid)),
+            grad_act * gate_part * sigmoid,
+        ],
+        axis=1,
+    ).astype(BF16)
+    grad_in = dot(grad_gate_up, up, ((1,), (1,)), BF16)
+    grad_up = dot(x_all, grad_gate_up, ((0,), (0,)), BF16)
+    grad_down = dot(grad_rows, activated, ((0,), (0,)), BF16)
+    parts = jnp.concatenate([out_part, grad_in, prob_cols.astype(BF16)], axis=1)
+    sums = sum_rows(parts.reshape(4, PLANES, rows, 2 * width + 128), 4)
+
+    output = (middle + sums[:, :width]).astype(BF16)
+    hi = sums[:, 2 * width + 1 : 2 * width + 1 + experts]
+    lo = sums[:, 2 * width + 33 : 2 * width + 33 + experts]
+    grad_probs = hi + lo
+    probs = jax.nn.softmax(dot(second_in, router, ((1,), (0,))), axis=-1)
+    grad_logits = (
+        probs * (grad_probs - jnp.sum(probs * grad_probs, axis=1, keepdims=True))
+    ).astype(BF16)
+    grad_second = sums[:, width : 2 * width] + dot(grad_logits, router, ((1,), (1,)))
+    grad_output = cotangent.astype(F32)
+    grad_normed_two = grad_second * gain_two
+    gain_two_part = jnp.sum(grad_second * normed_two, axis=0)
+    grad_middle = grad_output + inverse_two * (
+        grad_normed_two
+        - normed_two * jnp.mean(grad_normed_two * normed_two, axis=-1, keepdims=True)
+    )
+    router_part = dot(second_in, grad_logits, ((0,), (0,)))
+    grad_attention = grad_middle.astype(BF16)
+    grad_out_part = dot(mixed, grad_attention, ((0,), (0,)), BF16)
+    grad_mixed = dot(grad_attention, out_weight, ((1,), (1,)), BF16)
+
+    valid = jnp.array(
+        [[a <= i < b for i in range(WINDOW)] for a, b in KEEP], dtype=BF16
+    )[z]
+    grad_heads = swap_planes(windows(grad_mixed), 5).reshape(seqlen, WINDOW, HEAD_DIM)
+    grad_heads = grad_heads * valid[None, :, None]
+    row_delta = jnp.sum(grad_heads.astype(F32) * mixed_exact, axis=2).T
+    grad_values = jnp.einsum("hqk,qhd->khd", weights_low, grad_heads, preferred_element_type=F32)
+    grad_weights = jnp.einsum("qhd,khd->hqk", grad_heads, value_rows, preferred_element_type=F32)
+    grad_scores = (weights_exact * (grad_weights - row_delta[..., None])).astype(BF16)
+    grad_query = jnp.einsum("hqk,khd->qhd", grad_scores, key_rows, preferred_element_type=F32)
+    grad_keys = jnp.einsum("hqk,qhd->khd", grad_scores, query_rows, preferred_element_type=F32)
+    grad_projected = jnp.concatenate(
+        [
+            (rotate_back(grad_query, cosine, sine_table) * scale).reshape(seqlen, size),
+            rotate_back(grad_keys, cosine, sine_table).reshape(seqlen, size),
+            grad_values.reshape(seqlen, size),
+        ],
+        axis=1,
+    ).astype(BF16)
+    grad_qkv_part = dot(first_in, grad_projected, ((0,), (0,)), BF16)
+    first_part = dot(grad_projected, wq, ((1,), (1,)))
+    gain_one_part = jnp.sum(first_part * seq_normed, axis=0)
+    misc_part = jnp.concatenate(
+        [
+            router_part,
+            gain_one_part[:, None],
+            gain_two_part[:, None],
+            jnp.zeros((width, 128 - experts - 2), F32),
+        ],
+        axis=1,
+    ).astype(BF16)
+    half = width // 2
+    dense = jnp.stack([jnp.concatenate([grad_qkv_part, misc_part], axis=1), grad_out_part])
+    dense = dense.reshape(2, PLANES, 4, width // 16, 2, half)
+    dense = jnp.transpose(dense, (0, 4, 1, 2, 3, 5))
+    first_all, q_all, o_all = sum_dense(
+        first_part.astype(BF16).reshape(PLANES, rows, width), dense, 6
+    )
+    grad_first = jnp.sum(first_all.astype(F32), axis=0)
+    inputs = tokens.astype(F32)
+    inverse_one = rms_inverse(inputs)
+    normed_one = inputs * inverse_one
+    grad_normed_one = grad_first * gain_one
+    grad_tokens = grad_middle + inverse_one * (
+        grad_normed_one
+        - normed_one * jnp.mean(grad_normed_one * normed_one, axis=-1, keepdims=True)
+    )
+    q_all = q_all.reshape(4, 2, PLANES, width // 16, half)
+    q_all = jnp.transpose(q_all, (2, 0, 3, 1, 4)).reshape(PLANES, 4 * (width // 16), width)
+    o_all = o_all.reshape(4, 2, width // 16, half)
+    out_sum = jnp.transpose(o_all, (0, 2, 1, 3)).reshape(4 * (width // 16), width).astype(F32)
+    qkv_sum = jnp.concatenate(
+        [from_windows(q_all[:, :, i * size : (i + 1) * size]) for i in range(3)], axis=1
+    ).astype(F32)
+    misc_sum = jnp.sum(q_all[:, :, 3 * size :].astype(F32), axis=0)
+
+    grads = jnp.concatenate([grad_up, grad_down], axis=1).reshape(
+        PLANES, 2, width // PLANES // 2, 3 * FF
+    )
+    table = spread_grads(grads, 7).reshape(experts + 1, width // PLANES, 3 * FF)
+    up_sum = jnp.transpose(table[:, :, : 2 * FF], (1, 0, 2)).astype(F32)
+    down_sum = jnp.transpose(table[:, :, 2 * FF :], (1, 0, 2)).astype(F32)
+    return (
+        output,
+        grad_tokens.astype(BF16),
+        misc_sum[:, experts],
+        qkv_sum,
+        out_sum,
+        misc_sum[:, experts + 1],
+        misc_sum[:, :experts],
+        up_sum,
+        down_sum,
+    )
+
+
 def solution(mesh):
+    fits = mesh.shape["wide"] == 8 and mesh.shape["narrow"] == PLANES
     return jax.shard_map(
-        local,
+        expert_local if fits else local,
         mesh=mesh,
         in_specs=(
             P(("wide", "narrow"), None),

time: 2430 us -> 1010 us (0.42)
  waiting for transfers between devices: 1740 us -> 0 us
  Pallas kernels: 0 us -> 658 us
  blocking collectives: 190 us -> 0 us
  local copies, waits for them, and re-layouts: 193 us -> 128 us
  matrix products: 186 us -> 125 us
  starting transfers between devices: 27.6 us -> 0 us
  other arithmetic: 68.4 us -> 93.2 us
    all_gather x9 -> x0, waiting for transfers between devices: 708 us -> none  [the longest x1 375 us: local(): lax.all_gather(w_up, ('wide', 'narrow'), axis=0, tiled=True)]
    pallas_call x0 -> x7, Pallas kernels: none -> 658 us  [the longest x1 208 us: spread_inputs(): comm_call(spread_inputs_kernel, 'spread_inputs', 1, [jax.ShapeDtypeStruct...]
    all_to_all x4 -> x0, waiting for transfers between devices: 437 us -> none  [the longest x1 219 us: local(): lax.all_to_all(grad_rows, 'narrow', split_axis=2, concat_axis=1, tiled=True)]
    psum x1 -> x0, waiting for transfers between devices: 334 us -> none  [local(): lax.psum(shortened((expert_grads,) + tuple(dense_parts)), 'wide')]
    reduce_scatter x2 -> x0, waiting for transfers between devices: 199 us -> none  [the longest x1 171 us: local(): lax.psum_scatter(grad_qkv_weight.astype(jnp.bfloat16), 'narrow', scatter_...]
    all_gather x3 -> x0, blocking collectives: 118 us -> none  [the longest x1 59.6 us: local(): lax.all_gather(w_router, ('wide', 'narrow'), axis=0, tiled=True)]
    unnamed x149 -> x112, local copies, waits for them, and re-layouts: 91 us -> 17.2 us
    dot_general x29 -> x22, matrix products: 186 us -> 122 us  [the longest x16 106 us: dot(): lax.dot_general(a, b, ((dims[0], dims[1]), ((), ())), preferred_element_t...]
  transfers between devices with their start and end apart: 19 -> 0, of which waited for: 14 -> 0; matrix products, arithmetic and copies ran while one was open for 9% -> 0% of each run, Pallas kernels for 0% -> 0%
where the time goes in v1:
time: 1010 us
  Pallas kernels  658 us (65%)
  local copies, waits for them, and re-layouts  128 us (13%)
  matrix products  125 us (12%)
  other arithmetic  93.2 us (9%)
    pallas_call x1, Pallas kernels, spread_inputs(): comm_call(spread_inputs_kernel, 'spread_inputs', 1, [jax.ShapeDtypeStruct...  208 us
    pallas_call x1, Pallas kernels, spread_grads(): comm_call(spread_grads_kernel, 'spread_grads', collective, [jax.ShapeDtyp...  161 us
    pallas_call x1, Pallas kernels, sum_rows(): comm_call(sum_rows_kernel, 'sum_rows', collective, [jax.ShapeDtypeStruct(...  137 us
    dot_general x16, matrix products, dot(): lax.dot_general(a, b, ((dims[0], dims[1]), ((), ())), preferred_element_t...  106 us
    pallas_call x1, Pallas kernels, sum_dense(): comm_call(sum_dense_kernel, 'sum_dense', collective, [jax.ShapeDtypeStruc...  65.3 us
    pallas_call x1, Pallas kernels, gather_rows(): comm_call(gather_rows_kernel, 'gather_rows', collective, [jax.ShapeDtypeS...  59.7 us
    pallas_call x2, Pallas kernels, swap_planes(): comm_call(swap_planes_kernel, 'swap_planes', collective, [jax.ShapeDtypeS...  27.6 us
    convert_element_type x1, other arithmetic, expert_local(): up_sum = jnp.transpose(table[:, :, :2 * FF], (1, 0, 2)).astype(F32)  25.7 us

profile of v1, /device:TPU:29, one launch (start us, length us, event | category | flops | bytes accessed | tf_op | source)
XLA Modules:
  0.0 1006.4 jit_solution(13278343912017878998)
XLA Ops:
  0.7 1.3 dynamic-slice_bitcast_fusion
  2.7 1.1 fusion.41
  9.3 1.8 concatenate.63.cot
  11.2 1.2 slice_bitcast_fusion.31
  13.2 1.5 copy.163
  15.6 2.0 copy.217
  17.6 207.5 %spread_inputs.1 = (bf16[4,128,1280]{2,1,0:T(8,128)(2,1)}, bf16[4,16,128]{2,1,0:T(8,128)(2,1)}, bf16[8,4,40,1280]{3,2,1,0:T(8,128)(2,1)}, bf16[8,4,40,1280]{3,2,...) custom-call(bf16[128,1280]{1,0:T(8,128)(2,1)} %tok.1, ...), custom_call_target="tpu_custom_call" | custom-call | tf_op jit(solution)/shard_map/spread_inputs/pallas_call | solution.py:617
  225.8 1.6 multiply_reduce_fusion.1
  228.4 1.1 slice.302
  229.5 5.2 slice.307
  234.8 8.3 copy.210
  243.1 1.3 fusion.100
  245.3 4.2 fusion.19
  250.7 1.2 copy.167
  252.8 2.3 fusion.110
  255.1 3.2 fusion.104
  258.3 5.5 fusion.105
  264.9 12.2 %swap_planes.2 = bf16[4,128,384]{2,1,0:T(8,128)(2,1)} custom-call(bf16[4,128,384]{2,1,0:T(8,128)(2,1)} %copy.173.x), custom_call_target="tpu_custom_call" | custom-call | tf_op jit(solution)/shard_map/swap_planes/pallas_call | solution.py:645
  279.0 2.7 multiply_reduce_fusion.5
  281.9 1.3 fusion.109
  283.6 59.7 %gather_rows.1 = bf16[4,4,128,1280]{3,2,1,0:T(8,128)(2,1)} custom-call(bf16[128,1280]{1,0:T(8,128)(2,1)} %copy-done.7), custom_call_target="tpu_custom_call" | custom-call | tf_op jit(solution)/shard_map/gather_rows/pallas_call | solution.py:685
  343.3 4.2 fusion.108
  347.7 15.2 %fusion.9 = f32[2048,1792]{0,1:T(8,128)} fusion(bf16[2048,1280]{1,0:T(8,128)(2,1)S(1)} %bitcast.181, bf16[1280,2688]{1,0:T(8,128)(2,1)} %bitcast.218), kind=kOutput, calls=%fused_computation.25 | convolution fusion | flops 9395240960 | bytes 24510464 | tf_op jit(solution)/shard_map/dot_general | solution.py:953
  362.9 16.0 %multiply_convert_fusion.1 = (bf16[2048,896]{0,1:T(8,128)(2,1)}, bf16[2048,896]{0,1:T(8,128)(2,1)}, bf16[2048,896]{0,1:T(8,128)(2,1)S(1)}) fusion(f32[2048,1792]{0,1:T(8,128)} %fusion.9, bf16[1280,2688]{1,0:T(8,128)(2,1)} %bitcast.219, bf16[2048,1280]{0,1:T(8,128)(2,1)} %copy.210, f32[2048]{0:T(1024)S(1)} %get-tuple-element.58), kind=kOutput, calls=%fused_computation.17 | convolution fusion | flops 4734844928 | bytes 33234944 | tf_op jit(solution)/shard_map/dot_general | solution.py:953
  378.9 16.2 %convolution_convert_fusion.4 = bf16[1280,1792]{1,0:T(8,128)(2,1)} fusion(bf16[2048,1280]{1,0:T(8,128)(2,1)S(1)} %bitcast.182, bf16[2048,896]{0,1:T(8,128)(2,1)} %get-tuple-element.61, bf16[2048,896]{0,1:T(8,128)(2,1)} %get-tuple-element.60), kind=kOutput, calls=%fused_computation.14 | convolution fusion | flops 9412214784 | bytes 17170432 | tf_op jit(solution)/shard_map/dot_general | solution.py:953
  395.1 14.9 %convolution_convert_fusion.2 = bf16[2048,1280]{0,1:T(8,128)(2,1)} fusion(bf16[2048,896]{0,1:T(8,128)(2,1)} %get-tuple-element.61, bf16[2048,896]{0,1:T(8,128)(2,1)} %get-tuple-element.60, bf16[1280,2688]{1,0:T(8,128)(2,1)} %bitcast.220), kind=kOutput, calls=%fused_computation.12 | convolution fusion | flops 9412542464 | bytes 17170432 | tf_op jit(solution)/shard_map/dot_general | solution.py:953
  410.1 10.1 %fusion.1 = (bf16[2048,1280]{0,1:T(8,128)(2,1)}, f32[2048]{0:T(1024)S(1)}) fusion(f32[2048]{0:T(1024)S(1)} %get-tuple-element.58, bf16[2048,1280]{0,1:T(8,128)(2,1)} %copy.210, bf16[2048,896]{0,1:T(8,128)(2,1)S(1)} %get-tuple-element.62, bf16[1280,2688]{1,0:T(8,128)(2,1)} %bitcast.221), kind=kOutput, calls=%fused_computation.7 | convolution fusion | flops 4715968512 | bytes 16465920 | tf_op jit(solution)/shard_map/dot_general | solution.py:953
  420.2 8.5 fusion.11
  428.7 5.6 pad_maximum_fusion.2
  434.4 16.1 %pad_maximum_fusion = bf16[2048,2688]{0,1:T(8,128)(2,1)} fusion(bf16[2048,128]{0,1:T(8,128)(2,1)S(1)} %select_add_fusion, bf16[2048,1280]{0,1:T(8,128)(2,1)} %convolution_convert_fusion.2, bf16[2048,1280]{0,1:T(8,128)(2,1)} %get-tuple-element.63), kind=kLoop, calls=%fused_computation.6 | loop fusion | flops 33030144 | bytes 22020096 | tf_op jit(solution)/shard_map/concatenate | solution.py:1063
  450.5 14.6 %copy.177 = bf16[2048,2688]{1,0:T(8,128)(2,1)} copy(bf16[2048,2688]{0,1:T(8,128)(2,1)} %pad_maximum_fusion) | data formatting | bytes 22020096 | tf_op jit(solution)/shard_map/concatenate | solution.py:1063
  465.1 136.7 %sum_rows.1 = f32[128,2688]{1,0:T(8,128)} custom-call(bf16[4,4,128,2688]{3,2,1,0:T(8,128)(2,1)} %bitcast.179), custom_call_target="tpu_custom_call" | custom-call | tf_op jit(solution)/shard_map/sum_rows/pallas_call | solution.py:755
  601.9 1.2 multiply_reduce_fusion.6
  603.1 1.1 multiply_convert_fusion.9
  605.0 1.6 multiply_reduce_fusion.3
  606.7 2.1 multiply_add_fusion
  609.6 1.2 convolution_convert_fusion.5
  611.7 15.4 %swap_planes.3 = bf16[4,128,384]{2,1,0:T(8,128)(2,1)} custom-call(bf16[4,128,384]{2,1,0:T(8,128)(2,1)} %pad_maximum_fusion.10.x), custom_call_target="tpu_custom_call" | custom-call | tf_op jit(solution)/shard_map/swap_planes/pallas_call | solution.py:645
  627.1 1.2 copy.179
  628.5 5.5 convolution_convert_fusion.7
  634.0 1.4 multiply_reduce_fusion.2
  635.4 1.7 multiply_convert_fusion.3
  640.7 3.1 multiply_reduce_fusion
  643.8 3.3 convolution_convert_fusion.1
  647.8 13.1 %concatenate.75 = bf16[1280,1280]{0,1:T(8,128)(2,1)S(1)} concatenate(bf16[1280,1152]{0,1:T(8,128)(2,1)} %convolution_convert_fusion.1, bf16[1280,15]{0,1:T(8,128)(2,1)S(1)} %copy-done.34, bf16[1280,1]{0,1:T(2,128)(2,1)S(1)} %broadcast_in_dim.134, bf16[1280,1]{0,1:T(2,128)(2,1)S(1)} %broadcast_in_dim.135, bf16[1280,111]{0,1:T(8,128)(2,1)} %broadcast_in_dim.136), dimensions={1} | concatenate | bytes 6553600 | tf_op jit(solution)/shard_map/concatenate | solution.py:1119
  661.0 8.9 reshape.276
  669.9 9.3 copy.187
  679.2 2.2 convolution_convert_fusion.3
  681.4 3.1 stack.90
  684.5 2.5 copy.188
  687.4 3.5 maximum_bitcast_fusion.x
  690.9 65.3 %sum_dense.1 = (bf16[4,128,1280]{2,1,0:T(8,128)(2,1)}, bf16[8,4,80,640]{3,2,1,0:T(8,128)(2,1)}, bf16[8,80,640]{2,1,0:T(8,128)(2,1)}) custom-call(bf16[4,128,1280]{2,1,0:T(8,128)(2,1)} %bitcast.202, bf16[2,2,4,4,80,640]{5,4,3,2,1,0:T(8,128)(2,1)} %maximum_bitcast_fusion.x), custom_call_target="tpu_custom_call" | custom-call | tf_op jit(solution)/shard_map/sum_dense/pallas_call | solution.py:916
  756.2 2.4 convert_reduce_fusion
  758.6 5.3 copy.189
  764.0 3.8 reshape.268
  767.7 1.5 fusion.36
  769.2 2.4 fusion.40
  775.2 1.3 copy.213
  776.9 2.6 convert_element_type.239
  779.5 161.5 %spread_grads.1 = bf16[4,4,2,160,2688]{4,3,2,1,0:T(8,128)(2,1)} custom-call(bf16[4,2,160,2688]{3,2,1,0:T(8,128)(2,1)} %bitcast.183), custom_call_target="tpu_custom_call" | custom-call | tf_op jit(solution)/shard_map/spread_grads/pallas_call | solution.py:815
  940.9 8.0 slice.333
  948.9 15.9 %slice.332 = bf16[16,320,1792]{2,1,0:T(8,128)(2,1)} slice(bf16[16,320,2688]{2,1,0:T(8,128)(2,1)} %bitcast.178), slice={[0:16], [0:320], [0:1792]} | slice | bytes 36700160 | tf_op jit(solution)/shard_map/slice | solution.py:1147
  964.8 15.6 %convert_bitcast_fusion.1 = f32[320,16,896]{2,1,0:T(8,128)} fusion(bf16[16,320,896]{2,1,0:T(8,128)(2,1)} %slice.333), kind=kLoop, calls=%fused_computation.2 | loop fusion | flops 4587520 | bytes 27525120 | tf_op jit(solution)/shard_map/convert_element_type | solution.py:1148
  980.5 25.7 %convert_bitcast_fusion = f32[320,16,1792]{2,1,0:T(8,128)} fusion(bf16[16,320,1792]{2,1,0:T(8,128)(2,1)} %slice.332), kind=kLoop, calls=%fused_computation.1 | loop fusion | flops 9175040 | bytes 55050240 | tf_op jit(solution)/shard_map/convert_element_type | solution.py:1147
  (176 shorter events, 27.7 us)
Async XLA Ops:
  0.6 14.0 %copy-start.19 = (bf16[40,16,1792]{2,1,0:T(8,128)(2,1)S(1)}, bf16[40,16,1792]{2,1,0:T(8,128)(2,1)}, u32[]{:S(2)}) copy-start(bf16[40,16,1792]{2,1,0:T(8,128)(2,1)} %param.21) | copy-start | bytes 6881284
  11.2 241.1 %copy-start.15 = (f32[512,128]{0,1:T(8,128)}, f32[512,128]{0,1:T(8,128)S(1)}, u32[]{:S(2)}) copy-start(f32[512,128]{0,1:T(8,128)S(1)} %get-tuple-element.124) | copy-start | bytes 786436
  11.2 241.1 %copy-start.17 = (f32[512,128]{0,1:T(8,128)}, f32[512,128]{0,1:T(8,128)S(1)}, u32[]{:S(2)}) copy-start(f32[512,128]{0,1:T(8,128)S(1)} %get-tuple-element.125) | copy-start | bytes 786436
  227.5 17.4 %copy-start.37 = (f32[512]{0:T(512)}, f32[512]{0:T(512)S(1)}, u32[]{:S(2)}) copy-start(f32[512]{0:T(512)S(1)} %rsqrt_bitcast_fusion) | copy-start | bytes 6148
  234.8 10.0 copy-start.5
  244.9 4.6 copy-start.35
  245.3 4.2 copy-start.22
  251.8 6.5 copy-start.20
  252.8 5.5 copy-start.9
  252.8 5.5 copy-start.11
  252.8 2.3 copy-start.33
  258.3 20.7 %copy-start.4 = (bf16[128,1280]{1,0:T(8,128)(2,1)S(1)}, bf16[128,1280]{1,0:T(8,128)(2,1)}, u32[]{:S(2)}) copy-start(bf16[128,1280]{1,0:T(8,128)(2,1)} %tok.1) | copy-start | bytes 983044
  278.0 5.3 copy-start.30
  278.0 5.3 copy-start.32
  279.0 4.3 copy-start.26
  279.0 4.3 copy-start.28
  281.9 1.7 copy-start.7
  343.3 4.4 copy-start
  378.9 31.2 %copy-start.43 = (bf16[2048,896]{0,1:T(8,128)(2,1)}, bf16[2048,896]{0,1:T(8,128)(2,1)S(1)}, u32[]{:S(2)}) copy-start(bf16[2048,896]{0,1:T(8,128)(2,1)S(1)} %get-tuple-element.62) | copy-start | bytes 11010052
  378.9 41.3 %slice-start = ((s8[5242880]{0:T(1024)(128)(4,1)}), s8[1048576]{0:T(1024)(128)(4,1)S(1)}, s32[]{:S(2)}) async-start(s8[5242880]{0:T(1024)(128)(4,1)} %bitcast.193), calls=%async_computation | async-start | bytes 2097152
  395.1 25.1 %slice-start.1 = ((s8[5242880]{0:T(1024)(128)(4,1)}), s8[4194304]{0:T(1024)(128)(4,1)S(1)}, s32[]{:S(2)}) async-start(s8[5242880]{0:T(1024)(128)(4,1)} %bitcast.193), calls=%async_computation.1 | async-start | bytes 8388608
  428.7 5.6 copy-start.40
  428.7 5.6 copy-start.41
  465.1 139.1 %copy-start.8 = (bf16[128,1280]{1,0:T(8,128)(2,1)S(1)}, bf16[128,1280]{1,0:T(8,128)(2,1)}, u32[]{:S(2)}) copy-start(bf16[128,1280]{1,0:T(8,128)(2,1)} %copy-done.7) | copy-start | bytes 983044
  465.1 141.6 %copy-start.21 = (bf16[128,1280]{1,0:T(8,128)(2,1)S(1)}, bf16[128,1280]{1,0:T(8,128)(2,1)}, u32[]{:S(2)}) copy-start(bf16[128,1280]{1,0:T(8,128)(2,1)} %param.15) | copy-start | bytes 983044
  601.9 7.7 copy-start.13
  608.7 0.9 copy-start.3
  628.5 6.9 copy-start.14
  634.0 3.1 copy-start.10
  635.4 2.4 copy-start.12
  635.4 2.4 copy-start.18
  637.8 1.0 copy-start.16
  638.3 1.3 copy-start.6
  638.3 2.3 copy-start.24
  638.3 2.3 copy-start.38
  638.4 2.4 copy-start.42
  640.7 3.1 copy-start.23
  643.8 4.0 copy-start.34
  669.9 9.3 copy-start.27
  669.9 9.3 copy-start.29
  669.9 9.3 copy-start.31
  684.5 2.9 copy-start.1
  763.9 3.8 copy-start.36
  763.9 3.8 copy-start.39
  767.7 6.5 copy-start.25
  774.3 2.1 copy-start.2

commit v2 on v1

--- a/solution.py
+++ b/solution.py
@@ -499,7 +499,7 @@
             pltpu.SemaphoreType.DMA((sems,)),
         ],
         compiler_params=pltpu.CompilerParams(
-            collective_id=collective, has_side_effects=True, vmem_limit_bytes=56 * 2**20
+            collective_id=collective, has_side_effects=True, vmem_limit_bytes=62 * 2**20
         ),
         name=name,
     )
@@ -653,46 +653,6 @@
     )(x)[0]
 
 
-def gather_rows_kernel(x, out, send_sems, recv_sems):
-    w, z = place()
-    chip = w // 2
-    greet(w, z)
-    net = Net(send_sems, recv_sems)
-    own = net.keep(x, out.at[chip, z])
-    ring = {}
-    for step in (1, 2, 3):
-        to, _ = other_plane(z, step)
-        ring[step] = net.send(x, out.at[chip, z], (w, to))
-    own.wait()
-    gathers = []
-    for step in (0, 1, 2, 3):
-        _, source = other_plane(z, step)
-        if step:
-            ring[step].wait_recv()
-        gather = PlaneGather(
-            net, w, z, lambda i, source=source: out.at[i // 2, source], step, False
-        )
-        gather.begin()
-        gathers.append(gather)
-    for gather in gathers:
-        gather.relay()
-    for gather in gathers:
-        gather.end()
-    net.finish()
-
-
-def gather_rows(x, collective):
-    return comm_call(
-        gather_rows_kernel,
-        "gather_rows",
-        collective,
-        [jax.ShapeDtypeStruct((4, PLANES) + x.shape, x.dtype)],
-        [pl.ANY],
-        [pl.ANY],
-        40,
-    )(x)[0]
-
-
 def add_blocks(out, *terms):
     rows = out.shape[0]
 
@@ -707,235 +667,819 @@
     lax.fori_loop(0, rows // 16, body, 0)
 
 
-def sum_rows_kernel(x, out, got_one, got_two, got_far, part, ready, send_sems, recv_sems):
+def mul(a, b, over_a, over_b):
+    return lax.dot_general(a, b, (((over_a,), (over_b,)), ((), ())), preferred_element_type=F32)
+
+
+def at(start, size):
+    return pl.ds(pl.multiple_of(start, 128), size)
+
+
+def loop(first, last, body):
+    def step(i, carry):
+        body(i)
+        return carry
+
+    lax.fori_loop(first, last, step, 0)
+
+
+def experts_kernel(
+    x_in, cot_in, weights_in, misc_in, grads_o, outs_o, sums_o,
+    x, cot, weights, misc, act, scaled, slopes, gate, outs, parts, got_one, got_two, got_far, stage,
+    load_sems, send_sems, recv_sems,
+):
     w, z = place()
     chip = w // 2
+    expert = chip * PLANES + z
+    rows, width = x_in.shape
+    hidden = weights.shape[1] // 3
+    group_rows = 4 * rows
+
+    def remote(kind, step, src, dst, device):
+        return pltpu.make_async_remote_copy(
+            src_ref=src,
+            dst_ref=dst,
+            send_sem=send_sems.at[kind, step],
+            recv_sem=recv_sems.at[kind, step],
+            device_id=device,
+            device_id_type=MESH_IDS,
+        )
+
+    def plane_of(step, sign):
+        return lax.rem(z + PLANES + sign * step, PLANES)
+
+    def step_at(turn):
+        step = 0
+        for plane, steps in enumerate(((3, 2, 1, 0), (1, 3, 2, 0), (3, 1, 2, 0), (1, 2, 3, 0))):
+            for number, value in enumerate(steps):
+                step = jnp.where((z == plane) & (turn == number), value, step)
+        return step
+
+    def axes(turn):
+        first = 1 + lax.rem(turn, 2)
+        return first, 3 - first
+
+    def ring(step, up):
+        to = lax.rem(step + 1, 4) if up else lax.rem(step + 3, 4)
+        return pltpu.make_async_remote_copy(
+            src_ref=x.at[step, chip],
+            dst_ref=x.at[to, chip],
+            send_sem=send_sems.at[0 if up else 8, step],
+            recv_sem=recv_sems.at[0, to],
+            device_id=(w, z + 1 if up else z - 1),
+            device_id_type=MESH_IDS,
+        )
+
+    def goes(step, up):
+        if up:
+            return (z >= step) & (z < PLANES - 1)
+        return ((z < step) | (step == 0)) & (z > 0)
+
+    def pass_on(step):
+        for up in (True, False):
+
+            @pl.when(goes(step, up))
+            def _():
+                ring(step, up).start()
+
+    def arrive(step):
+        pltpu.make_async_remote_copy(
+            src_ref=x.at[step, chip],
+            dst_ref=x.at[step, chip],
+            send_sem=send_sems.at[0, step],
+            recv_sem=recv_sems.at[0, step],
+            device_id=(w, z),
+            device_id_type=MESH_IDS,
+        ).wait_recv()
+
+    def direct(step, flip):
+        block = x.at[step, chip]
+        return remote(flip, step, block, block, (w ^ (2 * flip), z))
+
+    def across(turn):
+        first, second = axes(turn)
+        step = step_at(turn)
+        block = x.at[step, chip ^ first]
+        return remote(3, step, block, block, (w ^ (2 * second), z))
+
+    def near(turn, which):
+        first, _ = axes(turn)
+        step = step_at(turn)
+        block = chip ^ 3 if which else chip ^ first
+        return remote(
+            4 + which, step, parts.at[step, block], got_one.at[step, which], (w ^ (2 * first), z)
+        )
+
+    def cross(turn):
+        _, second = axes(turn)
+        step = step_at(turn)
+        return remote(
+            6, step, parts.at[step, chip ^ second], got_two.at[step], (w ^ (2 * second), z)
+        )
+
+    def far(step):
+        return remote(7, step, parts.at[step, chip], got_far.at[step - 1], (w, plane_of(step, -1)))
+
+    def cot_load(step):
+        return pltpu.make_async_copy(
+            cot_in.at[:, plane_of(step, -1)], cot.at[step], load_sems.at[step]
+        )
+
+    def outs_out(turn):
+        return pltpu.make_async_copy(
+            outs.at[lax.rem(turn, 2)], outs_o.at[step_at(turn)], load_sems.at[9 + lax.rem(turn, 2)]
+        )
+
+    def grads_out(low, size, slot):
+        return pltpu.make_async_copy(
+            stage.at[slot, :, pl.ds(0, size)], grads_o.at[:, low], load_sems.at[4 + slot]
+        )
+
+    loads = [
+        pltpu.make_async_copy(src, dst, load_sems.at[6 + i])
+        for i, (src, dst) in enumerate(((x_in, x.at[0, chip]), (misc_in, misc), (weights_in, weights)))
+    ]
+    for load in loads:
+        load.start()
+    loop(0, 4, lambda step: cot_load(step).start())
     greet(w, z)
-    net = Net(send_sems, recv_sems)
-    steps = (1, 2, 3, 0)
-    near, cross, far = {}, {}, []
-    for step in steps:
-        to, _ = other_plane(z, step)
-        first = 1 if step % 2 == 0 else 2
-        peer = (w ^ (2 * first), z)
-        near[step] = (
-            net.send(x.at[chip ^ 3, to], got_one.at[step, 1], peer),
-            net.send(x.at[chip ^ first, to], got_one.at[step, 0], peer),
-        )
-    for step in steps:
-        to, _ = other_plane(z, step)
-        first = 1 if step % 2 == 0 else 2
-        second = 3 - first
-        near[step][0].wait_recv()
-        add_blocks(part.at[step], x.at[chip ^ second, to], got_one.at[step, 1])
-        cross[step] = net.send(part.at[step], got_two.at[step], (w ^ (2 * second), z))
-    for step in steps:
-        to, _ = other_plane(z, step)
-        near[step][1].wait_recv()
-        cross[step].wait_recv()
-        if step:
-            add_blocks(ready.at[step - 1], x.at[chip, to], got_one.at[step, 0], got_two.at[step])
-            far.append(net.send(ready.at[step - 1], got_far.at[step - 1], (w, to)))
-    for copy in far:
-        copy.wait_recv()
+    loads[0].wait()
+    pass_on(0)
+
+    def begin(turn):
+        step = step_at(turn)
+
+        @pl.when(turn < 3)
+        def _():
+            arrive(step)
+            pass_on(step)
+
+        direct(step, 1).start()
+        direct(step, 2).start()
+
+    def relay(turn):
+        step = step_at(turn)
+        direct(step, 1).wait_recv()
+        direct(step, 2).wait_recv()
+        across(turn).start()
+
+    begin(0)
+    begin(1)
+    relay(0)
+    begin(2)
+    begin(3)
+    loads[1].wait()
+    loads[2].wait()
+
+    def first_half(step):
+        cot_load(step).wait()
+        rows_in = x[step].reshape(group_rows, width)
+        members = cot[step, :, :, width:].reshape(group_rows, 128).astype(F32)
+        logits = mul(rows_in, misc[...], 1, 0)
+        lane = lax.broadcasted_iota(jnp.int32, logits.shape, 1)
+        routed = (lane > 0) & (lane < 16)
+        top = jnp.max(jnp.where(routed, logits, -1e30), axis=1, keepdims=True)
+        powers = jnp.where(routed, jnp.exp(logits - top), 0.0)
+        probs = jnp.where(lane == 0, 1.0, powers / jnp.sum(powers, axis=1, keepdims=True))
+        own = jnp.where(lane == expert, members, 0.0)
+        gate[0] = jnp.broadcast_to(jnp.sum(probs * own, axis=1, keepdims=True), gate.shape[1:])
+        gate[1] = own
+
+        def hidden_chunk(low, size):
+            here = x[step].reshape(group_rows, width)
+            gate_part = mul(here, weights[:, at(low, size)], 1, 0)
+            up_part = mul(here, weights[:, at(hidden + low, size)], 1, 0)
+            grad_act = mul(
+                cot[step, :, :, :width].reshape(group_rows, width),
+                weights[:, at(2 * hidden + low, size)],
+                1,
+                0,
+            )
+            scale = gate[0][:, :1]
+            grad_act = grad_act * scale
+            sigmoid = 1.0 / (1.0 + jnp.exp(-gate_part))
+            silu = gate_part * sigmoid
+            activated = (silu * up_part).astype(BF16)
+            act[:, at(low, size)] = activated
+            scaled[step, :, at(low, size)] = (activated.astype(F32) * scale).astype(BF16)
+            slopes[step, :, at(low, size)] = (
+                grad_act * up_part * (sigmoid + silu * (1.0 - sigmoid))
+            ).astype(BF16)
+            slopes[step, :, at(hidden + low, size)] = (grad_act * silu).astype(BF16)
+
+        loop(0, hidden // 256, lambda i: hidden_chunk(i * 256, 256))
+        if hidden % 256:
+            hidden_chunk(hidden // 256 * 256, hidden % 256)
+
+    def second_half(turn, step):
+        def width_body(i, total):
+            low = i * 256
+            expert_rows = mul(act[...], weights[at(low, 256), 2 * hidden :], 1, 1)
+            expert_rows = expert_rows.astype(BF16).astype(F32)
+            outs[lax.rem(turn, 2), :, :, at(low, 256)] = (
+                (expert_rows * gate[0][:, :1]).astype(BF16).reshape(4, rows, 256)
+            )
+            product = expert_rows * cot[step, :, :, at(low, 256)].reshape(group_rows, 256).astype(F32)
+            grad_in = mul(slopes[step], weights[at(low, 256), : 2 * hidden], 1, 1)
+            parts[step, :, :, at(low, 256)] = grad_in.astype(BF16).reshape(4, rows, 256)
+            return total + product[:, :128] + product[:, 128:]
+
+        total = lax.fori_loop(0, width // 256, width_body, jnp.zeros((group_rows, 128), F32))
+        prob = jnp.sum(total, axis=1, keepdims=True) * gate[1]
+        high = prob.astype(BF16)
+        low = (prob - high.astype(F32)).astype(BF16)
+        low = pltpu.roll(low.astype(F32), 32, 1).astype(BF16)
+        parts[step, :, :, width:] = (high + low).reshape(4, rows, 128)
+
+    def send_cross(turn):
+        _, second = axes(turn)
+        step = step_at(turn)
+        near(turn, 1).wait_recv()
+        block = parts.at[step, chip ^ second]
+        add_blocks(block, block, got_one.at[step, 1])
+        cross(turn).start()
+
+    def send_far(turn):
+        step = step_at(turn)
+        near(turn, 0).wait_recv()
+        cross(turn).wait_recv()
+        block = parts.at[step, chip]
+        add_blocks(block, block, got_one.at[step, 0], got_two.at[step])
+        far(step).start()
+
+    def group(turn):
+        step = step_at(turn)
+        across(turn).wait_recv()
+        first_half(step)
+
+        @pl.when(turn < 2)
+        def _():
+            relay(2 * turn + 1)
+
+        @pl.when(turn > 1)
+        def _():
+            outs_out(turn - 2).wait()
+
+        second_half(turn, step)
+        near(turn, 1).start()
+        near(turn, 0).start()
+        outs_out(turn).start()
+
+        @pl.when(turn == 0)
+        def _():
+            relay(2)
+
+        @pl.when(turn > 0)
+        def _():
+            send_cross(turn - 1)
+
+        @pl.when(turn > 1)
+        def _():
+            send_far(turn - 2)
+
+    loop(0, 4, group)
+
+    def weight_chunk(left, right, low, size, offset, i):
+        slot = lax.rem(i, 2)
+
+        @pl.when(i >= 2)
+        def _():
+            grads_out(pl.ds(0, 256), 256, slot).wait()
+
+        total = None
+        for step in range(4):
+            term = mul(
+                left[step, :, :, :width].reshape(group_rows, width), right[step, :, at(low, size)], 0, 0
+            )
+            total = term if total is None else total + term
+        stage[slot, :, :size] = total.astype(BF16)
+        grads_out(at(offset + low, size), size, slot).start()
+
+    ups, downs = 2 * hidden // 256, hidden // 256
+
+    def up_chunk(i):
+        weight_chunk(x, slopes, i * 256, 256, 0, i)
+
+    def down_chunk(i):
+        weight_chunk(cot, scaled, (i - ups) * 256, 256, 2 * hidden, i)
+
+    loop(0, 3, up_chunk)
+    send_cross(3)
+    send_far(2)
+    loop(3, ups, up_chunk)
+    loop(ups, ups + downs, down_chunk)
+    last = ups + downs
+    if hidden % 256:
+        weight_chunk(cot, scaled, downs * 256, hidden % 256, 2 * hidden, jnp.int32(last))
+        grads_out(pl.ds(0, 256), 256, (last - 1) % 2).wait()
+        grads_out(pl.ds(0, hidden % 256), hidden % 256, last % 2).wait()
+    else:
+        grads_out(pl.ds(0, 256), 256, last % 2).wait()
+        grads_out(pl.ds(0, 256), 256, (last - 1) % 2).wait()
+    outs_out(2).wait()
+    outs_out(3).wait()
+    near(3, 0).wait_recv()
+    cross(3).wait_recv()
+    loop(1, 4, lambda step: far(step).wait_recv())
     add_blocks(
-        out,
-        x.at[chip, z],
+        sums_o,
+        parts.at[0, chip],
         got_one.at[0, 0],
         got_two.at[0],
         got_far.at[0],
         got_far.at[1],
         got_far.at[2],
     )
-    net.finish()
-
-
-def sum_rows(x, collective):
-    rows, width = x.shape[2:]
-    return comm_call(
-        sum_rows_kernel,
-        "sum_rows",
-        collective,
-        [jax.ShapeDtypeStruct((rows, width), F32)],
-        [pltpu.VMEM],
-        [pltpu.VMEM],
-        24,
-        [
+
+    def settle(turn):
+        step = step_at(turn)
+        direct(step, 1).wait_send()
+        direct(step, 2).wait_send()
+        across(turn).wait_send()
+        near(turn, 0).wait_send()
+        near(turn, 1).wait_send()
+        cross(turn).wait_send()
+
+        @pl.when(turn < 3)
+        def _():
+            far(step).wait_send()
+
+        for up in (True, False):
+
+            @pl.when(goes(step, up))
+            def _():
+                ring(step, up).wait_send()
+
+    loop(0, 4, settle)
+
+
+def run_experts(second_in, cot_all, weights, misc, collective):
+    rows, width = second_in.shape
+    hidden = weights.shape[1] // 3
+    sums_width = width + 128
+    block = (rows, sums_width)
+    return pl.pallas_call(
+        experts_kernel,
+        out_shape=[
+            jax.ShapeDtypeStruct((width, 3 * hidden), BF16),
+            jax.ShapeDtypeStruct((4, 4, rows, width), BF16),
+            jax.ShapeDtypeStruct((rows, sums_width), F32),
+        ],
+        in_specs=[pl.BlockSpec(memory_space=pl.ANY)] * 4,
+        out_specs=[
+            pl.BlockSpec(memory_space=pl.ANY),
+            pl.BlockSpec(memory_space=pl.ANY),
+            pl.BlockSpec(memory_space=pltpu.VMEM),
+        ],
+        scratch_shapes=[
+            pltpu.VMEM((4, 4, rows, width), BF16),
+            pltpu.VMEM((4, 4, rows, width + 128), BF16),
+            pltpu.VMEM((width, 3 * hidden), BF16),
+            pltpu.VMEM((width, 128), BF16),
+            pltpu.VMEM((4 * rows, hidden), BF16),
+            pltpu.VMEM((4, 4 * rows, hidden), BF16),
+            pltpu.VMEM((4, 4 * rows, 2 * hidden), BF16),
+            pltpu.VMEM((2, 4 * rows, 128), F32),
+            pltpu.VMEM((2, 4, rows, width), BF16),
+            pltpu.VMEM((4, 4) + block, BF16),
+            pltpu.VMEM((4, 2) + block, BF16),
+            pltpu.VMEM((4,) + block, BF16),
+            pltpu.VMEM((3,) + block, BF16),
+            pltpu.VMEM((2, width, 256), BF16),
+            pltpu.SemaphoreType.DMA((11,)),
+            pltpu.SemaphoreType.DMA((9, 4)),
+            pltpu.SemaphoreType.DMA((8, 4)),
+        ],
+        compiler_params=pltpu.CompilerParams(
+            collective_id=collective, has_side_effects=True, vmem_limit_bytes=62 * 2**20
+        ),
+        name="experts",
+    )(second_in, cot_all, weights, misc)
+
+
+def finish_kernel(
+    outs_in, grads_in, first_in, dense_q, dense_o, sums_o, table_o, first_o, q_o, o_o,
+    outs, outs_one, outs_two, outs_far, grads_own, grads_got, dense, dense_got, dense_one,
+    dense_two, dense_far, dense_sum, load_sems, send_sems, recv_sems,
+):
+    w, z = place()
+    chip, core = w // 2, w % 2
+    steps = (1, 2, 3, 0)
+    block_rows = o_o.shape[0] // 4
+    half = o_o.shape[1] // 2
+    plane_rows = o_o.shape[0]
+
+    def remote(kind, step, src, dst, device):
+        return pltpu.make_async_remote_copy(
+            src_ref=src,
+            dst_ref=dst,
+            send_sem=send_sems.at[kind, step],
+            recv_sem=recv_sems.at[kind, step],
+            device_id=device,
+            device_id_type=MESH_IDS,
+        )
+
+    def plane_of(step, sign):
+        return lax.rem(z + PLANES + sign * step, PLANES)
+
+    def axes(step):
+        first = 1 + lax.rem(step, 2)
+        return first, 3 - first
+
+    class Gather:
+        def __init__(self, base, step, turn, slot):
+            self.base, self.step, self.slot = base, step, slot
+            self.first, self.second = axes(turn)
+
+        def copy(self, kind, owner, flip):
+            ref = self.slot(owner)
+            return remote(self.base + kind, self.step, ref, ref, (w ^ flip, z))
+
+        def begin(self):
+            self.copy(0, w, 2).start()
+            self.copy(1, w, 4).start()
+            self.copy(2, w, 1).start()
+
+        def relay(self):
+            self.copy(0, w, 2).wait_recv()
+            self.copy(1, w, 4).wait_recv()
+            self.across().start()
+            self.copy(4, w ^ 2, 1).start()
+            self.copy(5, w ^ 4, 1).start()
+
+        def across(self):
+            return self.copy(3, w ^ (2 * self.first), 2 * self.second)
+
+        def end(self):
+            self.across().wait_recv()
+            self.copy(6, w ^ 6, 1).start()
+
+        def settle(self):
+            for copy in (
+                self.copy(0, w, 2),
+                self.copy(1, w, 4),
+                self.copy(2, w, 1),
+                self.across(),
+                self.copy(4, w ^ 2, 1),
+                self.copy(5, w ^ 4, 1),
+                self.copy(6, w ^ 6, 1),
+            ):
+                copy.wait_send()
+            for kind in (2, 4, 5, 6):
+                self.copy(kind, w, 1).wait_recv()
+
+    def grads_load(step):
+        return pltpu.make_async_copy(
+            grads_in.at[plane_of(step, 1), core], grads_own.at[step], load_sems.at[0, step]
+        )
+
+    def grads_swap(step):
+        return remote(
+            0, step, grads_in.at[plane_of(step, 1), 1 - core], grads_got.at[step], (w ^ 1, z)
+        )
+
+    def grads_ring(step):
+        return remote(1, step, grads_own.at[step], table_o.at[chip, z, core], (w, plane_of(step, 1)))
+
+    def grads_keep():
+        return pltpu.make_async_copy(
+            grads_own.at[0], table_o.at[chip, z, core], load_sems.at[1, 0]
+        )
+
+    def grads_gather(step):
+        source = plane_of(step, -1)
+        return Gather(2, step, step, lambda i: table_o.at[i // 2, source, i % 2])
+
+    def outs_load(step):
+        return pltpu.make_async_copy(outs_in.at[step], outs.at[step], load_sems.at[2, step])
+
+    def near(step, which):
+        first, _ = axes(step)
+        block = chip ^ 3 if which else chip ^ first
+        return remote(
+            9 + which, step, outs.at[step, block], outs_one.at[step, which], (w ^ (2 * first), z)
+        )
+
+    def cross(step):
+        _, second = axes(step)
+        return remote(
+            11, step, outs.at[step, chip ^ second], outs_two.at[step], (w ^ (2 * second), z)
+        )
+
+    def far(step):
+        return remote(12, step, outs.at[step, chip], outs_far.at[step - 1], (w, plane_of(step, -1)))
+
+    def dense_part(kind, step, side):
+        rows = pl.ds(pl.multiple_of(plane_of(step, 1) * plane_rows, 16), plane_rows)
+        return (dense_q, dense_o)[kind].at[rows, at(side * half, half)]
+
+    def dense_load(kind, step):
+        return pltpu.make_async_copy(
+            dense_part(kind, step, core), dense.at[kind, step], load_sems.at[3 + kind, step]
+        )
+
+    def dense_swap(kind, step):
+        return remote(
+            13 + 4 * kind, step, dense_part(kind, step, 1 - core), dense_got.at[kind, step], (w ^ 1, z)
+        )
+
+    def rows_of(block):
+        return pl.ds(pl.multiple_of(block * block_rows, 16), block_rows)
+
+    def dense_axes(kind):
+        return 1 + kind, 2 - kind
+
+    def dense_near(kind, step, which):
+        first, _ = dense_axes(kind)
+        block = chip ^ 3 if which else chip ^ first
+        return remote(
+            14 + 4 * kind + which,
+            step,
+            dense.at[kind, step, rows_of(block)],
+            dense_one.at[kind, step, which],
+            (w ^ (2 * first), z),
+        )
+
+    def dense_cross(kind, step):
+        _, second = dense_axes(kind)
+        return remote(
+            16 + 4 * kind,
+            step,
+            dense.at[kind, step, rows_of(chip ^ second)],
+            dense_two.at[kind, step],
+            (w ^ (2 * second), z),
+        )
+
+    def place_of(owner):
+        return rows_of(owner // 2), at(lax.rem(owner, 2) * half, half)
+
+    def dense_ring(kind, step):
+        own = dense.at[kind, step, rows_of(chip)]
+        rows, columns = place_of(w)
+        to = q_o.at[z, rows, columns] if kind == 0 else dense_far.at[step - 1]
+        return remote(21 + kind, step, own, to, (w, plane_of(step, 1)))
+
+    def dense_keep():
+        rows, columns = place_of(w)
+        return pltpu.make_async_copy(
+            dense.at[0, 0, rows_of(chip)], q_o.at[z, rows, columns], load_sems.at[1, 1]
+        )
+
+    def dense_last():
+        rows, columns = place_of(w)
+        return pltpu.make_async_copy(dense_sum, o_o.at[rows, columns], load_sems.at[1, 2])
+
+    def q_slot(step):
+        source = plane_of(step, -1)
+
+        def slot(owner):
+            rows, columns = place_of(owner)
+            return q_o.at[source, rows, columns]
+
+        return slot
+
+    def o_slot(owner):
+        rows, columns = place_of(owner)
+        return o_o.at[rows, columns]
+
+    def q_gather(step):
+        return Gather(23, step, step, q_slot(step))
+
+    def o_gather():
+        return Gather(30, 0, 0, o_slot)
+
+    def first_ring(step):
+        return remote(37, step, first_in.at[plane_of(step, 1)], first_o.at[z], (w, plane_of(step, 1)))
+
+    def first_keep():
+        return pltpu.make_async_copy(first_in.at[z], first_o.at[z], load_sems.at[1, 3])
+
+    for step in steps:
+        grads_load(step).start()
+    for step in steps:
+        outs_load(step).start()
+        for kind in (0, 1):
+            dense_load(kind, step).start()
+    first_keep().start()
+    greet(w, z)
+    for step in steps:
+        grads_swap(step).start()
+    for step in steps:
+        for kind in (0, 1):
+            dense_swap(kind, step).start()
+    for step in (1, 2, 3):
+        first_ring(step).start()
+
+    def grads_ready(step):
+        grads_load(step).wait()
+        grads_swap(step).wait_recv()
+        add_blocks(grads_own.at[step], grads_own.at[step], grads_got.at[step])
+
+    def dense_ready(kind, step):
+        dense_load(kind, step).wait()
+        dense_swap(kind, step).wait_recv()
+        add_blocks(dense.at[kind, step], dense.at[kind, step], dense_got.at[kind, step])
+        dense_near(kind, step, 1).start()
+        dense_near(kind, step, 0).start()
+
+    loop(1, 4, lambda step: (grads_ready(step), grads_ring(step).start()))
+    grads_ready(0)
+    keep = grads_keep()
+    keep.start()
+
+    def dense_start(step):
+        dense_ready(0, step)
+        dense_ready(1, step)
+
+    loop(0, 4, dense_start)
+    keep.wait()
+    grads_gather(0).begin()
+
+    def outs_start(step):
+        outs_load(step).wait()
+        near(step, 1).start()
+        near(step, 0).start()
+
+    loop(0, 4, outs_start)
+
+    def dense_cross_start(step):
+        for kind in (0, 1):
+            _, second = dense_axes(kind)
+            dense_near(kind, step, 1).wait_recv()
+            block = dense.at[kind, step, rows_of(chip ^ second)]
+            add_blocks(block, block, dense_one.at[kind, step, 1])
+            dense_cross(kind, step).start()
+
+    loop(0, 4, dense_cross_start)
+
+    def grads_next(step):
+        grads_ring(step).wait_recv()
+        grads_gather(step).begin()
+
+    loop(1, 2, grads_next)
+
+    def outs_cross(step):
+        _, second = axes(step)
+        near(step, 1).wait_recv()
+        block = outs.at[step, chip ^ second]
+        add_blocks(block, block, outs_one.at[step, 1])
+        cross(step).start()
+
+    loop(0, 4, outs_cross)
+
+    def dense_finish(step):
+        for kind in (0, 1):
+            dense_near(kind, step, 0).wait_recv()
+            dense_cross(kind, step).wait_recv()
+            block = dense.at[kind, step, rows_of(chip)]
+            add_blocks(block, block, dense_one.at[kind, step, 0], dense_two.at[kind, step])
+
+    loop(0, 4, dense_finish)
+
+    def dense_ring_start(step):
+        dense_ring(0, step).start()
+        dense_ring(1, step).start()
+
+    loop(1, 4, dense_ring_start)
+    keep = dense_keep()
+    keep.start()
+    loop(2, 3, grads_next)
+    loop(0, 1, lambda step: grads_gather(step).relay())
+    keep.wait()
+    q_gather(0).begin()
+
+    def outs_finish(step):
+        near(step, 0).wait_recv()
+        cross(step).wait_recv()
+        block = outs.at[step, chip]
+        add_blocks(block, block, outs_one.at[step, 0], outs_two.at[step])
+
+        @pl.when(step > 0)
+        def _():
+            far(step).start()
+
+    loop(0, 4, outs_finish)
+    loop(3, 4, grads_next)
+
+    def q_next(step):
+        dense_ring(0, step).wait_recv()
+        q_gather(step).begin()
+        dense_ring(1, step).wait_recv()
+
+    loop(1, 4, q_next)
+    add_blocks(
+        dense_sum, dense.at[1, 0, rows_of(chip)], dense_far.at[0], dense_far.at[1], dense_far.at[2]
+    )
+    keep = dense_last()
+    keep.start()
+    keep.wait()
+    o_gather().begin()
+    loop(1, 4, lambda step: grads_gather(step).relay())
+    loop(0, 4, lambda step: q_gather(step).relay())
+    o_gather().relay()
+    loop(1, 4, lambda step: far(step).wait_recv())
+    add_blocks(sums_o, outs.at[0, chip], outs_far.at[0], outs_far.at[1], outs_far.at[2])
+    loop(0, 4, lambda step: grads_gather(step).end())
+    loop(0, 4, lambda step: q_gather(step).end())
+    o_gather().end()
+    loop(0, 4, lambda step: grads_gather(step).settle())
+    loop(0, 4, lambda step: q_gather(step).settle())
+    o_gather().settle()
+    first_keep().wait()
+
+    def settle(step):
+        grads_swap(step).wait_send()
+        near(step, 0).wait_send()
+        near(step, 1).wait_send()
+        cross(step).wait_send()
+        for kind in (0, 1):
+            dense_swap(kind, step).wait_send()
+            dense_near(kind, step, 0).wait_send()
+            dense_near(kind, step, 1).wait_send()
+            dense_cross(kind, step).wait_send()
+
+    loop(0, 4, settle)
+
+    def settle_rings(step):
+        first_ring(step).wait_recv()
+        first_ring(step).wait_send()
+        grads_ring(step).wait_send()
+        far(step).wait_send()
+        dense_ring(0, step).wait_send()
+        dense_ring(1, step).wait_send()
+
+    loop(1, 4, settle_rings)
+
+
+def finish(outs, grads, first, dense_q, dense_o, collective):
+    rows, width = first.shape[1:]
+    plane_rows = width // PLANES
+    block = (plane_rows // 4, width // 2)
+    return pl.pallas_call(
+        finish_kernel,
+        out_shape=[
+            jax.ShapeDtypeStruct((rows, width), F32),
+            jax.ShapeDtypeStruct((4, PLANES) + grads.shape[1:], BF16),
+            jax.ShapeDtypeStruct(first.shape, BF16),
+            jax.ShapeDtypeStruct((PLANES, plane_rows, width), BF16),
+            jax.ShapeDtypeStruct((plane_rows, width), BF16),
+        ],
+        in_specs=[pl.BlockSpec(memory_space=pl.ANY)] * 5,
+        out_specs=[pl.BlockSpec(memory_space=pltpu.VMEM)] + [pl.BlockSpec(memory_space=pl.ANY)] * 4,
+        scratch_shapes=[
+            pltpu.VMEM((4, 4, rows, width), BF16),
             pltpu.VMEM((4, 2, rows, width), BF16),
             pltpu.VMEM((4, rows, width), BF16),
             pltpu.VMEM((3, rows, width), BF16),
-            pltpu.VMEM((4, rows, width), BF16),
-            pltpu.VMEM((3, rows, width), BF16),
-        ],
-    )(x)[0]
-
-
-def spread_grads_kernel(x, out, got, mine, total, send_sems, recv_sems):
-    w, z = place()
-    chip, core = w // 2, w % 2
-    greet(w, z)
-    net = Net(send_sems, recv_sems)
-    steps = (1, 2, 3, 0)
-    swap, load, ring, gathers = {}, {}, {}, []
-    for step in steps:
-        to, _ = other_plane(z, step)
-        swap[step] = net.send(x.at[to, 1 - core], got.at[step], (w ^ 1, z))
-        load[step] = net.keep(x.at[to, core], mine.at[step])
-    for step in steps:
-        to, _ = other_plane(z, step)
-        load[step].wait()
-        swap[step].wait_recv()
-        add_blocks(total.at[step], mine.at[step], got.at[step])
-        if step:
-            ring[step] = net.send(total.at[step], out.at[chip, z, core], (w, to))
-        else:
-            own = net.keep(total.at[step], out.at[chip, z, core])
-    own.wait()
-    for step in (0, 1, 2, 3):
-        _, source = other_plane(z, step)
-        if step:
-            ring[step].wait_recv()
-        gather = PlaneGather(
-            net, w, z, lambda i, source=source: out.at[i // 2, source, i % 2], step, True
-        )
-        gather.begin()
-        gathers.append(gather)
-    for gather in gathers:
-        gather.relay()
-    for gather in gathers:
-        gather.end()
-    for gather in gathers:
-        gather.settle()
-    net.finish()
-
-
-def spread_grads(x, collective):
-    rows, width = x.shape[2:]
-    block = (4, rows, width)
-    return comm_call(
-        spread_grads_kernel,
-        "spread_grads",
-        collective,
-        [jax.ShapeDtypeStruct((4, PLANES, 2, rows, width), BF16)],
-        [pl.ANY],
-        [pl.ANY],
-        64,
-        [pltpu.VMEM(block, BF16), pltpu.VMEM(block, BF16), pltpu.VMEM(block, BF16)],
-    )(x)[0]
-
-
-def sum_dense_kernel(
-    first, x, first_o, q_o, o_o, got, mine, part, got_one, got_two, sent, ready, got_far, send_sems, recv_sems
-):
-    w, z = place()
-    chip, core = w // 2, w % 2
-    greet(w, z)
-    net = Net(send_sems, recv_sems)
-    steps = (1, 2, 3, 0)
-    own = net.keep(first.at[z], first_o.at[z])
-    swap, load, flow, near, cross, far, gathers = {}, {}, [], {}, {}, {}, []
-    for step in steps:
-        to, _ = other_plane(z, step)
-        for kind in (0, 1):
-            swap[step, kind] = net.send(x.at[kind, 1 - core, to], got.at[kind, step], (w ^ 1, z))
-            load[step, kind] = net.keep(x.at[kind, core, to], mine.at[kind, step])
-    for step in (1, 2, 3):
-        to, _ = other_plane(z, step)
-        flow.append(net.send(first.at[to], first_o.at[z], (w, to)))
-    for step in steps:
-        for kind in (0, 1):
-            load[step, kind].wait()
-            swap[step, kind].wait_recv()
-            for block in range(4):
-                add_blocks(
-                    part.at[kind, step, block], mine.at[kind, step, block], got.at[kind, step, block]
-                )
-            first_flip = 1 + kind
-            peer = (w ^ (2 * first_flip), z)
-            near[step, kind] = (
-                net.send(part.at[kind, step, chip ^ 3], got_one.at[kind, step, 1], peer),
-                net.send(part.at[kind, step, chip ^ first_flip], got_one.at[kind, step, 0], peer),
-            )
-    for step in steps:
-        for kind in (0, 1):
-            second = 2 - kind
-            near[step, kind][0].wait_recv()
-            add_blocks(
-                sent.at[kind, step], part.at[kind, step, chip ^ second], got_one.at[kind, step, 1]
-            )
-            cross[step, kind] = net.send(
-                sent.at[kind, step], got_two.at[kind, step], (w ^ (2 * second), z)
-            )
-    for step in steps:
-        to, _ = other_plane(z, step)
-        for kind in (0, 1):
-            near[step, kind][1].wait_recv()
-            cross[step, kind].wait_recv()
-            add_blocks(
-                ready.at[kind, step],
-                part.at[kind, step, chip],
-                got_one.at[kind, step, 0],
-                got_two.at[kind, step],
-            )
-        if step:
-            far[step, 0] = net.send(ready.at[0, step], q_o.at[w, z], (w, to))
-            far[step, 1] = net.send(ready.at[1, step], got_far.at[step - 1], (w, to))
-        else:
-            kept = net.keep(ready.at[0, 0], q_o.at[w, z])
-    kept.wait()
-    for step in (0, 1, 2, 3):
-        _, source = other_plane(z, step)
-        if step:
-            far[step, 0].wait_recv()
-        gather = PlaneGather(net, w, z, lambda i, source=source: q_o.at[i, source], step, True)
-        gather.begin()
-        gathers.append(gather)
-    for step in (1, 2, 3):
-        far[step, 1].wait_recv()
-    add_blocks(mine.at[1, 0, 0], ready.at[1, 0], got_far.at[0], got_far.at[1], got_far.at[2])
-    last = net.keep(mine.at[1, 0, 0], o_o.at[w])
-    last.wait()
-    gather = PlaneGather(net, w, z, lambda i: o_o.at[i], 0, True)
-    gather.begin()
-    gathers.append(gather)
-    for gather in gathers:
-        gather.relay()
-    for gather in gathers:
-        gather.end()
-    for gather in gathers:
-        gather.settle()
-    own.wait()
-    for copy in flow:
-        copy.wait_recv()
-    net.finish()
-
-
-def sum_dense(first, x, collective):
-    rows, width = x.shape[4:]
-    block = (rows, width)
-    return comm_call(
-        sum_dense_kernel,
-        "sum_dense",
-        collective,
-        [
-            jax.ShapeDtypeStruct(first.shape, BF16),
-            jax.ShapeDtypeStruct((8, PLANES) + block, BF16),
-            jax.ShapeDtypeStruct((8,) + block, BF16),
-        ],
-        [pl.ANY, pl.ANY],
-        [pl.ANY, pl.ANY, pl.ANY],
-        140,
-        [
-            pltpu.VMEM((2, 4, 4) + block, BF16),
-            pltpu.VMEM((2, 4, 4) + block, BF16),
-            pltpu.VMEM((2, 4, 4) + block, BF16),
+            pltpu.VMEM((4,) + grads.shape[2:], BF16),
+            pltpu.VMEM((4,) + grads.shape[2:], BF16),
+            pltpu.VMEM((2, 4, plane_rows, width // 2), BF16),
+            pltpu.VMEM((2, 4, plane_rows, width // 2), BF16),
             pltpu.VMEM((2, 4, 2) + block, BF16),
             pltpu.VMEM((2, 4) + block, BF16),
-            pltpu.VMEM((2, 4) + block, BF16),
-            pltpu.VMEM((2, 4) + block, BF16),
             pltpu.VMEM((3,) + block, BF16),
+            pltpu.VMEM(block, BF16),
+            pltpu.SemaphoreType.DMA((5, 4)),
+            pltpu.SemaphoreType.DMA((38, 4)),
+            pltpu.SemaphoreType.DMA((38, 4)),
         ],
-    )(first, x)
+        compiler_params=pltpu.CompilerParams(
+            collective_id=collective, has_side_effects=True, vmem_limit_bytes=60 * 2**20
+        ),
+        name="finish",
+    )(outs, grads, first, dense_q, dense_o)
+
+
+def widen_kernel(table, up_o, down_o):
+    columns = table.shape[2]
+    split = up_o.shape[2]
+    for low in range(0, columns, 128):
+        part = jnp.swapaxes(table[:, :, low : low + 128].astype(F32), 0, 1)
+        if low < split:
+            up_o[:, :, low : low + 128] = part
+        else:
+            down_o[:, :, low - split : low - split + 128] = part
+
+
+def widen(table):
+    experts, rows, columns = table.shape
+    split = columns // 3 * 2
+    step = 16
+    return pl.pallas_call(
+        widen_kernel,
+        grid=(rows // step,),
+        out_shape=[
+            jax.ShapeDtypeStruct((rows, experts, split), F32),
+            jax.ShapeDtypeStruct((rows, experts, columns - split), F32),
+        ],
+        in_specs=[pl.BlockSpec((experts, step, columns), lambda i: (0, i, 0))],
+        out_specs=[
+            pl.BlockSpec((step, experts, split), lambda i: (i, 0, 0)),
+            pl.BlockSpec((step, experts, columns - split), lambda i: (i, 0, 0)),
+        ],
+        compiler_params=pltpu.CompilerParams(vmem_limit_bytes=48 * 2**20),
+        name="widen",
+    )(table)
 
 
 def windows(x):
@@ -962,11 +1506,16 @@
     seqlen = PLANES * rows
     size = WINDOW * HEAD_DIM
     scale = HEAD_DIM ** (-0.5)
-    w, z = place()
-    expert = (w // 2) * PLANES + z
+    z = lax.axis_index("narrow")
 
     misc = jnp.concatenate(
-        [w_router, gain_attn[:, None], gain_ffn[:, None], jnp.zeros((own, 128 - experts - 2), BF16)],
+        [
+            jnp.zeros((own, 1), BF16),
+            w_router,
+            gain_attn[:, None],
+            gain_ffn[:, None],
+            jnp.zeros((own, 128 - experts - 3), BF16),
+        ],
         axis=1,
     )
     wq_send = jnp.concatenate(
@@ -990,9 +1539,9 @@
     wq_all = wq_all.reshape(width, 3 * size + 128)
     misc_all = wq_all[:, 3 * size :]
     wq = wq_all[:, : 3 * size]
-    router = misc_all[:, :experts]
-    gain_one = misc_all[:, experts].astype(F32)
-    gain_two = misc_all[:, experts + 1].astype(F32)
+    router = misc_all[:, 1 : experts + 1]
+    gain_one = misc_all[:, experts + 1].astype(F32)
+    gain_two = misc_all[:, experts + 2].astype(F32)
     out_weight = wo_all.reshape(width, width)
 
     seq_in = tok_all.reshape(seqlen, width).astype(F32)
@@ -1023,55 +1572,17 @@
     normed_two = middle * inverse_two
     second_in = (normed_two * gain_two).astype(BF16)
 
-    x_all = gather_rows(second_in, 3).reshape(-1, width)
-    cot_all = cot_all.reshape(-1, width + 128)
-    cot_rows = cot_all[:, :width]
-    members = cot_all[:, width : width + experts + 1].astype(F32)
     weights = we_all.reshape(width, 3 * FF)
-    up, down = weights[:, : 2 * FF], weights[:, 2 * FF :]
-    probs_all = jax.nn.softmax(dot(x_all, router, ((1,), (0,))), axis=-1)
-    mine = (jnp.arange(experts + 1) == expert).astype(F32)[None, :]
-    shared_one = jnp.ones((x_all.shape[0], 1), F32)
-    member_own = jnp.sum(members * mine, axis=1, keepdims=True)
-    gate = jnp.sum(
-        jnp.concatenate([shared_one, probs_all], axis=1) * members * mine, axis=1, keepdims=True
-    )
-    gate_up = dot(x_all, up, ((1,), (0,)))
-    gate_part, up_part = gate_up[:, :FF], gate_up[:, FF:]
-    sigmoid = jax.nn.sigmoid(gate_part)
-    activated = (gate_part * sigmoid * up_part).astype(BF16)
-    expert_rows = dot(activated, down, ((1,), (1,)), BF16).astype(F32)
-    cot_f = cot_rows.astype(F32)
-    out_part = (gate * expert_rows).astype(BF16)
-    grad_prob = jnp.sum(expert_rows * cot_f, axis=1, keepdims=True) * member_own
-    prob_hi = grad_prob.astype(BF16)
-    prob_lo = (grad_prob - prob_hi.astype(F32)).astype(BF16)
-    lane = jnp.arange(128)[None, :]
-    prob_cols = jnp.where(lane == expert, prob_hi, 0) + jnp.where(lane == expert + 32, prob_lo, 0)
-    grad_rows = (gate * cot_f).astype(BF16)
-    grad_act = dot(grad_rows, down, ((1,), (0,)))
-    grad_gate_up = jnp.concatenate(
-        [
-            grad_act * up_part * sigmoid * (1.0 + gate_part * (1.0 - sigmoid)),
-            grad_act * gate_part * sigmoid,
-        ],
-        axis=1,
-    ).astype(BF16)
-    grad_in = dot(grad_gate_up, up, ((1,), (1,)), BF16)
-    grad_up = dot(x_all, grad_gate_up, ((0,), (0,)), BF16)
-    grad_down = dot(grad_rows, activated, ((0,), (0,)), BF16)
-    parts = jnp.concatenate([out_part, grad_in, prob_cols.astype(BF16)], axis=1)
-    sums = sum_rows(parts.reshape(4, PLANES, rows, 2 * width + 128), 4)
-
-    output = (middle + sums[:, :width]).astype(BF16)
-    hi = sums[:, 2 * width + 1 : 2 * width + 1 + experts]
-    lo = sums[:, 2 * width + 33 : 2 * width + 33 + experts]
+    grads, outs, sums = run_experts(second_in, cot_all, weights, misc_all, 3)
+
+    hi = sums[:, width + 1 : width + 1 + experts]
+    lo = sums[:, width + 33 : width + 33 + experts]
     grad_probs = hi + lo
     probs = jax.nn.softmax(dot(second_in, router, ((1,), (0,))), axis=-1)
     grad_logits = (
         probs * (grad_probs - jnp.sum(probs * grad_probs, axis=1, keepdims=True))
     ).astype(BF16)
-    grad_second = sums[:, width : 2 * width] + dot(grad_logits, router, ((1,), (1,)))
+    grad_second = sums[:, :width] + dot(grad_logits, router, ((1,), (1,)))
     grad_output = cotangent.astype(F32)
     grad_normed_two = grad_second * gain_two
     gain_two_part = jnp.sum(grad_second * normed_two, axis=0)
@@ -1115,13 +1626,16 @@
         ],
         axis=1,
     ).astype(BF16)
-    half = width // 2
-    dense = jnp.stack([jnp.concatenate([grad_qkv_part, misc_part], axis=1), grad_out_part])
-    dense = dense.reshape(2, PLANES, 4, width // 16, 2, half)
-    dense = jnp.transpose(dense, (0, 4, 1, 2, 3, 5))
-    first_all, q_all, o_all = sum_dense(
-        first_part.astype(BF16).reshape(PLANES, rows, width), dense, 6
-    )
+    dense_q = jnp.concatenate([grad_qkv_part, misc_part], axis=1)
+    sums, table, first_all, q_all, o_all = finish(
+        outs,
+        grads.reshape(PLANES, 2, width // PLANES // 2, 3 * FF),
+        first_part.astype(BF16).reshape(PLANES, rows, width),
+        dense_q,
+        grad_out_part,
+        6,
+    )
+    output = (middle + sums).astype(BF16)
     grad_first = jnp.sum(first_all.astype(F32), axis=0)
     inputs = tokens.astype(F32)
     inverse_one = rms_inverse(inputs)
@@ -1131,21 +1645,13 @@
         grad_normed_one
         - normed_one * jnp.mean(grad_normed_one * normed_one, axis=-1, keepdims=True)
     )
-    q_all = q_all.reshape(4, 2, PLANES, width // 16, half)
-    q_all = jnp.transpose(q_all, (2, 0, 3, 1, 4)).reshape(PLANES, 4 * (width // 16), width)
-    o_all = o_all.reshape(4, 2, width // 16, half)
-    out_sum = jnp.transpose(o_all, (0, 2, 1, 3)).reshape(4 * (width // 16), width).astype(F32)
+    out_sum = o_all.astype(F32)
     qkv_sum = jnp.concatenate(
         [from_windows(q_all[:, :, i * size : (i + 1) * size]) for i in range(3)], axis=1
     ).astype(F32)
     misc_sum = jnp.sum(q_all[:, :, 3 * size :].astype(F32), axis=0)
 
-    grads = jnp.concatenate([grad_up, grad_down], axis=1).reshape(
-        PLANES, 2, width // PLANES // 2, 3 * FF
-    )
-    table = spread_grads(grads, 7).reshape(experts + 1, width // PLANES, 3 * FF)
-    up_sum = jnp.transpose(table[:, :, : 2 * FF], (1, 0, 2)).astype(F32)
-    down_sum = jnp.transpose(table[:, :, 2 * FF :], (1, 0, 2)).astype(F32)
+    up_sum, down_sum = widen(table.reshape(experts + 1, width // PLANES, 3 * FF))
     return (
         output,
         grad_tokens.astype(BF16),

time: 1010 us -> 719 us (0.71)
  local copies, waits for them, and re-layouts: 128 us -> 32.7 us
  matrix products: 125 us -> 41.1 us
  other arithmetic: 93.2 us -> 24.7 us
  Pallas kernels: 658 us -> 605 us
    dot_general x16 -> x9, matrix products: 106 us -> 19.7 us  [dot(): lax.dot_general(a, b, ((dims[0], dims[1]), ((), ())), preferred_element_t...]
    pallas_call x4 -> x3, Pallas kernels: 423 us -> 368 us  [the longest x1 217 us: finish(): pl.pallas_call(finish_kernel, out_shape=[jax.ShapeDtypeStruct((rows, widt...]
    convert_element_type x7 -> x3, other arithmetic: 41.5 us -> 6.1 us  [the longest x1 2.42 us: expert_local(): out_sum = o_all.astype(F32)]
    slice x5 -> x1, local copies, waits for them, and re-layouts: 31.5 us -> 1.72 us  [expert_local(): misc_all = wq_all[:, 3 * size:]]
    another operation x4 -> x1, local copies, waits for them, and re-layouts: 23.9 us -> 1.7 us  [expert_local(): jnp.stack([jnp.concatenate([grad_qkv_part, misc_part], axis=1), grad_out_...]
    concatenate x3 -> x0, other arithmetic: 21.8 us -> none  [the longest x1 16.1 us: expert_local(): parts = jnp.concatenate([out_part, grad_in, prob_cols.astype(BF16)], axis=1)]
    concatenate x3 -> x2, local copies, waits for them, and re-layouts: 27.8 us -> 6.75 us  [the longest x1 6.65 us: expert_local(): dense_q = jnp.concatenate([grad_qkv_part, misc_part], axis=1)]
    unnamed x112 -> x91, local copies, waits for them, and re-layouts: 17.2 us -> 5.92 us
where the time goes in v2:
time: 719 us; the launch traced here: 706 us
  Pallas kernels  605 us (84%)
  matrix products  41.1 us (6%)
  local copies, waits for them, and re-layouts  32.7 us (5%)
  other arithmetic  24.7 us (3%)
    pallas_call x1, Pallas kernels, finish(): pl.pallas_call(finish_kernel, out_shape=[jax.ShapeDtypeStruct((rows, widt...  217 us
    pallas_call x1, Pallas kernels, spread_inputs(): comm_call(spread_inputs_kernel, 'spread_inputs', 1, [jax.ShapeDtypeStruct...  208 us
    pallas_call x1, Pallas kernels, run_experts(): pl.pallas_call(experts_kernel, out_shape=[jax.ShapeDtypeStruct((width, 3...  119 us
    pallas_call x1, Pallas kernels, widen(): pl.pallas_call(widen_kernel, grid=(rows // step,), out_shape=[jax.ShapeDt...  31.5 us
    pallas_call x2, Pallas kernels, swap_planes(): comm_call(swap_planes_kernel, 'swap_planes', collective, [jax.ShapeDtypeS...  30.1 us
    dot_general x9, matrix products, dot(): lax.dot_general(a, b, ((dims[0], dims[1]), ((), ())), preferred_element_t...  19.7 us

profile of v2, /device:TPU:29, one launch (start us, length us, event | category | flops | bytes accessed | tf_op | source)
XLA Modules:
  0.0 705.6 jit_solution(13307226689590409662)
XLA Ops:
  0.7 1.2 dynamic-slice_bitcast_fusion
  1.9 0.7 convert_element_type.109
  2.6 1.1 fusion.26
  3.7 0.6 add_rsqrt_fusion
  4.3 0.7 fusion.50
  5.0 0.6 broadcast_in_dim.42.ids
  5.6 0.8 copy.154
  6.3 0.8 copy.155
  7.1 0.8 copy.153
  8.1 0.5 fusion.47
  8.7 2.0 concatenate.49.cot
  10.8 0.8 pad_maximum_fusion.4.wq
  11.6 1.5 copy.157
  13.1 0.7 copy.156
  14.0 2.0 copy.191
  16.0 207.5 %spread_inputs.1 = (bf16[4,128,1280]{2,1,0:T(8,128)(2,1)}, bf16[4,16,128]{2,1,0:T(8,128)(2,1)}, bf16[8,4,40,1280]{3,2,1,0:T(8,128)(2,1)}, bf16[8,4,40,1280]{3,2,...) custom-call(bf16[128,1280]{1,0:T(8,128)(2,1)} %tok.1, ...), custom_call_target="tpu_custom_call" | custom-call | tf_op jit(solution)/shard_map/spread_inputs/pallas_call | solution.py:617
  223.5 0.8 slice_reduce_fusion.2
  224.4 1.8 multiply_reduce_fusion.1
  226.2 1.7 convert_reduce_fusion.1
  227.9 0.9 fusion.10
  228.8 1.7 slice.268.misc_in
  230.9 1.9 fusion.6
  233.3 0.9 copy.160
  234.6 0.5 fusion.15
  235.1 2.3 fusion.72
  237.4 3.1 fusion.67
  240.6 5.6 fusion.68
  246.3 1.0 copy.166.x
  247.3 12.2 %swap_planes.2 = bf16[4,128,384]{2,1,0:T(8,128)(2,1)} custom-call(bf16[4,128,384]{2,1,0:T(8,128)(2,1)} %copy.166.x), custom_call_target="tpu_custom_call" | custom-call | tf_op jit(solution)/shard_map/swap_planes/pallas_call | solution.py:645
  259.5 0.9 slice_bitcast_fusion.7
  260.4 1.0 slice_bitcast_fusion.5
  261.4 2.7 multiply_reduce_fusion.5
  264.2 0.9 multiply_convert_fusion.3.x_in
  265.0 119.0 %experts.1 = (bf16[1280,2688]{1,0:T(8,128)(2,1)}, bf16[4,4,128,1280]{3,2,1,0:T(8,128)(2,1)}, f32[128,1408]{1,0:T(8,128)}) custom-call(bf16[128,1280]{1,0:T(8,128)(2,1)} %multiply_convert_fusion.3.x_in, bf16[4,4,128,1408]{3,2,1,0:T(8,128)(2,1)} %get-tuple-element.29.cot_in, bf16[1280,2688]{1,0:T(8,128)(2,1)} %bitcast.135, bf16[1280,128]{1,0:T(8,128)(2,1)} %slice.268.misc_in), custom_call_target="tpu_custom_call" | custom-call | tf_op jit(solution)/shard_map/experts/pallas_call | solution.py:1021
  384.1 1.5 fusion.71
  385.9 1.1 multiply_reduce_fusion.6
  387.0 1.2 multiply_convert_fusion.6
  388.2 0.8 convolution_convert_fusion.3
  389.0 2.3 multiply_reduce_fusion.3
  391.6 1.2 convolution_convert_fusion.2
  392.8 0.8 pad_maximum_fusion.5.x
  393.7 17.9 %swap_planes.3 = bf16[4,128,384]{2,1,0:T(8,128)(2,1)} custom-call(bf16[4,128,384]{2,1,0:T(8,128)(2,1)} %pad_maximum_fusion.5.x), custom_call_target="tpu_custom_call" | custom-call | tf_op jit(solution)/shard_map/swap_planes/pallas_call | solution.py:645
  411.5 1.2 copy.168
  413.0 5.5 convolution_convert_fusion.4
  418.8 2.8 multiply_convert_fusion
  421.6 1.7 copy.176
  423.3 1.0 broadcast_in_dim.98
  424.2 1.6 convolution_bitcast_fusion
  425.9 0.5 broadcast_multiply_fusion.1
  427.0 0.8 copy-done.3
  427.8 1.0 copy-done.21
  428.8 3.1 multiply_reduce_fusion
  432.2 3.5 convolution_convert_fusion.1
  435.8 6.7 concatenate.58.dense_q
  442.5 2.8 convolution_convert_fusion.dense_o
  445.2 216.9 %finish.1 = (f32[128,1280]{1,0:T(8,128)}, bf16[4,4,2,160,2688]{4,3,2,1,0:T(8,128)(2,1)}, bf16[4,128,1280]{2,1,0:T(8,128)(2,1)}, bf16[4,320,1280]{2,1,0:T(8,128)(2,1)}, bf16[320,1280]{1,0:T(8,128)(2,1)}) custom-call(bf16[4,4,128,1280]{3,2,1,0:T(8,128)(2,1)} %get-tuple-element.31.outs_in, bf16[4,2,160,2688]{3,2,1,0:T(8,128)(2,1)} %bitcast.134, ...), custom_call_target="tpu_custom_call" | custom-call | tf_op jit(solution)/shard_map/finish/pallas_call | solution.py:1418
  662.2 2.0 add_convert_fusion
  664.1 1.0 convert_reduce_fusion.3
  665.2 0.9 slice_reduce_fusion
  666.0 0.7 copy.179
  667.2 1.0 fusion.25
  668.2 2.4 convert_element_type.139
  671.0 2.6 convert_element_type.138
  673.6 31.5 %widen.1 = (f32[320,16,1792]{2,1,0:T(8,128)}, f32[320,16,896]{2,1,0:T(8,128)}) custom-call(bf16[16,320,2688]{2,1,0:T(8,128)(2,1)} %bitcast.127), custom_call_target="tpu_custom_call" | custom-call | tf_op jit(solution)/shard_map/widen/pallas_call | solution.py:1468
  (123 shorter events, 4.7 us)
Async XLA Ops:
  0.6 10.1 %copy-start.23 = (bf16[40,3840]{1,0:T(8,128)(2,1)S(1)}, bf16[40,3840]{1,0:T(8,128)(2,1)}, u32[]{:S(2)}) copy-start(bf16[40,3840]{1,0:T(8,128)(2,1)} %param.17) | copy-start | bytes 921604
  8.7 4.4 copy-start.12
  10.7 223.9 %copy-start.10 = (f32[512,128]{0,1:T(8,128)}, f32[512,128]{0,1:T(8,128)S(1)}, u32[]{:S(2)}) copy-start(f32[512,128]{0,1:T(8,128)S(1)} %get-tuple-element.135) | copy-start | bytes 786436
  223.5 7.0 copy-start.2
  224.4 6.6 copy-start.20
  226.2 6.6 copy-start.33
  230.9 1.9 copy-start.16
  235.1 5.5 copy-start.6
  235.1 11.1 %copy-start.5 = (bf16[512,3,128]{0,2,1:T(8,128)(2,1)}, bf16[512,3,128]{0,2,1:T(8,128)(2,1)S(1)}, u32[]{:S(2)}) copy-start(bf16[512,3,128]{0,2,1:T(8,128)(2,1)S(1)} %get-tuple-element.96) | copy-start | bytes 1179652
  235.1 2.3 copy-start.30
  237.4 3.2 copy-start.13
  240.6 172.4 %copy-start.31 = (f32[3,512]{1,0:T(4,128)}, f32[3,512]{1,0:T(4,128)S(1)}, u32[]{:S(2)}) copy-start(f32[3,512]{1,0:T(4,128)S(1)} %broadcast_divide_fusion) | copy-start | bytes 18436
  246.2 15.2 %copy-start = (bf16[128,1280]{1,0:T(8,128)(2,1)S(1)}, bf16[128,1280]{1,0:T(8,128)(2,1)}, u32[]{:S(2)}) copy-start(bf16[128,1280]{1,0:T(8,128)(2,1)} %tok.1) | copy-start | bytes 983044
  260.4 3.7 copy-start.28
  261.4 2.8 copy-start.24
  261.4 2.8 copy-start.26
  265.0 119.1 %copy-start.1 = (bf16[128,1280]{1,0:T(8,128)(2,1)S(1)}, bf16[128,1280]{1,0:T(8,128)(2,1)}, u32[]{:S(2)}) copy-start(bf16[128,1280]{1,0:T(8,128)(2,1)} %multiply_convert_fusion.3.x_in) | copy-start | bytes 983044
  384.1 7.3 %copy-start.19 = (bf16[128,1280]{1,0:T(8,128)(2,1)S(1)}, bf16[128,1280]{1,0:T(8,128)(2,1)}, u32[]{:S(2)}) copy-start(bf16[128,1280]{1,0:T(8,128)(2,1)} %param.15) | copy-start | bytes 983044
  387.0 4.6 copy-start.8
  392.8 20.2 %copy-start.36 = (bf16[3]{0:T(256)(128)(2,1)S(1)}, bf16[3]{0:T(256)(128)(2,1)}, u32[]{:S(2)}) copy-start(bf16[3]{0:T(256)(128)(2,1)} %dynamic-slice_bitcast_fusion) | copy-start | bytes 22
  413.0 5.8 copy-start.4
  413.0 5.6 copy-start.22
  418.7 4.5 copy-start.32
  423.3 2.6 copy-start.7
  423.3 2.6 copy-start.11
  426.4 1.3 copy-start.3
  426.4 2.3 copy-start.21
  426.5 2.3 copy-start.34
  426.5 2.4 copy-start.37
  428.8 3.3 copy-start.17
  432.1 3.6 copy-start.14
  432.1 3.6 copy-start.15
  435.7 6.7 copy-start.25
  435.8 6.7 copy-start.27
  435.8 6.7 copy-start.29
  662.1 4.6 copy-start.18
  662.2 4.8 copy-start.35
  667.0 3.7 copy-start.9

commit v3 on v2

--- a/solution.py
+++ b/solution.py
@@ -455,38 +455,6 @@
     pl.semaphore_wait(barrier, len(peers))
 
 
-class PlaneGather:
-    def __init__(self, net, w, z, slot, number, cores):
-        self.net, self.w, self.z, self.slot, self.cores = net, w, z, slot, cores
-        self.first, self.second = (2, 4) if number % 2 == 0 else (4, 2)
-
-    def push(self, slot_of, flip):
-        ref = self.slot(slot_of)
-        return self.net.send(ref, ref, (self.w ^ flip, self.z))
-
-    def begin(self):
-        self.direct = {flip: self.push(self.w, flip) for flip in (2, 4)}
-        self.core = [self.push(self.w, 1)] if self.cores else []
-
-    def relay(self):
-        self.direct[self.first].wait_recv()
-        self.across = self.push(self.w ^ self.first, self.second)
-        if self.cores:
-            self.core.append(self.push(self.w ^ self.first, 1))
-        self.direct[self.second].wait_recv()
-        if self.cores:
-            self.core.append(self.push(self.w ^ self.second, 1))
-
-    def end(self):
-        self.across.wait_recv()
-        if self.cores:
-            self.core.append(self.push(self.w ^ 6, 1))
-
-    def settle(self):
-        for copy in self.core:
-            copy.wait_recv()
-
-
 def comm_call(kernel, name, collective, out_shape, in_spaces, out_spaces, sems, scratch=(), moved=0):
     return pl.pallas_call(
         kernel,
@@ -505,125 +473,20 @@
     )
 
 
-def spread_inputs_kernel(
-    tok, ids, wq, wo, we, cot, tok_o, ids_o, wq_o, wo_o, we_o, cot_o, hop, send_sems, recv_sems
-):
-    w, z = place()
-    chip = w // 2
-    greet(w, z)
-    net = Net(send_sems, recv_sems)
-    own = [
-        net.keep(tok, tok_o.at[z]),
-        net.keep(ids, ids_o.at[z]),
-        net.keep(wq.at[z], wq_o.at[w, z]),
-        net.keep(wo, wo_o.at[w, z]),
-        net.keep(we.at[z, chip], we_o.at[w, z]),
-        net.keep(cot, cot_o.at[chip, z]),
-    ]
-    ring, gathers = {}, {}
-    for step in (1, 2, 3):
-        to, _ = other_plane(z, step)
-        ring["tok", step] = net.send(tok, tok_o.at[z], (w, to))
-        ring["ids", step] = net.send(ids, ids_o.at[z], (w, to))
-        ring["wq", step] = net.send(wq.at[to], wq_o.at[w, z], (w, to))
-    for step in (1, 2, 3):
-        to, _ = other_plane(z, step)
-        for flip in (1, 2, 3):
-            ring["we", step, flip] = net.send(
-                we.at[to, chip ^ flip], hop.at[step - 1, flip - 1], (w, to)
-            )
-        ring["we", step, 0] = net.send(we.at[to, chip], we_o.at[w, z], (w, to))
-        ring["cot", step] = net.send(cot, cot_o.at[chip, z], (w, to))
-        ring["wo", step] = net.send(wo, wo_o.at[w, z], (w, to))
-    for copy in own:
-        copy.wait()
-    weights = {}
-    for flip in (1, 2, 3):
-        weights[0, flip] = net.send(
-            we.at[z, chip ^ flip], we_o.at[w, z], (w ^ (2 * flip), z)
-        )
-    core = [net.send(we_o.at[w, z], we_o.at[w, z], (w ^ 1, z))]
-
-    def start_gather(kind, step):
-        _, source = other_plane(z, step)
-        slot = {
-            "wq": lambda i: wq_o.at[i, source],
-            "wo": lambda i: wo_o.at[i, source],
-            "cot": lambda i: cot_o.at[i // 2, source],
-        }[kind]
-        gathers[kind, step] = PlaneGather(net, w, z, slot, step, kind != "cot")
-        gathers[kind, step].begin()
-
-    start_gather("wq", 0)
-    start_gather("wo", 0)
-    start_gather("cot", 0)
-    for step in (1, 2, 3):
-        ring["wq", step].wait_recv()
-        start_gather("wq", step)
-    for step in (0, 1, 2, 3):
-        gathers["wq", step].relay()
-    gathers["wo", 0].relay()
-    gathers["cot", 0].relay()
-    for step in (0, 1, 2, 3):
-        gathers["wq", step].end()
-    gathers["wo", 0].end()
-    gathers["cot", 0].end()
-    for step in (1, 2, 3):
-        _, source = other_plane(z, step)
-        for flip in (1, 2, 3):
-            ring["we", step, flip].wait_recv()
-            weights[step, flip] = net.send(
-                hop.at[step - 1, flip - 1], we_o.at[w, source], (w ^ (2 * flip), z)
-            )
-        ring["we", step, 0].wait_recv()
-        core.append(net.send(we_o.at[w, source], we_o.at[w, source], (w ^ 1, z)))
-        for kind in ("cot", "wo"):
-            ring[kind, step].wait_recv()
-            start_gather(kind, step)
-        ring["tok", step].wait_recv()
-        ring["ids", step].wait_recv()
-    for step in (0, 1, 2, 3):
-        _, source = other_plane(z, step)
-        for flip in (1, 2, 3):
-            weights[step, flip].wait_recv()
-            peer = w ^ (2 * flip)
-            core.append(net.send(we_o.at[peer, source], we_o.at[peer, source], (w ^ 1, z)))
-        if step:
-            for kind in ("cot", "wo"):
-                gathers[kind, step].relay()
-    for step in (1, 2, 3):
-        for kind in ("cot", "wo"):
-            gathers[kind, step].end()
-    for gather in gathers.values():
-        gather.settle()
-    for copy in core:
-        copy.wait_recv()
-    net.finish()
-
-
-def spread_inputs(tok, ids, wq, wo, we, cot):
-    rows, width = tok.shape
-    own = wo.shape[0]
-    hidden3 = we.shape[-1]
-    shapes = [
-        (PLANES, rows, width),
-        (PLANES,) + ids.shape,
-        (8, PLANES) + wq.shape[1:],
-        (8, PLANES) + wo.shape,
-        (8, PLANES, own, hidden3),
-        (4, PLANES) + cot.shape,
-        (3, 3, own, hidden3),
-    ]
-    out = comm_call(
-        spread_inputs_kernel,
-        "spread_inputs",
-        1,
-        [jax.ShapeDtypeStruct(shape, BF16) for shape in shapes],
-        [pl.ANY] * 6,
-        [pl.ANY] * 7,
-        160,
-    )(tok, ids, wq, wo, we, cot)
-    return out[:6]
+def mul(a, b, over_a, over_b):
+    return lax.dot_general(a, b, (((over_a,), (over_b,)), ((), ())), preferred_element_type=F32)
+
+
+def at(start, size):
+    return pl.ds(pl.multiple_of(start, 128), size)
+
+
+def loop(first, last, body):
+    def step(i, carry):
+        body(i)
+        return carry
+
+    lax.fori_loop(first, last, step, 0)
 
 
 def swap_planes_kernel(x, out, send_sems, recv_sems):
@@ -653,6 +516,453 @@
     )(x)[0]
 
 
+class Links:
+    def __init__(self, send_sems, recv_sems):
+        self.w, self.z = place()
+        self.send_sems, self.recv_sems = send_sems, recv_sems
+
+    def copy(self, kind, step, src, dst, device):
+        return pltpu.make_async_remote_copy(
+            src_ref=src,
+            dst_ref=dst,
+            send_sem=self.send_sems.at[kind, step],
+            recv_sem=self.recv_sems.at[kind, step],
+            device_id=device,
+            device_id_type=MESH_IDS,
+        )
+
+    def plane(self, step, sign):
+        return lax.rem(self.z + PLANES + sign * step, PLANES)
+
+
+def step_at(z, turn):
+    step = 0
+    for plane, steps in enumerate(((3, 2, 1, 0), (1, 3, 2, 0), (3, 1, 2, 0), (1, 2, 3, 0))):
+        for number, value in enumerate(steps):
+            step = jnp.where((z == plane) & (turn == number), value, step)
+    return step
+
+
+class Chain:
+    def __init__(self, links, base, own, slot):
+        self.links, self.base, self.own, self.slot = links, base, own, slot
+
+    def goes(self, step, up):
+        z = self.links.z
+        if up:
+            return (z >= step) & (z < PLANES - 1)
+        return ((z < step) | (step == 0)) & (z > 0)
+
+    def ring(self, step, up, own=False):
+        links = self.links
+        to = lax.rem(step + 1, 4) if up else lax.rem(step + 3, 4)
+        ref = self.slot(links.plane(step, -1))
+        return pltpu.make_async_remote_copy(
+            src_ref=self.own if own else ref,
+            dst_ref=ref,
+            send_sem=links.send_sems.at[self.base if up else self.base + 1, step],
+            recv_sem=links.recv_sems.at[self.base, to],
+            device_id=(links.w, links.z + 1 if up else links.z - 1),
+            device_id_type=MESH_IDS,
+        )
+
+    def hand_on(self, step, own=False):
+        for up in (True, False):
+
+            @pl.when(self.goes(step, up))
+            def _():
+                self.ring(step, up, own).start()
+
+    def begin(self):
+        self.hand_on(0, True)
+
+    def arrive(self, turn):
+        step = step_at(self.links.z, turn)
+        ref = self.slot(self.links.plane(step, -1))
+        self.links.copy(self.base, step, ref, ref, (self.links.w, self.links.z)).wait_recv()
+        self.hand_on(step)
+
+    def settle(self):
+        def body(step):
+            for up in (True, False):
+
+                @pl.when(self.goes(step, up))
+                def _():
+                    self.ring(step, up).wait_send()
+
+        loop(0, 4, body)
+
+
+class Gather:
+    def __init__(self, links, base, step, turn, slot, cores=True):
+        self.links, self.base, self.step, self.slot, self.cores = links, base, step, slot, cores
+        self.first = 1 + lax.rem(turn, 2)
+        self.second = 3 - self.first
+
+    def copy(self, kind, owner, flip):
+        ref = self.slot(owner)
+        return self.links.copy(
+            self.base + kind, self.step, ref, ref, (self.links.w ^ flip, self.links.z)
+        )
+
+    def begin(self):
+        w = self.links.w
+        self.copy(0, w, 2).start()
+        self.copy(1, w, 4).start()
+        if self.cores:
+            self.copy(4, w, 1).start()
+
+    def relay(self):
+        w = self.links.w
+        self.copy(0, w, 2).wait_recv()
+        self.copy(1, w, 4).wait_recv()
+        self.across().start()
+        if self.cores:
+            self.copy(3, w ^ 2, 1).start()
+            self.copy(5, w ^ 4, 1).start()
+
+    def across(self):
+        return self.copy(2, self.links.w ^ (2 * self.first), 2 * self.second)
+
+    def end(self):
+        self.across().wait_recv()
+        if self.cores:
+            self.copy(6, self.links.w ^ 6, 1).start()
+
+    def settle(self):
+        w = self.links.w
+        self.copy(0, w, 2).wait_send()
+        self.copy(1, w, 4).wait_send()
+        self.across().wait_send()
+        if self.cores:
+            for kind, owner in ((4, w), (3, w ^ 2), (5, w ^ 4), (6, w ^ 6)):
+                copy = self.copy(kind, owner, 1)
+                copy.wait_send()
+                copy.wait_recv()
+
+
+def softmax_rows(scores, mask):
+    masked = scores + mask
+    powers = jnp.exp(masked - jnp.max(masked, axis=1, keepdims=True))
+    return powers * (1.0 / jnp.sum(powers, axis=1, keepdims=True))
+
+
+def start_kernel(
+    tok_in, ids_in, wq_in, wo_in, we_in, cot_in, cos_in, sin_in,
+    we_o, cot_o, wq_o, wo_o, first_o, qkv_o, exact_o, mixed_o, mixed_rows_o, middle_o, second_o, hop,
+    tok, ids, wq_blocks, wo_blocks, staged, mask, mixed_got, mixed_send,
+    load_sems, send_sems, recv_sems,
+):
+    links = Links(send_sems, recv_sems)
+    w, z = links.w, links.z
+    chip = w // 2
+    rows, width = tok_in.shape
+    seqlen = PLANES * rows
+    size = WINDOW * HEAD_DIM
+    own = wo_in.shape[0]
+    keeps = [
+        pltpu.make_async_copy(src, dst, load_sems.at[i])
+        for i, (src, dst) in enumerate(
+            (
+                (tok_in, tok.at[z]),
+                (ids_in, ids.at[z]),
+                (wq_in.at[z], wq_blocks.at[w, z]),
+                (wo_in, wo_blocks.at[w, z]),
+                (cot_in, cot_o.at[chip, z]),
+            )
+        )
+    ]
+    for keep in keeps:
+        keep.start()
+    greet(w, z)
+
+    tok_chain = Chain(links, 0, tok_in, lambda p: tok.at[p])
+    ids_chain = Chain(links, 2, ids_in, lambda p: ids.at[p])
+    wo_chain = Chain(links, 4, wo_in, lambda p: wo_blocks.at[w, p])
+    cot_chain = Chain(links, 6, cot_in, lambda p: cot_o.at[chip, p])
+
+    def wq_ring(step):
+        to = links.plane(step, 1)
+        return links.copy(8, step, wq_in.at[to], wq_blocks.at[w, z], (w, to))
+
+    def wq_gather(step):
+        source = links.plane(step, -1)
+        return Gather(links, 9, step, step, lambda i: wq_blocks.at[i, source])
+
+    def wo_gather(turn):
+        step = step_at(z, turn)
+        source = links.plane(step, -1)
+        return Gather(links, 16, step, turn, lambda i: wo_blocks.at[i, source])
+
+    def cot_gather(turn):
+        step = step_at(z, turn)
+        source = links.plane(step, -1)
+        return Gather(links, 23, step, turn, lambda i: cot_o.at[i // 2, source], False)
+
+    def weights_ring(step, flip):
+        to = links.plane(step, 1)
+        return links.copy(
+            26 + flip, step, we_in.at[to, chip ^ flip], hop.at[step - 1, chip ^ flip], (w, to)
+        )
+
+    def weights_block(step, flip):
+        return hop.at[step - 1, chip ^ flip] if step else we_in.at[z, chip ^ flip]
+
+    def weights_plane(step, flip):
+        to = we_o.at[w, links.plane(step, -1)]
+        return links.copy(29 + flip, step, weights_block(step, flip), to, (w ^ (2 * flip), z))
+
+    def weights_keep(step):
+        return pltpu.make_async_copy(
+            weights_block(step, 0), we_o.at[w, links.plane(step, -1)], load_sems.at[6 + step]
+        )
+
+    def weights_core(step, flip):
+        block = we_o.at[w ^ (2 * flip), links.plane(step, -1)]
+        return links.copy(
+            34 + flip, step, block if flip else weights_block(step, 0), block, (w ^ 1, z)
+        )
+
+    def weights_send(step):
+        for flip in (3, 1, 2, 0):
+            weights_ring(step, flip).start()
+
+    def weights_next(step):
+        for flip in (3, 1, 2):
+            if step:
+                weights_ring(step, flip).wait_recv()
+            weights_plane(step, flip).start()
+        if step:
+            weights_ring(step, 0).wait_recv()
+        weights_core(step, 0).start()
+        weights_keep(step).start()
+
+    def weights_end(step):
+        for flip in (1, 2, 3):
+            weights_plane(step, flip).wait_recv()
+            weights_core(step, flip).start()
+
+    def mixed_ring(step):
+        to = links.plane(step, 1)
+        return links.copy(38, step, mixed_send.at[to], mixed_got.at[z], (w, to))
+
+    tok_chain.begin()
+    ids_chain.begin()
+    for step in (1, 2, 3):
+        wq_ring(step).start()
+    for keep in keeps:
+        keep.wait()
+    wq_gather(0).begin()
+    tok_chain.arrive(0)
+    ids_chain.arrive(0)
+    for step in (1, 2, 3):
+        wq_ring(step).wait_recv()
+        wq_gather(step).begin()
+    wo_chain.begin()
+    tok_chain.arrive(1)
+    ids_chain.arrive(1)
+    cot_chain.begin()
+    end_plane = (z == 0) | (z == PLANES - 1)
+
+    @pl.when(jnp.logical_not(end_plane))
+    def _():
+        tok_chain.arrive(2)
+        ids_chain.arrive(2)
+
+    loop(0, 4, lambda step: wq_gather(step).relay())
+
+    @pl.when(end_plane)
+    def _():
+        tok_chain.arrive(2)
+        ids_chain.arrive(2)
+        weights_send(1)
+        weights_send(3)
+
+    wo_chain.arrive(0)
+    wo_gather(0).begin()
+    wo_gather(3).begin()
+    cot_gather(3).begin()
+    weights_next(0)
+    for i in range(PLANES):
+        for j in range(PLANES):
+            here = (slice(i * rows, (i + 1) * rows), slice(j * rows, (j + 1) * rows))
+            if j > i:
+                mask[here] = jnp.full((rows, rows), -1e30, F32)
+            else:
+                same = ids[i, rows:, :].astype(F32) == ids[j, :rows, :].astype(F32)
+                if i == j:
+                    same = same & (
+                        lax.broadcasted_iota(jnp.int32, (rows, rows), 1)
+                        <= lax.broadcasted_iota(jnp.int32, (rows, rows), 0)
+                    )
+                mask[here] = jnp.where(same, 0.0, -1e30)
+    loop(0, 4, lambda step: wq_gather(step).end())
+    loop(0, 4, lambda step: wq_gather(step).settle())
+
+    def assemble(blocks, to):
+        def body(i):
+            for p in range(PLANES):
+                staged[p * own : (p + 1) * own, :] = blocks[i, p].astype(F32)
+            span = PLANES * own
+            to[pl.ds(pl.multiple_of(i * span, 16), span), :] = staged[...].astype(BF16)
+
+        loop(0, blocks.shape[0], body)
+
+    cot_chain.arrive(0)
+    cot_gather(0).begin()
+    assemble(wq_blocks, wq_o)
+    gains = jnp.transpose(wq_o[:, size * 3 :].astype(F32))
+    gain_one = gains[16:17, :]
+    gain_two = gains[17:18, :]
+
+    def normalise(p):
+        block = tok[p].astype(F32)
+        inverse = lax.rsqrt(jnp.mean(block * block, axis=1, keepdims=True) + epsilon)
+        first_o[p] = (block * inverse * gain_one).astype(BF16)
+
+    loop(0, PLANES, normalise)
+    wo_chain.arrive(1)
+    wo_gather(1).begin()
+    cot_chain.arrive(1)
+    cot_gather(1).begin()
+
+    def project(p):
+        span = pl.ds(pl.multiple_of(p * rows, 128), rows)
+        cosine, sine = cos_in[span, :], sin_in[span, :]
+        for kind in range(3):
+            part = mul(first_o[p], wq_o[:, kind * size : (kind + 1) * size], 1, 0)
+            for head in range(WINDOW):
+                here = part[:, head * HEAD_DIM : (head + 1) * HEAD_DIM]
+                if kind < 2:
+                    here = here * cosine + pltpu.roll(here, HEAD_DIM // 2, 1) * sine
+                if kind == 0:
+                    here = here * (HEAD_DIM ** (-0.5))
+                qkv_o[kind, head, span, :] = here.astype(BF16)
+
+    loop(0, PLANES, project)
+    wo_chain.arrive(2)
+    wo_gather(2).begin()
+    cot_chain.arrive(2)
+    cot_gather(2).begin()
+
+    @pl.when(jnp.logical_not(end_plane))
+    def _():
+        weights_send(1)
+        weights_send(3)
+
+    def attend(head):
+        exact = softmax_rows(mul(qkv_o[0, head], qkv_o[1, head], 1, 1), mask[...])
+        exact_o[head] = exact
+        mixed_o[head] = mul(exact.astype(BF16), qkv_o[2, head], 1, 0)
+
+    loop(0, WINDOW, attend)
+    for p in range(PLANES):
+        for head in range(WINDOW):
+            mixed_send[p, :, head * HEAD_DIM : (head + 1) * HEAD_DIM] = mixed_o[
+                head, p * rows : (p + 1) * rows, :
+            ].astype(BF16)
+    for step in (1, 2, 3):
+        mixed_ring(step).start()
+    mixed_got[z] = mixed_send[z]
+    weights_send(2)
+    loop(0, 4, lambda turn: wo_gather(turn).relay())
+    loop(0, 4, lambda turn: wo_gather(turn).end())
+    weights_next(1)
+    loop(0, 4, lambda turn: cot_gather(turn).relay())
+    weights_end(0)
+    weights_next(3)
+    loop(0, 4, lambda turn: wo_gather(turn).settle())
+    assemble(wo_blocks, wo_o)
+    for step in (1, 2, 3):
+        mixed_ring(step).wait_recv()
+    column = 0
+    for p, (a, b) in enumerate(KEEP):
+        span = (b - a) * HEAD_DIM
+        mixed_rows_o[:, column : column + span] = mixed_got[p, :, a * HEAD_DIM : b * HEAD_DIM]
+        column += span
+
+    def out_project(i):
+        here = at(i * 256, 256)
+        middle_o[:, here] = tok_in_f32(tok, z, here) + mul(mixed_rows_o[...], wo_o[:, here], 1, 0)
+
+    loop(0, width // 256, out_project)
+    middle = middle_o[...]
+    inverse = lax.rsqrt(jnp.mean(middle * middle, axis=1, keepdims=True) + epsilon)
+    second_o[...] = (middle * inverse * gain_two).astype(BF16)
+    weights_end(1)
+    loop(0, 4, lambda turn: cot_gather(turn).end())
+    weights_end(3)
+    weights_next(2)
+    weights_end(2)
+    loop(0, 4, lambda turn: cot_gather(turn).settle())
+    for chain in (tok_chain, ids_chain, wo_chain, cot_chain):
+        chain.settle()
+    for step in (0, 1, 2, 3):
+        weights_keep(step).wait()
+        for flip in (0, 1, 2, 3):
+            if step:
+                weights_ring(step, flip).wait_send()
+            if flip:
+                weights_plane(step, flip).wait_send()
+            weights_core(step, flip).wait_send()
+            weights_core(step, flip).wait_recv()
+        if step:
+            wq_ring(step).wait_send()
+            mixed_ring(step).wait_send()
+
+
+def tok_in_f32(tok, z, here):
+    return tok[z, :, here].astype(F32)
+
+
+def start(tok, ids, wq, wo, we, cot, cosine, sine, collective):
+    rows, width = tok.shape
+    own = wo.shape[0]
+    hidden3 = we.shape[-1]
+    seqlen = PLANES * rows
+    size = WINDOW * HEAD_DIM
+    blocks = (8, PLANES, own, width)
+    any_out = pl.BlockSpec(memory_space=pl.ANY)
+    vmem_out = pl.BlockSpec(memory_space=pltpu.VMEM)
+    shapes = [
+        ((8, PLANES, own, hidden3), BF16, any_out),
+        ((4, PLANES) + cot.shape, BF16, any_out),
+        ((width, width), BF16, vmem_out),
+        ((width, width), BF16, vmem_out),
+        ((PLANES, rows, width), BF16, vmem_out),
+        ((3, WINDOW, seqlen, HEAD_DIM), BF16, vmem_out),
+        ((WINDOW, seqlen, seqlen), F32, vmem_out),
+        ((WINDOW, seqlen, HEAD_DIM), F32, vmem_out),
+        ((rows, width), BF16, vmem_out),
+        ((rows, width), F32, vmem_out),
+        ((rows, width), BF16, vmem_out),
+        ((3, 4, own, hidden3), BF16, any_out),
+    ]
+    return pl.pallas_call(
+        start_kernel,
+        out_shape=[jax.ShapeDtypeStruct(shape, kind) for shape, kind, _ in shapes],
+        in_specs=[any_out] * 6 + [vmem_out] * 2,
+        out_specs=[spec for _, _, spec in shapes],
+        scratch_shapes=[
+            pltpu.VMEM((PLANES, rows, width), BF16),
+            pltpu.VMEM((PLANES,) + ids.shape, BF16),
+            pltpu.VMEM(blocks, BF16),
+            pltpu.VMEM(blocks, BF16),
+            pltpu.VMEM((PLANES * own, width), F32),
+            pltpu.VMEM((seqlen, seqlen), F32),
+            pltpu.VMEM((PLANES, rows, size), BF16),
+            pltpu.VMEM((PLANES, rows, size), BF16),
+            pltpu.SemaphoreType.DMA((10,)),
+            pltpu.SemaphoreType.DMA((39, 4)),
+            pltpu.SemaphoreType.DMA((39, 4)),
+        ],
+        compiler_params=pltpu.CompilerParams(
+            collective_id=collective, has_side_effects=True, vmem_limit_bytes=56 * 2**20
+        ),
+        name="start",
+    )(tok, ids, wq, wo, we, cot, cosine, sine)[:-1]
+
+
 def add_blocks(out, *terms):
     rows = out.shape[0]
 
@@ -665,22 +975,6 @@
         return carry
 
     lax.fori_loop(0, rows // 16, body, 0)
-
-
-def mul(a, b, over_a, over_b):
-    return lax.dot_general(a, b, (((over_a,), (over_b,)), ((), ())), preferred_element_type=F32)
-
-
-def at(start, size):
-    return pl.ds(pl.multiple_of(start, 128), size)
-
-
-def loop(first, last, body):
-    def step(i, carry):
-        body(i)
-        return carry
-
-    lax.fori_loop(first, last, step, 0)
 
 
 def experts_kernel(
@@ -797,7 +1091,13 @@
 
     loads = [
         pltpu.make_async_copy(src, dst, load_sems.at[6 + i])
-        for i, (src, dst) in enumerate(((x_in, x.at[0, chip]), (misc_in, misc), (weights_in, weights)))
+        for i, (src, dst) in enumerate(
+            (
+                (x_in, x.at[0, chip]),
+                (misc_in.at[:, pl.ds(misc_in.shape[1] - 128, 128)], misc),
+                (weights_in, weights),
+            )
+        )
     ]
     for load in loads:
         load.start()
@@ -1532,48 +1832,30 @@
         axis=1,
     )
     cot_send = jnp.concatenate([cotangent, member_cols], axis=1)
-    ids_send = jnp.broadcast_to(seq_ids.astype(BF16)[None, :], (16, rows))
-    tok_all, ids_all, wq_all, wo_all, we_all, cot_all = spread_inputs(
-        tokens, ids_send, wq_send, w_out, we_send, cot_send
-    )
-    wq_all = wq_all.reshape(width, 3 * size + 128)
+    ids_f = seq_ids.astype(BF16)
+    ids_send = jnp.concatenate(
+        [
+            jnp.broadcast_to(ids_f[None, :], (rows, rows)),
+            jnp.broadcast_to(ids_f[:, None], (rows, rows)),
+        ]
+    )
+    half_dim = HEAD_DIM // 2
+    cosine, sine_table = rotary(jnp.arange(seqlen, dtype=F32), HEAD_DIM)
+    sine_signed = sine_table[:, 0, :] * jnp.where(jnp.arange(HEAD_DIM) < half_dim, -1.0, 1.0)
+    we_all, cot_all, wq_all, out_weight, first_in, qkv, weights_exact, mixed_exact, mixed, middle, second_in = start(
+        tokens, ids_send, wq_send, w_out, we_send, cot_send, cosine[:, 0, :], sine_signed, 1
+    )
     misc_all = wq_all[:, 3 * size :]
     wq = wq_all[:, : 3 * size]
     router = misc_all[:, 1 : experts + 1]
     gain_one = misc_all[:, experts + 1].astype(F32)
     gain_two = misc_all[:, experts + 2].astype(F32)
-    out_weight = wo_all.reshape(width, width)
-
-    seq_in = tok_all.reshape(seqlen, width).astype(F32)
-    seq_normed = seq_in * rms_inverse(seq_in)
-    first_in = (seq_normed * gain_one).astype(BF16)
-    projected = dot(first_in, wq, ((1,), (0,)))
-    cosine, sine_table = rotary(jnp.arange(seqlen, dtype=F32), HEAD_DIM)
-    pq, pk, pv = (
-        projected[:, i * size : (i + 1) * size].reshape(seqlen, WINDOW, HEAD_DIM) for i in range(3)
-    )
-    query_rows = (rotate(pq, cosine, sine_table) * scale).astype(BF16)
-    key_rows = rotate(pk, cosine, sine_table).astype(BF16)
-    value_rows = pv.astype(BF16)
-    ids = ids_all[:, 0, :].reshape(seqlen)
-    at = jnp.arange(seqlen, dtype=jnp.int32)
-    allowed = ((at[None, :] <= at[:, None]) & (ids[None, :] == ids[:, None]))[None]
-    scores = jnp.einsum("qhd,khd->hqk", query_rows, key_rows, preferred_element_type=F32)
-    masked = jnp.where(allowed, scores, -1e30)
-    top = jnp.max(masked, axis=2, keepdims=True)
-    powers = jnp.where(allowed, jnp.exp(masked - top), 0.0)
-    weights_exact = powers * (1.0 / jnp.sum(powers, axis=2, keepdims=True))
-    weights_low = weights_exact.astype(BF16)
-    mixed_exact = jnp.einsum("hqk,khd->qhd", weights_low, value_rows, preferred_element_type=F32)
-    mixed_send = mixed_exact.astype(BF16).reshape(PLANES, rows, size)
-    mixed = from_windows(swap_planes(mixed_send, 2))
-    middle = tokens.astype(F32) + dot(mixed, out_weight, ((1,), (0,)))
+    first_in = first_in.reshape(seqlen, width)
     inverse_two = rms_inverse(middle)
     normed_two = middle * inverse_two
-    second_in = (normed_two * gain_two).astype(BF16)
 
     weights = we_all.reshape(width, 3 * FF)
-    grads, outs, sums = run_experts(second_in, cot_all, weights, misc_all, 3)
+    grads, outs, sums = run_experts(second_in, cot_all, weights, wq_all, 3)
 
     hi = sums[:, width + 1 : width + 1 + experts]
     lo = sums[:, width + 33 : width + 33 + experts]
@@ -1600,12 +1882,14 @@
     )[z]
     grad_heads = swap_planes(windows(grad_mixed), 5).reshape(seqlen, WINDOW, HEAD_DIM)
     grad_heads = grad_heads * valid[None, :, None]
-    row_delta = jnp.sum(grad_heads.astype(F32) * mixed_exact, axis=2).T
+    query_rows, key_rows, value_rows = qkv[0], qkv[1], qkv[2]
+    weights_low = weights_exact.astype(BF16)
+    row_delta = jnp.einsum("qhd,hqd->hq", grad_heads.astype(F32), mixed_exact)
     grad_values = jnp.einsum("hqk,qhd->khd", weights_low, grad_heads, preferred_element_type=F32)
-    grad_weights = jnp.einsum("qhd,khd->hqk", grad_heads, value_rows, preferred_element_type=F32)
+    grad_weights = jnp.einsum("qhd,hkd->hqk", grad_heads, value_rows, preferred_element_type=F32)
     grad_scores = (weights_exact * (grad_weights - row_delta[..., None])).astype(BF16)
-    grad_query = jnp.einsum("hqk,khd->qhd", grad_scores, key_rows, preferred_element_type=F32)
-    grad_keys = jnp.einsum("hqk,qhd->khd", grad_scores, query_rows, preferred_element_type=F32)
+    grad_query = jnp.einsum("hqk,hkd->qhd", grad_scores, key_rows, preferred_element_type=F32)
+    grad_keys = jnp.einsum("hqk,hqd->khd", grad_scores, query_rows, preferred_element_type=F32)
     grad_projected = jnp.concatenate(
         [
             (rotate_back(grad_query, cosine, sine_table) * scale).reshape(seqlen, size),
@@ -1616,7 +1900,7 @@
     ).astype(BF16)
     grad_qkv_part = dot(first_in, grad_projected, ((0,), (0,)), BF16)
     first_part = dot(grad_projected, wq, ((1,), (1,)))
-    gain_one_part = jnp.sum(first_part * seq_normed, axis=0)
+    gain_one_part = jnp.sum(first_part * first_in.astype(F32), axis=0) / gain_one
     misc_part = jnp.concatenate(
         [
             router_part,

time: 719 us -> 642 us (0.89)
  Pallas kernels: 605 us -> 557 us
  matrix products: 41.1 us -> 20 us
    pallas_call x1, Pallas kernels: 208 us -> 167 us  [start(): pl.pallas_call(start_kernel, out_shape=[jax.ShapeDtypeStruct(shape, kind)...]
    pallas_call x2 -> x1, Pallas kernels: 30.1 us -> 12 us  [swap_planes(): comm_call(swap_planes_kernel, 'swap_planes', collective, [jax.ShapeDtypeS...]
    pallas_call x1, Pallas kernels: 119 us -> 129 us  [run_experts(): pl.pallas_call(experts_kernel, out_shape=[jax.ShapeDtypeStruct((width, 3...]
    dot_general x5 -> x3, matrix products: 12.8 us -> 2.93 us  [the longest x1 1.85 us: expert_local(): jnp.einsum('qhd,hkd->hqk', grad_heads, value_rows, preferred_element_type...]
    dot_general x9 -> x7, matrix products: 19.7 us -> 14 us  [dot(): lax.dot_general(a, b, ((dims[0], dims[1]), ((), ())), preferred_element_t...]
where the time goes in v3:
time: 642 us; the launch traced here: 632 us
  Pallas kernels  557 us (87%)
  local copies, waits for them, and re-layouts  28.6 us (4%)
  other arithmetic  24.4 us (4%)
  matrix products  20 us (3%)
    pallas_call x1, Pallas kernels, finish(): pl.pallas_call(finish_kernel, out_shape=[jax.ShapeDtypeStruct((rows, widt...  218 us
    pallas_call x1, Pallas kernels, start(): pl.pallas_call(start_kernel, out_shape=[jax.ShapeDtypeStruct(shape, kind)...  167 us
    pallas_call x1, Pallas kernels, run_experts(): pl.pallas_call(experts_kernel, out_shape=[jax.ShapeDtypeStruct((width, 3...  129 us
    pallas_call x1, Pallas kernels, widen(): pl.pallas_call(widen_kernel, grid=(rows // step,), out_shape=[jax.ShapeDt...  31.5 us
    dot_general x7, matrix products, dot(): lax.dot_general(a, b, ((dims[0], dims[1]), ((), ())), preferred_element_t...  14 us

profile of v3, /device:TPU:29, one launch (start us, length us, event | category | flops | bytes accessed | tf_op | source)
XLA Modules:
  0.0 631.6 jit_solution(3595005462443937563)
XLA Ops:
  0.6 0.7 dynamic-slice_bitcast_fusion
  1.3 0.7 convert_element_type.83
  2.0 1.1 fusion.18
  3.2 0.7 fusion.38
  3.9 0.8 copy.110
  4.6 0.8 copy.111
  5.4 0.8 copy.109
  6.4 0.7 pad_maximum_fusion.8.ids_in
  7.2 1.8 concatenate.44.cot_in
  9.0 1.0 slice_bitcast_fusion.15
  10.0 0.8 pad_maximum_fusion.4.wq_in
  10.8 1.0 fusion.30
  11.8 0.9 pad_maximum_fusion.7
  12.6 0.8 copy.121
  13.5 0.8 copy.120
  14.3 1.5 copy.113
  15.8 0.7 copy.112
  16.5 0.2 pad_maximum_fusion
  16.7 2.0 copy.138
  18.7 166.7 %start.1 = (bf16[8,4,40,2688]{3,2,1,0:T(8,128)(2,1)}, bf16[4,4,128,1408]{3,2,1,0:T(8,128)(2,1)}, bf16[1280,1280]{1,0:T(8,128)(2,1)}, bf16[1280,1280]{1,0:T(8,128...) custom-call(bf16[128,1280]{1,0:T(8,128)(2,1)} %tok_in.1, ...), custom_call_target="tpu_custom_call" | custom-call | tf_op jit(solution)/shard_map/start/pallas_call | solution.py:941
  185.4 1.2 multiply_reduce_fusion.4
  186.6 1.5 fusion.43
  188.1 1.7 convert_reduce_fusion.1
  190.0 0.2 fusion.37
  190.2 129.2 %experts.1 = (bf16[1280,2688]{1,0:T(8,128)(2,1)}, bf16[4,4,128,1280]{3,2,1,0:T(8,128)(2,1)}, f32[128,1408]{1,0:T(8,128)}) custom-call(bf16[128,1280]{1,0:T(8,128)(2,1)} %get-tuple-element.31.x_in, bf16[4,4,128,1408]{3,2,1,0:T(8,128)(2,1)} %get-tuple-element.32.cot_in, bf16[1280,2688]{1,0:T(8,128)(2,1)} %bitcast.108, bf16[1280,1280]{1,0:T(8,128)(2,1)} %get-tuple-element.34.misc_in), custom_call_target="tpu_custom_call" | custom-call | tf_op jit(solution)/shard_map/experts/pallas_call | solution.py:1321
  319.4 1.1 multiply_reduce_fusion.5
  320.5 1.1 multiply_convert_fusion.1
  321.6 0.2 convolution_convert_fusion.3
  321.9 1.8 multiply_reduce_fusion.2
  323.7 0.2 multiply_add_fusion
  324.0 1.2 convolution_convert_fusion.2
  325.2 0.8 pad_maximum_fusion.5.x
  326.1 12.0 %swap_planes.1 = bf16[4,128,384]{2,1,0:T(8,128)(2,1)} custom-call(bf16[4,128,384]{2,1,0:T(8,128)(2,1)} %pad_maximum_fusion.5.x), custom_call_target="tpu_custom_call" | custom-call | tf_op jit(solution)/shard_map/swap_planes/pallas_call | solution.py:508
  338.0 1.2 copy.117
  339.3 0.2 reshape.115
  339.4 0.9 copy.125
  340.4 1.0 broadcast_in_dim.82
  341.3 3.1 fusion.4
  344.4 1.0 bitcast_convert_fusion
  345.4 2.5 copy.133
  347.9 1.7 multiply_reduce_fusion.1
  349.6 1.8 multiply_convert_fusion
  351.4 0.4 convolution_bitcast_fusion
  351.9 0.5 copy-done.18
  352.4 0.7 broadcast_multiply_fusion.1
  353.3 0.7 copy-done.17
  354.0 0.4 fusion.8
  354.5 1.0 copy-done.5
  355.5 3.0 multiply_reduce_fusion
  358.5 0.3 fusion.17
  358.9 3.5 convolution_convert_fusion.1
  362.5 6.5 %concatenate.50.dense_q = bf16[1280,1280]{1,0:T(8,128)(2,1)} concatenate(bf16[1280,1152]{1,0:T(8,128)(2,1)} %convolution_convert_fusion.1, bf16[1280,15]{1,0:T(8,128)(2,1)S(1)} %copy-done.12, bf16[1280,1]{1,0:T(8,128)(2,1)S(1)} %fusion.17, bf16[1280,1]{1,0:T(8,128)(2,1)S(1)} %copy-done.13, bf16[1280,111]{1,0:T(8,128)(2,1)S(1)} %broadcast_in_dim.81), dimensions={1} | concatenate | bytes 6553600 | tf_op jit(solution)/shard_map/concatenate | solution.py:1913
  368.9 2.8 convolution_convert_fusion.dense_o
  371.7 218.0 %finish.1 = (f32[128,1280]{1,0:T(8,128)}, bf16[4,4,2,160,2688]{4,3,2,1,0:T(8,128)(2,1)}, bf16[4,128,1280]{2,1,0:T(8,128)(2,1)}, bf16[4,320,1280]{2,1,0:T(8,128)(2,1)}, bf16[320,1280]{1,0:T(8,128)(2,1)}) custom-call(bf16[4,4,128,1280]{3,2,1,0:T(8,128)(2,1)} %get-tuple-element.35.outs_in, bf16[4,2,160,2688]{3,2,1,0:T(8,128)(2,1)} %bitcast.107, ...), custom_call_target="tpu_custom_call" | custom-call | tf_op jit(solution)/shard_map/finish/pallas_call | solution.py:1718
  589.8 2.0 add_convert_fusion
  591.8 1.0 convert_reduce_fusion.3
  592.8 0.9 slice_reduce_fusion
  593.7 0.7 copy.127
  594.4 0.2 convert_reduce_fusion
  594.6 0.2 fusion.12
  594.8 1.0 fusion.16
  595.8 1.3 convert_element_type.106
  597.5 2.6 convert_element_type.105
  600.1 31.5 %widen.1 = (f32[320,16,1792]{2,1,0:T(8,128)}, f32[320,16,896]{2,1,0:T(8,128)}) custom-call(bf16[16,320,2688]{2,1,0:T(8,128)(2,1)} %bitcast.104), custom_call_target="tpu_custom_call" | custom-call | tf_op jit(solution)/shard_map/widen/pallas_call | solution.py:1768
  (76 shorter events, 1.1 us)
Async XLA Ops:
  11.7 4.0 copy-start.11
  12.6 3.8 copy-start.10
  190.2 131.4 %copy-start.8 = (bf16[128,1280]{1,0:T(8,128)(2,1)S(1)}, bf16[128,1280]{1,0:T(8,128)(2,1)}, u32[]{:S(2)}) copy-start(bf16[128,1280]{1,0:T(8,128)(2,1)} %get-tuple-element.31.x_in) | copy-start | bytes 983044
  190.2 131.7 %copy-start.1 = (f32[128,1280]{1,0:T(8,128)S(1)}, f32[128,1280]{1,0:T(8,128)}, u32[]{:S(2)}) copy-start(f32[128,1280]{1,0:T(8,128)} %get-tuple-element.30) | copy-start | bytes 1966084
  319.4 4.3 copy-start.15
  321.6 2.3 copy-start.7
  324.0 1.3 copy-start.3
  344.4 5.2 copy-start
  349.5 1.9 copy-start.16
  351.4 1.0 copy-start.18
  353.0 1.0 copy-start.17
  353.1 1.3 copy-start.22
  353.2 2.3 copy-start.5
  353.2 2.3 copy-start.20
  358.8 3.6 copy-start.12
  358.9 3.6 copy-start.13
  362.5 6.5 %copy-start.4 = (f32[128,1280]{1,0:T(8,128)S(1)}, f32[128,1280]{1,0:T(8,128)}, u32[]{:S(2)}) copy-start(f32[128,1280]{1,0:T(8,128)} %copy-done.3) | copy-start | bytes 1966084
  362.5 6.5 %copy-start.21 = (bf16[128,1280]{1,0:T(8,128)(2,1)S(1)}, bf16[128,1280]{1,0:T(8,128)(2,1)}, u32[]{:S(2)}) copy-start(bf16[128,1280]{1,0:T(8,128)(2,1)} %get-tuple-element.43) | copy-start | bytes 983044
  371.7 218.1 %copy-start.2 = (f32[128,1280]{1,0:T(8,128)S(1)}, f32[128,1280]{1,0:T(8,128)}, u32[]{:S(2)}) copy-start(f32[128,1280]{1,0:T(8,128)} %get-tuple-element.30) | copy-start | bytes 1966084
  589.7 4.6 copy-start.14
  589.7 4.8 copy-start.6
  594.4 1.4 copy-start.19
  594.8 2.3 copy-start.9

commit v4 on v3

--- a/solution.py
+++ b/solution.py
@@ -413,39 +413,6 @@
     return w, z
 
 
-def other_plane(z, step):
-    return lax.rem(z + step, PLANES), lax.rem(z + PLANES - step, PLANES)
-
-
-class Net:
-    def __init__(self, send_sems, recv_sems):
-        self.send_sems, self.recv_sems, self.used, self.started = send_sems, recv_sems, 0, []
-
-    def send(self, src, dst, device):
-        copy = pltpu.make_async_remote_copy(
-            src_ref=src,
-            dst_ref=dst,
-            send_sem=self.send_sems.at[self.used],
-            recv_sem=self.recv_sems.at[self.used],
-            device_id=device,
-            device_id_type=MESH_IDS,
-        )
-        self.used += 1
-        copy.start()
-        self.started.append(copy)
-        return copy
-
-    def keep(self, src, dst):
-        copy = pltpu.make_async_copy(src, dst, self.send_sems.at[self.used])
-        self.used += 1
-        copy.start()
-        return copy
-
-    def finish(self):
-        for copy in self.started:
-            copy.wait_send()
-
-
 def greet(w, z):
     barrier = pltpu.get_barrier_semaphore()
     peers = [(w, lax.rem(z + step, PLANES)) for step in (1, 2, 3)]
@@ -455,24 +422,6 @@
     pl.semaphore_wait(barrier, len(peers))
 
 
-def comm_call(kernel, name, collective, out_shape, in_spaces, out_spaces, sems, scratch=(), moved=0):
-    return pl.pallas_call(
-        kernel,
-        out_shape=out_shape,
-        in_specs=[pl.BlockSpec(memory_space=space) for space in in_spaces],
-        out_specs=[pl.BlockSpec(memory_space=space) for space in out_spaces],
-        scratch_shapes=[
-            *scratch,
-            pltpu.SemaphoreType.DMA((sems,)),
-            pltpu.SemaphoreType.DMA((sems,)),
-        ],
-        compiler_params=pltpu.CompilerParams(
-            collective_id=collective, has_side_effects=True, vmem_limit_bytes=62 * 2**20
-        ),
-        name=name,
-    )
-
-
 def mul(a, b, over_a, over_b):
     return lax.dot_general(a, b, (((over_a,), (over_b,)), ((), ())), preferred_element_type=F32)
 
@@ -487,33 +436,6 @@
         return carry
 
     lax.fori_loop(first, last, step, 0)
-
-
-def swap_planes_kernel(x, out, send_sems, recv_sems):
-    w, z = place()
-    greet(w, z)
-    net = Net(send_sems, recv_sems)
-    own = net.keep(x.at[z], out.at[z])
-    copies = []
-    for step in (1, 2, 3):
-        to, _ = other_plane(z, step)
-        copies.append(net.send(x.at[to], out.at[z], (w, to)))
-    own.wait()
-    for copy in copies:
-        copy.wait_recv()
-    net.finish()
-
-
-def swap_planes(x, collective):
-    return comm_call(
-        swap_planes_kernel,
-        "swap_planes",
-        collective,
-        [jax.ShapeDtypeStruct(x.shape, x.dtype)],
-        [pl.ANY],
-        [pl.ANY],
-        8,
-    )(x)[0]
 
 
 class Links:
@@ -978,7 +900,7 @@
 
 
 def experts_kernel(
-    x_in, cot_in, weights_in, misc_in, grads_o, outs_o, sums_o,
+    x_in, cot_in, weights_in, misc_in, grads_o, outs_o, outs_one_o, sums_o,
     x, cot, weights, misc, act, scaled, slopes, gate, outs, parts, got_one, got_two, got_far, stage,
     load_sems, send_sems, recv_sems,
 ):
@@ -1073,6 +995,13 @@
 
     def far(step):
         return remote(7, step, parts.at[step, chip], got_far.at[step - 1], (w, plane_of(step, -1)))
+
+    def outs_near(step, which):
+        first, _ = axes(step)
+        block = chip ^ 3 if which else chip ^ first
+        return remote(
+            9 + which, step, outs_o.at[step, block], outs_one_o.at[step, which], (w ^ (2 * first), z)
+        )
 
     def cot_load(step):
         return pltpu.make_async_copy(
@@ -1221,8 +1150,6 @@
             outs_out(turn - 2).wait()
 
         second_half(turn, step)
-        near(turn, 1).start()
-        near(turn, 0).start()
         outs_out(turn).start()
 
         @pl.when(turn == 0)
@@ -1232,6 +1159,9 @@
         @pl.when(turn > 0)
         def _():
             send_cross(turn - 1)
+
+        near(turn, 1).start()
+        near(turn, 0).start()
 
         @pl.when(turn > 1)
         def _():
@@ -1265,8 +1195,12 @@
 
     loop(0, 3, up_chunk)
     send_cross(3)
+    outs_out(2).wait()
+    outs_out(3).wait()
+    loop(0, 4, lambda step: (outs_near(step, 1).start(), outs_near(step, 0).start()))
+    loop(3, 5, up_chunk)
     send_far(2)
-    loop(3, ups, up_chunk)
+    loop(5, ups, up_chunk)
     loop(ups, ups + downs, down_chunk)
     last = ups + downs
     if hidden % 256:
@@ -1276,8 +1210,6 @@
     else:
         grads_out(pl.ds(0, 256), 256, last % 2).wait()
         grads_out(pl.ds(0, 256), 256, (last - 1) % 2).wait()
-    outs_out(2).wait()
-    outs_out(3).wait()
     near(3, 0).wait_recv()
     cross(3).wait_recv()
     loop(1, 4, lambda step: far(step).wait_recv())
@@ -1299,6 +1231,9 @@
         near(turn, 0).wait_send()
         near(turn, 1).wait_send()
         cross(turn).wait_send()
+        for which in (0, 1):
+            outs_near(turn, which).wait_send()
+            outs_near(turn, which).wait_recv()
 
         @pl.when(turn < 3)
         def _():
@@ -1323,10 +1258,12 @@
         out_shape=[
             jax.ShapeDtypeStruct((width, 3 * hidden), BF16),
             jax.ShapeDtypeStruct((4, 4, rows, width), BF16),
+            jax.ShapeDtypeStruct((4, 2, rows, width), BF16),
             jax.ShapeDtypeStruct((rows, sums_width), F32),
         ],
         in_specs=[pl.BlockSpec(memory_space=pl.ANY)] * 4,
         out_specs=[
+            pl.BlockSpec(memory_space=pl.ANY),
             pl.BlockSpec(memory_space=pl.ANY),
             pl.BlockSpec(memory_space=pl.ANY),
             pl.BlockSpec(memory_space=pltpu.VMEM),
@@ -1347,8 +1284,8 @@
             pltpu.VMEM((3,) + block, BF16),
             pltpu.VMEM((2, width, 256), BF16),
             pltpu.SemaphoreType.DMA((11,)),
-            pltpu.SemaphoreType.DMA((9, 4)),
-            pltpu.SemaphoreType.DMA((8, 4)),
+            pltpu.SemaphoreType.DMA((11, 4)),
+            pltpu.SemaphoreType.DMA((11, 4)),
         ],
         compiler_params=pltpu.CompilerParams(
             collective_id=collective, has_side_effects=True, vmem_limit_bytes=62 * 2**20
@@ -1358,75 +1295,32 @@
 
 
 def finish_kernel(
-    outs_in, grads_in, first_in, dense_q, dense_o, sums_o, table_o, first_o, q_o, o_o,
-    outs, outs_one, outs_two, outs_far, grads_own, grads_got, dense, dense_got, dense_one,
-    dense_two, dense_far, dense_sum, load_sems, send_sems, recv_sems,
+    outs_in, outs_one_in, grads_in, heads_in, exact_in, mixed_in, qkv_in, first_in, wq_in, cos_in, sin_in,
+    rows_in, attn_in, misc_in, gain_in,
+    sums_o, table_o, first_o, q_o, o_o,
+    outs, outs_one, outs_two, outs_far, grads_own, grads_got, heads, exact, mixed, qkv, first, wq,
+    projected, first_part, dense, dense_got, dense_one, dense_two, dense_far, dense_sum,
+    load_sems, send_sems, recv_sems,
 ):
-    w, z = place()
+    links = Links(send_sems, recv_sems)
+    w, z = links.w, links.z
     chip, core = w // 2, w % 2
+    rows = outs.shape[2]
+    width = outs.shape[3]
+    size = WINDOW * HEAD_DIM
     steps = (1, 2, 3, 0)
     block_rows = o_o.shape[0] // 4
     half = o_o.shape[1] // 2
     plane_rows = o_o.shape[0]
-
-    def remote(kind, step, src, dst, device):
-        return pltpu.make_async_remote_copy(
-            src_ref=src,
-            dst_ref=dst,
-            send_sem=send_sems.at[kind, step],
-            recv_sem=recv_sems.at[kind, step],
-            device_id=device,
-            device_id_type=MESH_IDS,
-        )
-
-    def plane_of(step, sign):
-        return lax.rem(z + PLANES + sign * step, PLANES)
+    remote, plane_of = links.copy, links.plane
 
     def axes(step):
-        first = 1 + lax.rem(step, 2)
-        return first, 3 - first
-
-    class Gather:
-        def __init__(self, base, step, turn, slot):
-            self.base, self.step, self.slot = base, step, slot
-            self.first, self.second = axes(turn)
-
-        def copy(self, kind, owner, flip):
-            ref = self.slot(owner)
-            return remote(self.base + kind, self.step, ref, ref, (w ^ flip, z))
-
-        def begin(self):
-            self.copy(0, w, 2).start()
-            self.copy(1, w, 4).start()
-            self.copy(2, w, 1).start()
-
-        def relay(self):
-            self.copy(0, w, 2).wait_recv()
-            self.copy(1, w, 4).wait_recv()
-            self.across().start()
-            self.copy(4, w ^ 2, 1).start()
-            self.copy(5, w ^ 4, 1).start()
-
-        def across(self):
-            return self.copy(3, w ^ (2 * self.first), 2 * self.second)
-
-        def end(self):
-            self.across().wait_recv()
-            self.copy(6, w ^ 6, 1).start()
-
-        def settle(self):
-            for copy in (
-                self.copy(0, w, 2),
-                self.copy(1, w, 4),
-                self.copy(2, w, 1),
-                self.across(),
-                self.copy(4, w ^ 2, 1),
-                self.copy(5, w ^ 4, 1),
-                self.copy(6, w ^ 6, 1),
-            ):
-                copy.wait_send()
-            for kind in (2, 4, 5, 6):
-                self.copy(kind, w, 1).wait_recv()
+        one = 1 + lax.rem(step, 2)
+        return one, 3 - one
+
+    def heads_ring(step):
+        to = plane_of(step, 1)
+        return remote(37, step, heads_in.at[to], heads.at[z], (w, to))
 
     def grads_load(step):
         return pltpu.make_async_copy(
@@ -1448,39 +1342,35 @@
 
     def grads_gather(step):
         source = plane_of(step, -1)
-        return Gather(2, step, step, lambda i: table_o.at[i // 2, source, i % 2])
-
-    def outs_load(step):
-        return pltpu.make_async_copy(outs_in.at[step], outs.at[step], load_sems.at[2, step])
-
-    def near(step, which):
-        first, _ = axes(step)
-        block = chip ^ 3 if which else chip ^ first
+        return Gather(links, 2, step, step, lambda i: table_o.at[i // 2, source, i % 2])
+
+    def outs_loads(step):
+        _, two = axes(step)
+        return [
+            pltpu.make_async_copy(src, dst, load_sems.at[2 + 3 * (i > 0) + (i > 1), step])
+            for i, (src, dst) in enumerate(
+                (
+                    (outs_in.at[step, chip], outs.at[step, 0]),
+                    (outs_in.at[step, chip ^ two], outs.at[step, 1]),
+                    (outs_one_in.at[step], outs_one.at[step]),
+                )
+            )
+        ]
+
+    def cross(step):
+        _, two = axes(step)
+        return remote(11, step, outs.at[step, 1], outs_two.at[step], (w ^ (2 * two), z))
+
+    def far(step):
+        return remote(12, step, outs.at[step, 0], outs_far.at[step - 1], (w, plane_of(step, -1)))
+
+    def part(kind, step):
+        return dense.at[0, kind, plane_of(step, 1)]
+
+    def dense_swap(kind, step):
+        to = plane_of(step, 1)
         return remote(
-            9 + which, step, outs.at[step, block], outs_one.at[step, which], (w ^ (2 * first), z)
-        )
-
-    def cross(step):
-        _, second = axes(step)
-        return remote(
-            11, step, outs.at[step, chip ^ second], outs_two.at[step], (w ^ (2 * second), z)
-        )
-
-    def far(step):
-        return remote(12, step, outs.at[step, chip], outs_far.at[step - 1], (w, plane_of(step, -1)))
-
-    def dense_part(kind, step, side):
-        rows = pl.ds(pl.multiple_of(plane_of(step, 1) * plane_rows, 16), plane_rows)
-        return (dense_q, dense_o)[kind].at[rows, at(side * half, half)]
-
-    def dense_load(kind, step):
-        return pltpu.make_async_copy(
-            dense_part(kind, step, core), dense.at[kind, step], load_sems.at[3 + kind, step]
-        )
-
-    def dense_swap(kind, step):
-        return remote(
-            13 + 4 * kind, step, dense_part(kind, step, 1 - core), dense_got.at[kind, step], (w ^ 1, z)
+            13 + 4 * kind, step, dense.at[1, kind, to], dense_got.at[kind, step], (w ^ 1, z)
         )
 
     def rows_of(block):
@@ -1490,176 +1380,247 @@
         return 1 + kind, 2 - kind
 
     def dense_near(kind, step, which):
-        first, _ = dense_axes(kind)
-        block = chip ^ 3 if which else chip ^ first
+        one, _ = dense_axes(kind)
+        block = chip ^ 3 if which else chip ^ one
         return remote(
             14 + 4 * kind + which,
             step,
-            dense.at[kind, step, rows_of(block)],
+            part(kind, step).at[rows_of(block)],
             dense_one.at[kind, step, which],
-            (w ^ (2 * first), z),
+            (w ^ (2 * one), z),
         )
 
     def dense_cross(kind, step):
-        _, second = dense_axes(kind)
+        _, two = dense_axes(kind)
         return remote(
             16 + 4 * kind,
             step,
-            dense.at[kind, step, rows_of(chip ^ second)],
+            part(kind, step).at[rows_of(chip ^ two)],
             dense_two.at[kind, step],
-            (w ^ (2 * second), z),
+            (w ^ (2 * two), z),
         )
 
     def place_of(owner):
         return rows_of(owner // 2), at(lax.rem(owner, 2) * half, half)
 
     def dense_ring(kind, step):
-        own = dense.at[kind, step, rows_of(chip)]
-        rows, columns = place_of(w)
-        to = q_o.at[z, rows, columns] if kind == 0 else dense_far.at[step - 1]
+        own = part(kind, step).at[rows_of(chip)]
+        here, columns = place_of(w)
+        to = q_o.at[z, here, columns] if kind == 0 else dense_far.at[step - 1]
         return remote(21 + kind, step, own, to, (w, plane_of(step, 1)))
 
     def dense_keep():
-        rows, columns = place_of(w)
+        here, columns = place_of(w)
         return pltpu.make_async_copy(
-            dense.at[0, 0, rows_of(chip)], q_o.at[z, rows, columns], load_sems.at[1, 1]
+            part(0, 0).at[rows_of(chip)], q_o.at[z, here, columns], load_sems.at[1, 1]
         )
 
     def dense_last():
-        rows, columns = place_of(w)
-        return pltpu.make_async_copy(dense_sum, o_o.at[rows, columns], load_sems.at[1, 2])
+        here, columns = place_of(w)
+        return pltpu.make_async_copy(dense_sum, o_o.at[here, columns], load_sems.at[1, 2])
 
     def q_slot(step):
         source = plane_of(step, -1)
 
         def slot(owner):
-            rows, columns = place_of(owner)
-            return q_o.at[source, rows, columns]
+            here, columns = place_of(owner)
+            return q_o.at[source, here, columns]
 
         return slot
 
     def o_slot(owner):
-        rows, columns = place_of(owner)
-        return o_o.at[rows, columns]
+        here, columns = place_of(owner)
+        return o_o.at[here, columns]
 
     def q_gather(step):
-        return Gather(23, step, step, q_slot(step))
+        return Gather(links, 23, step, step, q_slot(step))
 
     def o_gather():
-        return Gather(30, 0, 0, o_slot)
+        return Gather(links, 30, 0, 0, o_slot)
 
     def first_ring(step):
-        return remote(37, step, first_in.at[plane_of(step, 1)], first_o.at[z], (w, plane_of(step, 1)))
+        to = plane_of(step, 1)
+        return remote(38, step, first_part.at[to], first_o.at[z], (w, to))
 
     def first_keep():
-        return pltpu.make_async_copy(first_in.at[z], first_o.at[z], load_sems.at[1, 3])
-
+        return pltpu.make_async_copy(first_part.at[z], first_o.at[z], load_sems.at[1, 3])
+
+    loads = [
+        pltpu.make_async_copy(src, dst, load_sems.at[3 + i // 4, i % 4])
+        for i, (src, dst) in enumerate(
+            (
+                (heads_in.at[z], heads.at[z]),
+                (exact_in, exact),
+                (mixed_in, mixed),
+                (qkv_in, qkv),
+                (first_in, first),
+                (wq_in, wq),
+            )
+        )
+    ]
     for step in steps:
         grads_load(step).start()
     for step in steps:
-        outs_load(step).start()
-        for kind in (0, 1):
-            dense_load(kind, step).start()
-    first_keep().start()
+        for load in outs_loads(step):
+            load.start()
+    for load in loads:
+        load.start()
     greet(w, z)
+    for step in (1, 2, 3):
+        heads_ring(step).start()
     for step in steps:
         grads_swap(step).start()
-    for step in steps:
-        for kind in (0, 1):
-            dense_swap(kind, step).start()
-    for step in (1, 2, 3):
-        first_ring(step).start()
 
     def grads_ready(step):
         grads_load(step).wait()
         grads_swap(step).wait_recv()
         add_blocks(grads_own.at[step], grads_own.at[step], grads_got.at[step])
 
-    def dense_ready(kind, step):
-        dense_load(kind, step).wait()
-        dense_swap(kind, step).wait_recv()
-        add_blocks(dense.at[kind, step], dense.at[kind, step], dense_got.at[kind, step])
-        dense_near(kind, step, 1).start()
-        dense_near(kind, step, 0).start()
-
-    loop(1, 4, lambda step: (grads_ready(step), grads_ring(step).start()))
     grads_ready(0)
     keep = grads_keep()
     keep.start()
 
-    def dense_start(step):
-        dense_ready(0, step)
-        dense_ready(1, step)
-
-    loop(0, 4, dense_start)
+    def outs_cross(step):
+        for load in outs_loads(step):
+            load.wait()
+        add_blocks(outs.at[step, 1], outs.at[step, 1], outs_one.at[step, 1])
+        cross(step).start()
+
     keep.wait()
     grads_gather(0).begin()
-
-    def outs_start(step):
-        outs_load(step).wait()
-        near(step, 1).start()
-        near(step, 0).start()
-
-    loop(0, 4, outs_start)
-
-    def dense_cross_start(step):
-        for kind in (0, 1):
-            _, second = dense_axes(kind)
-            dense_near(kind, step, 1).wait_recv()
-            block = dense.at[kind, step, rows_of(chip ^ second)]
-            add_blocks(block, block, dense_one.at[kind, step, 1])
-            dense_cross(kind, step).start()
-
-    loop(0, 4, dense_cross_start)
+    loop(1, 4, grads_ready)
+    loop(0, 4, outs_cross)
+    for step in (1, 2, 3):
+        heads_ring(step).wait_recv()
+    grads_ring(1).start()
+    grads_ring(3).start()
+
+    def out_weight(i):
+        side = i // (half // 128)
+        low = at((i - side * (half // 128)) * 128, 128)
+        total = mul(rows_in[...], attn_in[:, at(i * 128, 128)], 0, 0).astype(BF16)
+        dense[side ^ core, 1, :, :, low] = total.reshape(PLANES, plane_rows, 128)
+
+    loop(0, width // 128, out_weight)
+    for step in steps:
+        dense_swap(1, step).start()
+    for load in loads:
+        load.wait()
+
+    def head_back(head):
+        keep_head = jnp.float32(0)
+        for plane, (a, b) in enumerate(KEEP):
+            keep_head = jnp.where((z == plane) & (head >= a) & (head < b), 1.0, keep_head)
+        columns = at(head * HEAD_DIM, HEAD_DIM)
+        grad_rows = heads[:, :, columns].reshape(PLANES * rows, HEAD_DIM).astype(F32) * keep_head
+        delta = jnp.sum(grad_rows * mixed[head], axis=1, keepdims=True)
+        grad_rows = grad_rows.astype(BF16)
+        weights = exact[head]
+        grad_value = mul(weights.astype(BF16), grad_rows, 0, 0)
+        grad_scores = mul(grad_rows, qkv[2, head], 1, 1)
+        grad_scores = (weights * (grad_scores - delta)).astype(BF16)
+        grad_query = mul(grad_scores, qkv[1, head], 1, 0) * (HEAD_DIM ** (-0.5))
+        grad_key = mul(grad_scores, qkv[0, head], 0, 0)
+
+        def back(grads):
+            return grads * cos_in[...] + pltpu.roll(grads * sin_in[...], HEAD_DIM // 2, 1)
+
+        projected[:, columns] = back(grad_query).astype(BF16)
+        projected[:, at(size + head * HEAD_DIM, HEAD_DIM)] = back(grad_key).astype(BF16)
+        projected[:, at(2 * size + head * HEAD_DIM, HEAD_DIM)] = grad_value.astype(BF16)
+
+    loop(0, WINDOW, head_back)
 
     def grads_next(step):
         grads_ring(step).wait_recv()
         grads_gather(step).begin()
 
+    grads_gather(0).relay()
+
+    def qkv_weight(i):
+        side = i // (half // 128)
+        low = at((i - side * (half // 128)) * 128, 128)
+        total = mul(first[...].reshape(PLANES * rows, width), projected[:, at(i * 128, 128)], 0, 0)
+        dense[side ^ core, 0, :, :, low] = total.astype(BF16).reshape(PLANES, plane_rows, 128)
+
+    loop(0, 3 * size // 128, qkv_weight)
+    gain_parts = []
+    for i in range(width // 256):
+        here = slice(i * 256, (i + 1) * 256)
+        total = mul(projected[...], wq[here, : 3 * size], 1, 1)
+        first_part[:, :, here] = total.astype(BF16).reshape(PLANES, rows, 256)
+        scaled = total * first[:, :, here].reshape(PLANES * rows, 256).astype(F32)
+        gain_parts.append(jnp.sum(scaled, axis=0, keepdims=True))
+    gain_row = jnp.concatenate(gain_parts, axis=1) / gain_in[0:1, :]
+    gain_columns = jnp.transpose(jnp.broadcast_to(gain_row, (128, width)))
+    lane = lax.broadcasted_iota(jnp.int32, gain_columns.shape, 1)
+    misc = jnp.where(lane == 15, gain_columns, misc_in[...])
+    dense[1 ^ core, 0, :, :, half - 128 :] = misc.astype(BF16).reshape(PLANES, plane_rows, 128)
+    for step in steps:
+        dense_swap(0, step).start()
+
+    keep_first = first_keep()
+    keep_first.start()
+    for step in (1, 2, 3):
+        first_ring(step).start()
+    grads_ring(2).start()
     loop(1, 2, grads_next)
 
-    def outs_cross(step):
-        _, second = axes(step)
-        near(step, 1).wait_recv()
-        block = outs.at[step, chip ^ second]
-        add_blocks(block, block, outs_one.at[step, 1])
-        cross(step).start()
-
-    loop(0, 4, outs_cross)
+    def dense_ready(step):
+        for kind in (0, 1):
+            dense_swap(kind, step).wait_recv()
+            block = part(kind, step)
+            add_blocks(block, block, dense_got.at[kind, step])
+            dense_near(kind, step, 1).start()
+            dense_near(kind, step, 0).start()
+
+    loop(0, 4, dense_ready)
+
+    def outs_finish(step):
+        cross(step).wait_recv()
+        block = outs.at[step, 0]
+        add_blocks(block, block, outs_one.at[step, 0], outs_two.at[step])
+
+        @pl.when(step > 0)
+        def _():
+            far(step).start()
+
+    loop(0, 4, outs_finish)
+    grads_gather(0).end()
+    loop(3, 4, grads_next)
+    grads_gather(1).relay()
+
+    def dense_cross_start(step):
+        for kind in (0, 1):
+            _, two = dense_axes(kind)
+            dense_near(kind, step, 1).wait_recv()
+            block = part(kind, step).at[rows_of(chip ^ two)]
+            add_blocks(block, block, dense_one.at[kind, step, 1])
+            dense_cross(kind, step).start()
+
+    loop(0, 4, dense_cross_start)
+    grads_gather(1).end()
+    grads_gather(3).relay()
 
     def dense_finish(step):
         for kind in (0, 1):
             dense_near(kind, step, 0).wait_recv()
             dense_cross(kind, step).wait_recv()
-            block = dense.at[kind, step, rows_of(chip)]
+            block = part(kind, step).at[rows_of(chip)]
             add_blocks(block, block, dense_one.at[kind, step, 0], dense_two.at[kind, step])
 
+        @pl.when(step > 0)
+        def _():
+            dense_ring(0, step).start()
+            dense_ring(1, step).start()
+
     loop(0, 4, dense_finish)
-
-    def dense_ring_start(step):
-        dense_ring(0, step).start()
-        dense_ring(1, step).start()
-
-    loop(1, 4, dense_ring_start)
     keep = dense_keep()
     keep.start()
-    loop(2, 3, grads_next)
-    loop(0, 1, lambda step: grads_gather(step).relay())
     keep.wait()
     q_gather(0).begin()
-
-    def outs_finish(step):
-        near(step, 0).wait_recv()
-        cross(step).wait_recv()
-        block = outs.at[step, chip]
-        add_blocks(block, block, outs_one.at[step, 0], outs_two.at[step])
-
-        @pl.when(step > 0)
-        def _():
-            far(step).start()
-
-    loop(0, 4, outs_finish)
-    loop(3, 4, grads_next)
+    loop(2, 3, grads_next)
+    grads_gather(3).end()
 
     def q_next(step):
         dense_ring(0, step).wait_recv()
@@ -1668,29 +1629,27 @@
 
     loop(1, 4, q_next)
     add_blocks(
-        dense_sum, dense.at[1, 0, rows_of(chip)], dense_far.at[0], dense_far.at[1], dense_far.at[2]
+        dense_sum, part(1, 0).at[rows_of(chip)], dense_far.at[0], dense_far.at[1], dense_far.at[2]
     )
     keep = dense_last()
     keep.start()
     keep.wait()
     o_gather().begin()
-    loop(1, 4, lambda step: grads_gather(step).relay())
+    grads_gather(2).relay()
     loop(0, 4, lambda step: q_gather(step).relay())
     o_gather().relay()
     loop(1, 4, lambda step: far(step).wait_recv())
-    add_blocks(sums_o, outs.at[0, chip], outs_far.at[0], outs_far.at[1], outs_far.at[2])
-    loop(0, 4, lambda step: grads_gather(step).end())
+    add_blocks(sums_o, outs.at[0, 0], outs_far.at[0], outs_far.at[1], outs_far.at[2])
+    grads_gather(2).end()
     loop(0, 4, lambda step: q_gather(step).end())
     o_gather().end()
     loop(0, 4, lambda step: grads_gather(step).settle())
     loop(0, 4, lambda step: q_gather(step).settle())
     o_gather().settle()
-    first_keep().wait()
+    keep_first.wait()
 
     def settle(step):
         grads_swap(step).wait_send()
-        near(step, 0).wait_send()
-        near(step, 1).wait_send()
         cross(step).wait_send()
         for kind in (0, 1):
             dense_swap(kind, step).wait_send()
@@ -1703,6 +1662,7 @@
     def settle_rings(step):
         first_ring(step).wait_recv()
         first_ring(step).wait_send()
+        heads_ring(step).wait_send()
         grads_ring(step).wait_send()
         far(step).wait_send()
         dense_ring(0, step).wait_send()
@@ -1711,10 +1671,16 @@
     loop(1, 4, settle_rings)
 
 
-def finish(outs, grads, first, dense_q, dense_o, collective):
+def finish(
+    outs, outs_one, grads, heads, exact, mixed, qkv, first, wq, tables, rows_attn, misc, gain, collective
+):
     rows, width = first.shape[1:]
+    seqlen = PLANES * rows
+    size = WINDOW * HEAD_DIM
     plane_rows = width // PLANES
     block = (plane_rows // 4, width // 2)
+    any_spec = pl.BlockSpec(memory_space=pl.ANY)
+    vmem_spec = pl.BlockSpec(memory_space=pltpu.VMEM)
     return pl.pallas_call(
         finish_kernel,
         out_shape=[
@@ -1724,30 +1690,38 @@
             jax.ShapeDtypeStruct((PLANES, plane_rows, width), BF16),
             jax.ShapeDtypeStruct((plane_rows, width), BF16),
         ],
-        in_specs=[pl.BlockSpec(memory_space=pl.ANY)] * 5,
-        out_specs=[pl.BlockSpec(memory_space=pltpu.VMEM)] + [pl.BlockSpec(memory_space=pl.ANY)] * 4,
+        in_specs=[any_spec] * 9 + [vmem_spec] * 6,
+        out_specs=[vmem_spec] + [any_spec] * 4,
         scratch_shapes=[
-            pltpu.VMEM((4, 4, rows, width), BF16),
+            pltpu.VMEM((4, 2, rows, width), BF16),
             pltpu.VMEM((4, 2, rows, width), BF16),
             pltpu.VMEM((4, rows, width), BF16),
             pltpu.VMEM((3, rows, width), BF16),
             pltpu.VMEM((4,) + grads.shape[2:], BF16),
             pltpu.VMEM((4,) + grads.shape[2:], BF16),
-            pltpu.VMEM((2, 4, plane_rows, width // 2), BF16),
+            pltpu.VMEM(heads.shape, BF16),
+            pltpu.VMEM(exact.shape, F32),
+            pltpu.VMEM(mixed.shape, F32),
+            pltpu.VMEM(qkv.shape, BF16),
+            pltpu.VMEM(first.shape, BF16),
+            pltpu.VMEM(wq.shape, BF16),
+            pltpu.VMEM((seqlen, 3 * size), BF16),
+            pltpu.VMEM(first.shape, BF16),
+            pltpu.VMEM((2, 2, PLANES, plane_rows, width // 2), BF16),
             pltpu.VMEM((2, 4, plane_rows, width // 2), BF16),
             pltpu.VMEM((2, 4, 2) + block, BF16),
             pltpu.VMEM((2, 4) + block, BF16),
             pltpu.VMEM((3,) + block, BF16),
             pltpu.VMEM(block, BF16),
-            pltpu.SemaphoreType.DMA((5, 4)),
-            pltpu.SemaphoreType.DMA((38, 4)),
-            pltpu.SemaphoreType.DMA((38, 4)),
+            pltpu.SemaphoreType.DMA((7, 4)),
+            pltpu.SemaphoreType.DMA((39, 4)),
+            pltpu.SemaphoreType.DMA((39, 4)),
         ],
         compiler_params=pltpu.CompilerParams(
-            collective_id=collective, has_side_effects=True, vmem_limit_bytes=60 * 2**20
+            collective_id=collective, has_side_effects=True, vmem_limit_bytes=62 * 2**20
         ),
         name="finish",
-    )(outs, grads, first, dense_q, dense_o)
+    )(outs, outs_one, grads, heads, exact, mixed, qkv, first, wq, *tables, *rows_attn, misc, gain)
 
 
 def widen_kernel(table, up_o, down_o):
@@ -1764,7 +1738,7 @@
 def widen(table):
     experts, rows, columns = table.shape
     split = columns // 3 * 2
-    step = 16
+    step = rows // 4
     return pl.pallas_call(
         widen_kernel,
         grid=(rows // step,),
@@ -1777,7 +1751,7 @@
             pl.BlockSpec((step, experts, split), lambda i: (i, 0, 0)),
             pl.BlockSpec((step, experts, columns - split), lambda i: (i, 0, 0)),
         ],
-        compiler_params=pltpu.CompilerParams(vmem_limit_bytes=48 * 2**20),
+        compiler_params=pltpu.CompilerParams(vmem_limit_bytes=60 * 2**20),
         name="widen",
     )(table)
 
@@ -1805,8 +1779,6 @@
     experts = w_router.shape[1]
     seqlen = PLANES * rows
     size = WINDOW * HEAD_DIM
-    scale = HEAD_DIM ** (-0.5)
-    z = lax.axis_index("narrow")
 
     misc = jnp.concatenate(
         [
@@ -1846,16 +1818,14 @@
         tokens, ids_send, wq_send, w_out, we_send, cot_send, cosine[:, 0, :], sine_signed, 1
     )
     misc_all = wq_all[:, 3 * size :]
-    wq = wq_all[:, : 3 * size]
     router = misc_all[:, 1 : experts + 1]
     gain_one = misc_all[:, experts + 1].astype(F32)
     gain_two = misc_all[:, experts + 2].astype(F32)
-    first_in = first_in.reshape(seqlen, width)
     inverse_two = rms_inverse(middle)
     normed_two = middle * inverse_two
 
     weights = we_all.reshape(width, 3 * FF)
-    grads, outs, sums = run_experts(second_in, cot_all, weights, wq_all, 3)
+    grads, outs, outs_one, sums = run_experts(second_in, cot_all, weights, wq_all, 3)
 
     hi = sums[:, width + 1 : width + 1 + experts]
     lo = sums[:, width + 33 : width + 33 + experts]
@@ -1874,49 +1844,30 @@
     )
     router_part = dot(second_in, grad_logits, ((0,), (0,)))
     grad_attention = grad_middle.astype(BF16)
-    grad_out_part = dot(mixed, grad_attention, ((0,), (0,)), BF16)
     grad_mixed = dot(grad_attention, out_weight, ((1,), (1,)), BF16)
-
-    valid = jnp.array(
-        [[a <= i < b for i in range(WINDOW)] for a, b in KEEP], dtype=BF16
-    )[z]
-    grad_heads = swap_planes(windows(grad_mixed), 5).reshape(seqlen, WINDOW, HEAD_DIM)
-    grad_heads = grad_heads * valid[None, :, None]
-    query_rows, key_rows, value_rows = qkv[0], qkv[1], qkv[2]
-    weights_low = weights_exact.astype(BF16)
-    row_delta = jnp.einsum("qhd,hqd->hq", grad_heads.astype(F32), mixed_exact)
-    grad_values = jnp.einsum("hqk,qhd->khd", weights_low, grad_heads, preferred_element_type=F32)
-    grad_weights = jnp.einsum("qhd,hkd->hqk", grad_heads, value_rows, preferred_element_type=F32)
-    grad_scores = (weights_exact * (grad_weights - row_delta[..., None])).astype(BF16)
-    grad_query = jnp.einsum("hqk,hkd->qhd", grad_scores, key_rows, preferred_element_type=F32)
-    grad_keys = jnp.einsum("hqk,hqd->khd", grad_scores, query_rows, preferred_element_type=F32)
-    grad_projected = jnp.concatenate(
-        [
-            (rotate_back(grad_query, cosine, sine_table) * scale).reshape(seqlen, size),
-            rotate_back(grad_keys, cosine, sine_table).reshape(seqlen, size),
-            grad_values.reshape(seqlen, size),
-        ],
-        axis=1,
-    ).astype(BF16)
-    grad_qkv_part = dot(first_in, grad_projected, ((0,), (0,)), BF16)
-    first_part = dot(grad_projected, wq, ((1,), (1,)))
-    gain_one_part = jnp.sum(first_part * first_in.astype(F32), axis=0) / gain_one
     misc_part = jnp.concatenate(
         [
             router_part,
-            gain_one_part[:, None],
+            jnp.zeros((width, 1), F32),
             gain_two_part[:, None],
             jnp.zeros((width, 128 - experts - 2), F32),
         ],
         axis=1,
-    ).astype(BF16)
-    dense_q = jnp.concatenate([grad_qkv_part, misc_part], axis=1)
+    )
     sums, table, first_all, q_all, o_all = finish(
         outs,
+        outs_one,
         grads.reshape(PLANES, 2, width // PLANES // 2, 3 * FF),
-        first_part.astype(BF16).reshape(PLANES, rows, width),
-        dense_q,
-        grad_out_part,
+        windows(grad_mixed),
+        weights_exact,
+        mixed_exact,
+        qkv,
+        first_in,
+        wq_all,
+        (cosine[:, 0, :], sine_signed),
+        (mixed, grad_attention),
+        misc_part,
+        jnp.broadcast_to(gain_one[None, :], (8, width)),
         6,
     )
     output = (middle + sums).astype(BF16)

time: 642 us -> 577 us (0.90)
  Pallas kernels: 557 us -> 534 us
  local copies, waits for them, and re-layouts: 28.6 us -> 11.3 us
  matrix products: 20 us -> 5.94 us
    pallas_call x1 -> x0, Pallas kernels: 12 us -> none  [swap_planes(): comm_call(swap_planes_kernel, 'swap_planes', collective, [jax.ShapeDtypeS...]
    pallas_call x1, Pallas kernels: 218 us -> 210 us  [finish(): pl.pallas_call(finish_kernel, out_shape=[jax.ShapeDtypeStruct((rows, widt...]
    dot_general x7 -> x4, matrix products: 14 us -> 5.94 us  [dot(): lax.dot_general(a, b, ((dims[0], dims[1]), ((), ())), preferred_element_t...]
    concatenate x3 -> x2, local copies, waits for them, and re-layouts: 8.11 us -> 0.15 us  [expert_local(): jnp.concatenate([router_part, jnp.zeros((width, 1), F32), gain_two_part[:...]
where the time goes in v4:
time: 577 us; the launch traced here: 573 us
  Pallas kernels  534 us (93%)
  other arithmetic  20.6 us (4%)
  local copies, waits for them, and re-layouts  11.3 us (2%)
  matrix products  5.94 us (1%)
    pallas_call x1, Pallas kernels, finish(): pl.pallas_call(finish_kernel, out_shape=[jax.ShapeDtypeStruct((rows, widt...  210 us
    pallas_call x1, Pallas kernels, start(): pl.pallas_call(start_kernel, out_shape=[jax.ShapeDtypeStruct(shape, kind)...  167 us
    pallas_call x1, Pallas kernels, run_experts(): pl.pallas_call(experts_kernel, out_shape=[jax.ShapeDtypeStruct((width, 3...  131 us
    pallas_call x1, Pallas kernels, widen(): pl.pallas_call(widen_kernel, grid=(rows // step,), out_shape=[jax.ShapeDt...  26.7 us

profile of v4, /device:TPU:29, one launch (start us, length us, event | category | flops | bytes accessed | tf_op | source)
XLA Modules:
  0.0 572.9 jit_solution(13395583546347268890)
XLA Ops:
  0.6 0.0 copy-start.8
  0.7 0.8 convert_element_type.59
  1.4 1.1 fusion.7
  2.5 0.1 pad.1.clone
  2.6 0.1 pad.3.clone
  2.7 0.7 fusion.15
  3.4 0.8 copy.59
  4.2 0.8 copy.60
  4.9 0.8 copy.58
  5.7 0.1 concatenate.28
  5.8 0.1 copy.64
  6.0 0.7 pad_maximum_fusion.4.ids_in
  6.8 1.8 concatenate.31.cot_in
  8.6 1.0 slice_bitcast_fusion.15
  9.5 0.0 copy-start.7
  9.5 0.8 pad_maximum_fusion.1.wq_in
  10.3 1.0 fusion.11
  11.3 1.0 pad_maximum_fusion.3
  12.3 0.0 copy-done.8
  12.3 0.2 copy.62
  12.5 0.0 copy-done.7
  12.5 0.7 copy.61
  13.2 0.2 pad_maximum_fusion
  13.4 2.0 copy.71
  15.4 166.5 %start.1 = (bf16[8,4,40,2688]{3,2,1,0:T(8,128)(2,1)}, bf16[4,4,128,1408]{3,2,1,0:T(8,128)(2,1)}, bf16[1280,1280]{1,0:T(8,128)(2,1)}, bf16[1280,1280]{1,0:T(8,128...) custom-call(bf16[128,1280]{1,0:T(8,128)(2,1)} %tok_in.1, ...), custom_call_target="tpu_custom_call" | custom-call | tf_op jit(solution)/shard_map/start/pallas_call | solution.py:863
  182.0 1.2 multiply_reduce_fusion.2
  183.2 1.5 fusion.17
  184.8 1.6 convert_reduce_fusion.1
  186.3 0.6 broadcast_in_dim.87.gain_in
  187.0 0.1 copy.65
  187.1 0.2 fusion.14
  187.3 0.0 copy-start.4
  187.3 0.0 copy-start
  187.3 131.3 %experts.1 = (bf16[1280,2688]{1,0:T(8,128)(2,1)}, bf16[4,4,128,1280]{3,2,1,0:T(8,128)(2,1)}, bf16[4,2,128,1280]{3,2,1,0:T(8,128)(2,1)}, f32[128,1408]{1,0:T(8,128)}) custom-call(bf16[128,1280]{1,0:T(8,128)(2,1)} %get-tuple-element.32.x_in, bf16[4,4,128,1408]{3,2,1,0:T(8,128)(2,1)} %get-tuple-element.33.cot_in, bf16[1280,2688]{1,0:T(8,128)(2,1)} %bitcast.75, ...), custom_call_target="tpu_custom_call" | custom-call | tf_op jit(solution)/shard_map/experts/pallas_call | solution.py:1256
  318.6 0.0 copy-start.3
  318.6 1.1 multiply_reduce_fusion.3
  319.7 0.0 copy-done.4
  319.7 0.0 copy-start.2
  319.8 1.4 fusion.18
  321.2 0.0 copy-done
  321.2 1.8 multiply_reduce_fusion
  323.0 0.0 copy-done.3
  323.0 0.2 fusion.16.attn_in
  323.2 0.0 copy-done.2
  323.2 0.0 copy-start.5
  323.3 1.2 convolution_convert_fusion
  324.5 0.8 pad_maximum_fusion.2.heads_in
  325.3 0.0 copy-done.5
  325.3 0.2 broadcast_in_dim.88
  325.6 1.1 maximum_maximum_fusion.misc_in
  326.6 209.5 %finish.1 = (f32[128,1280]{1,0:T(8,128)}, bf16[4,4,2,160,2688]{4,3,2,1,0:T(8,128)(2,1)}, bf16[4,128,1280]{2,1,0:T(8,128)(2,1)}, bf16[4,320,1280]{2,1,0:T(8,128)(2,1)}, bf16[320,1280]{1,0:T(8,128)(2,1)}) custom-call(bf16[4,4,128,1280]{3,2,1,0:T(8,128)(2,1)} %get-tuple-element.36.outs_in, bf16[4,2,128,1280]{3,2,1,0:T(8,128)(2,1)} %get-tuple-element.37.outs_one_in, ...), custom_call_target="tpu_custom_call" | custom-call | tf_op jit(solution)/shard_map/finish/pallas_call | solution.py:1684
  536.2 0.0 copy-start.1
  536.2 1.1 convert_reduce_fusion.3
  537.3 0.9 slice_reduce_fusion
  538.1 0.7 copy.68
  538.9 1.6 convert_reduce_fusion
  540.5 0.0 copy-done.1
  540.5 0.0 copy-start.9
  540.5 0.2 fusion.2
  540.8 1.2 fusion.6
  542.0 0.0 copy-done.9
  542.0 1.3 convert_element_type.75
  543.7 2.6 convert_element_type.74
  546.2 26.7 %widen.1 = (f32[320,16,1792]{2,1,0:T(8,128)}, f32[320,16,896]{2,1,0:T(8,128)}) custom-call(bf16[16,320,2688]{2,1,0:T(8,128)(2,1)} %bitcast.71), custom_call_target="tpu_custom_call" | custom-call | tf_op jit(solution)/shard_map/widen/pallas_call | solution.py:1742
  (32 shorter events, 0.5 us)
Async XLA Ops:
  0.6 11.7 %copy-start.8 = (bf16[40,16,896]{2,1,0:T(8,128)(2,1)S(1)}, bf16[40,16,896]{2,1,0:T(8,128)(2,1)}, u32[]{:S(2)}) copy-start(bf16[40,16,896]{2,1,0:T(8,128)(2,1)} %param.21) | copy-start | bytes 3440644
  9.5 3.0 copy-start.7
  187.3 132.5 %copy-start.4 = (bf16[128,1280]{1,0:T(8,128)(2,1)S(1)}, bf16[128,1280]{1,0:T(8,128)(2,1)}, u32[]{:S(2)}) copy-start(bf16[128,1280]{1,0:T(8,128)(2,1)} %get-tuple-element.32.x_in) | copy-start | bytes 983044
  187.3 133.9 %copy-start = (f32[128,1280]{1,0:T(8,128)S(1)}, f32[128,1280]{1,0:T(8,128)}, u32[]{:S(2)}) copy-start(f32[128,1280]{1,0:T(8,128)} %get-tuple-element.31) | copy-start | bytes 1966084
  318.6 4.4 copy-start.3
  319.7 3.5 copy-start.2
  323.2 2.1 copy-start.5
  536.2 4.3 copy-start.1
  538.9 1.9 copy-start.10
  540.5 1.5 copy-start.9
  540.8 2.5 copy-start.6

commit v5 on v4

--- a/solution.py
+++ b/solution.py
@@ -465,6 +465,34 @@
     return step
 
 
+def direct_at(z, turn):
+    even = lax.rem(z, 2) == 0
+    first, second = jnp.where(even, 3, 1), jnp.where(even, 1, 3)
+    return jnp.where(turn == 0, first, jnp.where(turn == 1, second, jnp.where(turn == 2, 2, 0)))
+
+
+def send_next(z, send):
+    @pl.when(z < PLANES - 1)
+    def _():
+        send(1)
+
+    @pl.when(z > 0)
+    def _():
+        send(3)
+
+
+def send_beyond(z, send):
+    @pl.when(z == 0)
+    def _():
+        send(3)
+
+    @pl.when(z == PLANES - 1)
+    def _():
+        send(1)
+
+    send(2)
+
+
 class Chain:
     def __init__(self, links, base, own, slot):
         self.links, self.base, self.own, self.slot = links, base, own, slot
@@ -516,8 +544,9 @@
 
 
 class Gather:
-    def __init__(self, links, base, step, turn, slot, cores=True):
+    def __init__(self, links, base, step, turn, slot, cores=True, half=0):
         self.links, self.base, self.step, self.slot, self.cores = links, base, step, slot, cores
+        self.half = half
         self.first = 1 + lax.rem(turn, 2)
         self.second = 3 - self.first
 
@@ -538,16 +567,28 @@
         w = self.links.w
         self.copy(0, w, 2).wait_recv()
         self.copy(1, w, 4).wait_recv()
-        self.across().start()
+        for copy in self.across():
+            copy.start()
         if self.cores:
             self.copy(3, w ^ 2, 1).start()
             self.copy(5, w ^ 4, 1).start()
 
     def across(self):
-        return self.copy(2, self.links.w ^ (2 * self.first), 2 * self.second)
+        if not self.half:
+            return [self.copy(2, self.links.w ^ (2 * self.first), 2 * self.second)]
+        copies = []
+        for kind, flip in ((2, 2), (7, 4)):
+            ref = self.slot(self.links.w ^ flip).at[pl.ds((kind == 7) * self.half, self.half)]
+            copies.append(
+                self.links.copy(
+                    self.base + kind, self.step, ref, ref, (self.links.w ^ (6 - flip), self.links.z)
+                )
+            )
+        return copies
 
     def end(self):
-        self.across().wait_recv()
+        for copy in self.across():
+            copy.wait_recv()
         if self.cores:
             self.copy(6, self.links.w ^ 6, 1).start()
 
@@ -555,7 +596,8 @@
         w = self.links.w
         self.copy(0, w, 2).wait_send()
         self.copy(1, w, 4).wait_send()
-        self.across().wait_send()
+        for copy in self.across():
+            copy.wait_send()
         if self.cores:
             for kind, owner in ((4, w), (3, w ^ 2), (5, w ^ 4), (6, w ^ 6)):
                 copy = self.copy(kind, owner, 1)
@@ -627,42 +669,52 @@
             26 + flip, step, we_in.at[to, chip ^ flip], hop.at[step - 1, chip ^ flip], (w, to)
         )
 
-    def weights_block(step, flip):
-        return hop.at[step - 1, chip ^ flip] if step else we_in.at[z, chip ^ flip]
-
-    def weights_plane(step, flip):
-        to = we_o.at[w, links.plane(step, -1)]
-        return links.copy(29 + flip, step, weights_block(step, flip), to, (w ^ (2 * flip), z))
-
-    def weights_keep(step):
+    def weights_step(turn):
+        return 0 if turn == 3 else direct_at(z, turn)
+
+    def weights_block(turn, flip):
+        if turn == 3:
+            return we_in.at[z, chip ^ flip]
+        return hop.at[weights_step(turn) - 1, chip ^ flip]
+
+    def weights_place(turn, owner):
+        return we_o.at[owner, links.plane(weights_step(turn), -1)]
+
+    def weights_plane(turn, flip):
+        to = (w ^ (2 * flip), z)
+        return links.copy(
+            29 + flip, turn, weights_block(turn, flip), weights_place(turn, w), to
+        )
+
+    def weights_keep(turn):
         return pltpu.make_async_copy(
-            weights_block(step, 0), we_o.at[w, links.plane(step, -1)], load_sems.at[6 + step]
-        )
-
-    def weights_core(step, flip):
-        block = we_o.at[w ^ (2 * flip), links.plane(step, -1)]
+            weights_block(turn, 0), weights_place(turn, w), load_sems.at[6 + turn]
+        )
+
+    def weights_core(turn, flip):
+        block = weights_place(turn, w ^ (2 * flip))
         return links.copy(
-            34 + flip, step, block if flip else weights_block(step, 0), block, (w ^ 1, z)
+            34 + flip, turn, block if flip else weights_block(turn, 0), block, (w ^ 1, z)
         )
 
     def weights_send(step):
         for flip in (3, 1, 2, 0):
             weights_ring(step, flip).start()
 
-    def weights_next(step):
+    def weights_next(turn):
         for flip in (3, 1, 2):
-            if step:
-                weights_ring(step, flip).wait_recv()
-            weights_plane(step, flip).start()
-        if step:
-            weights_ring(step, 0).wait_recv()
-        weights_core(step, 0).start()
-        weights_keep(step).start()
-
-    def weights_end(step):
+            if turn < 3:
+                weights_ring(weights_step(turn), flip).wait_recv()
+            weights_plane(turn, flip).start()
+        if turn < 3:
+            weights_ring(weights_step(turn), 0).wait_recv()
+        weights_core(turn, 0).start()
+        weights_keep(turn).start()
+
+    def weights_end(turn):
         for flip in (1, 2, 3):
-            weights_plane(step, flip).wait_recv()
-            weights_core(step, flip).start()
+            weights_plane(turn, flip).wait_recv()
+            weights_core(turn, flip).start()
 
     def mixed_ring(step):
         to = links.plane(step, 1)
@@ -697,14 +749,13 @@
     def _():
         tok_chain.arrive(2)
         ids_chain.arrive(2)
-        weights_send(1)
-        weights_send(3)
+        send_next(z, weights_send)
 
     wo_chain.arrive(0)
     wo_gather(0).begin()
     wo_gather(3).begin()
     cot_gather(3).begin()
-    weights_next(0)
+    weights_next(3)
     for i in range(PLANES):
         for j in range(PLANES):
             here = (slice(i * rows, (i + 1) * rows), slice(j * rows, (j + 1) * rows))
@@ -769,8 +820,7 @@
 
     @pl.when(jnp.logical_not(end_plane))
     def _():
-        weights_send(1)
-        weights_send(3)
+        send_next(z, weights_send)
 
     def attend(head):
         exact = softmax_rows(mul(qkv_o[0, head], qkv_o[1, head], 1, 1), mask[...])
@@ -786,13 +836,13 @@
     for step in (1, 2, 3):
         mixed_ring(step).start()
     mixed_got[z] = mixed_send[z]
-    weights_send(2)
+    send_beyond(z, weights_send)
     loop(0, 4, lambda turn: wo_gather(turn).relay())
+    weights_next(0)
     loop(0, 4, lambda turn: wo_gather(turn).end())
-    weights_next(1)
     loop(0, 4, lambda turn: cot_gather(turn).relay())
+    weights_end(3)
     weights_end(0)
-    weights_next(3)
     loop(0, 4, lambda turn: wo_gather(turn).settle())
     assemble(wo_blocks, wo_o)
     for step in (1, 2, 3):
@@ -811,10 +861,10 @@
     middle = middle_o[...]
     inverse = lax.rsqrt(jnp.mean(middle * middle, axis=1, keepdims=True) + epsilon)
     second_o[...] = (middle * inverse * gain_two).astype(BF16)
+    loop(0, 4, lambda turn: cot_gather(turn).end())
+    weights_next(1)
+    weights_next(2)
     weights_end(1)
-    loop(0, 4, lambda turn: cot_gather(turn).end())
-    weights_end(3)
-    weights_next(2)
     weights_end(2)
     loop(0, 4, lambda turn: cot_gather(turn).settle())
     for chain in (tok_chain, ids_chain, wo_chain, cot_chain):
@@ -1056,7 +1106,7 @@
     begin(1)
     relay(0)
     begin(2)
-    begin(3)
+    relay(1)
     loads[1].wait()
     loads[2].wait()
 
@@ -1141,9 +1191,13 @@
         across(turn).wait_recv()
         first_half(step)
 
+        @pl.when(turn == 0)
+        def _():
+            begin(3)
+
         @pl.when(turn < 2)
         def _():
-            relay(2 * turn + 1)
+            relay(turn + 2)
 
         @pl.when(turn > 1)
         def _():
@@ -1151,10 +1205,6 @@
 
         second_half(turn, step)
         outs_out(turn).start()
-
-        @pl.when(turn == 0)
-        def _():
-            relay(2)
 
         @pl.when(turn > 0)
         def _():
@@ -1193,14 +1243,14 @@
     def down_chunk(i):
         weight_chunk(cot, scaled, (i - ups) * 256, 256, 2 * hidden, i)
 
-    loop(0, 3, up_chunk)
+    loop(0, 4, up_chunk)
     send_cross(3)
     outs_out(2).wait()
     outs_out(3).wait()
     loop(0, 4, lambda step: (outs_near(step, 1).start(), outs_near(step, 0).start()))
-    loop(3, 5, up_chunk)
+    loop(4, 6, up_chunk)
     send_far(2)
-    loop(5, ups, up_chunk)
+    loop(6, ups, up_chunk)
     loop(ups, ups + downs, down_chunk)
     last = ups + downs
     if hidden % 256:
@@ -1295,12 +1345,12 @@
 
 
 def finish_kernel(
-    outs_in, outs_one_in, grads_in, heads_in, exact_in, mixed_in, qkv_in, first_in, wq_in, cos_in, sin_in,
-    rows_in, attn_in, misc_in, gain_in,
-    sums_o, table_o, first_o, q_o, o_o,
+    outs_in, outs_one_in, grads_in, exact_in, mixed_in, qkv_in, first_in, wq_in, wo_in,
+    cos_in, sin_in, rows_in, sums_in, second_in, middle_in, cot_in, tok_in,
+    output_o, grad_o, table_o, q_o, o_o,
     outs, outs_one, outs_two, outs_far, grads_own, grads_got, heads, exact, mixed, qkv, first, wq,
-    projected, first_part, dense, dense_got, dense_one, dense_two, dense_far, dense_sum,
-    load_sems, send_sems, recv_sems,
+    wo, heads_send, attn, grad_middle, first_got, projected, first_part, dense, dense_got, dense_one,
+    dense_two, dense_far, dense_sum, load_sems, send_sems, recv_sems,
 ):
     links = Links(send_sems, recv_sems)
     w, z = links.w, links.z
@@ -1320,7 +1370,7 @@
 
     def heads_ring(step):
         to = plane_of(step, 1)
-        return remote(37, step, heads_in.at[to], heads.at[z], (w, to))
+        return remote(37, step, heads_send.at[to], heads.at[z], (w, to))
 
     def grads_load(step):
         return pltpu.make_async_copy(
@@ -1340,9 +1390,13 @@
             grads_own.at[0], table_o.at[chip, z, core], load_sems.at[1, 0]
         )
 
-    def grads_gather(step):
+    def grads_gather(turn):
+        step = direct_at(z, turn)
         source = plane_of(step, -1)
-        return Gather(links, 2, step, step, lambda i: table_o.at[i // 2, source, i % 2])
+        half = grads_own.shape[1] // 2
+        return Gather(
+            links, 2, step, turn, lambda i: table_o.at[i // 2, source, i % 2], True, half
+        )
 
     def outs_loads(step):
         _, two = axes(step)
@@ -1440,34 +1494,31 @@
 
     def first_ring(step):
         to = plane_of(step, 1)
-        return remote(38, step, first_part.at[to], first_o.at[z], (w, to))
-
-    def first_keep():
-        return pltpu.make_async_copy(first_part.at[z], first_o.at[z], load_sems.at[1, 3])
+        return remote(38, step, first_part.at[to], first_got.at[step - 1], (w, to))
 
     loads = [
         pltpu.make_async_copy(src, dst, load_sems.at[3 + i // 4, i % 4])
         for i, (src, dst) in enumerate(
             (
-                (heads_in.at[z], heads.at[z]),
+                (wq_in, wq),
+                (wo_in, wo),
                 (exact_in, exact),
                 (mixed_in, mixed),
                 (qkv_in, qkv),
                 (first_in, first),
-                (wq_in, wq),
             )
         )
     ]
+    for load in loads[:2]:
+        load.start()
     for step in steps:
         grads_load(step).start()
     for step in steps:
         for load in outs_loads(step):
             load.start()
-    for load in loads:
+    for load in loads[2:]:
         load.start()
     greet(w, z)
-    for step in (1, 2, 3):
-        heads_ring(step).start()
     for step in steps:
         grads_swap(step).start()
 
@@ -1487,24 +1538,57 @@
         cross(step).start()
 
     keep.wait()
-    grads_gather(0).begin()
+    grads_gather(3).begin()
+    for load in loads[:2]:
+        load.wait()
+
+    lane = lax.broadcasted_iota(jnp.int32, (rows, 128), 1)
+    routed = (lane > 0) & (lane < 16)
+    logits = jnp.where(routed, mul(second_in[...], wq[:, 3 * size :], 1, 0), -1e30)
+    powers = jnp.where(routed, jnp.exp(logits - jnp.max(logits, axis=1, keepdims=True)), 0.0)
+    probs = powers / jnp.sum(powers, axis=1, keepdims=True)
+    high_low = sums_in[:, width:]
+    grad_probs = jnp.where(routed, high_low + pltpu.roll(high_low, 96, 1), 0.0)
+    grad_logits = probs * (grad_probs - jnp.sum(probs * grad_probs, axis=1, keepdims=True))
+    grad_logits = grad_logits.astype(BF16)
+    gains = jnp.transpose(wq[:, 3 * size :].astype(F32))
+    gain_one, gain_two = gains[16:17, :], gains[17:18, :]
+    grad_second = sums_in[:, :width] + mul(grad_logits, wq[:, 3 * size :], 1, 1)
+    middle = middle_in[...]
+    inverse = lax.rsqrt(jnp.mean(middle * middle, axis=1, keepdims=True) + epsilon)
+    normed = middle * inverse
+    grad_normed = grad_second * gain_two
+    grad_here = cot_in[...].astype(F32) + inverse * (
+        grad_normed - normed * jnp.mean(grad_normed * normed, axis=1, keepdims=True)
+    )
+    grad_middle[...] = grad_here
+    attn[...] = grad_here.astype(BF16)
+    gain_two_row = jnp.sum(grad_second * normed, axis=0, keepdims=True)
+    router_part = mul(second_in[...], grad_logits, 0, 0)
+    for plane, begin in enumerate(STARTS):
+        grad_mixed = mul(
+            attn[...], wo[begin * HEAD_DIM : begin * HEAD_DIM + size, :], 1, 1
+        )
+        heads_send[plane] = grad_mixed.astype(BF16)
+    for step in (1, 2, 3):
+        heads_ring(step).start()
+    heads[z] = heads_send[z]
     loop(1, 4, grads_ready)
     loop(0, 4, outs_cross)
     for step in (1, 2, 3):
         heads_ring(step).wait_recv()
-    grads_ring(1).start()
-    grads_ring(3).start()
+    send_next(z, lambda step: grads_ring(step).start())
 
     def out_weight(i):
         side = i // (half // 128)
         low = at((i - side * (half // 128)) * 128, 128)
-        total = mul(rows_in[...], attn_in[:, at(i * 128, 128)], 0, 0).astype(BF16)
+        total = mul(rows_in[...], attn[:, at(i * 128, 128)], 0, 0).astype(BF16)
         dense[side ^ core, 1, :, :, low] = total.reshape(PLANES, plane_rows, 128)
 
     loop(0, width // 128, out_weight)
     for step in steps:
         dense_swap(1, step).start()
-    for load in loads:
+    for load in loads[2:]:
         load.wait()
 
     def head_back(head):
@@ -1531,11 +1615,11 @@
 
     loop(0, WINDOW, head_back)
 
-    def grads_next(step):
-        grads_ring(step).wait_recv()
-        grads_gather(step).begin()
-
-    grads_gather(0).relay()
+    def grads_next(turn):
+        grads_ring(direct_at(z, turn)).wait_recv()
+        grads_gather(turn).begin()
+
+    grads_gather(3).relay()
 
     def qkv_weight(i):
         side = i // (half // 128)
@@ -1551,20 +1635,16 @@
         first_part[:, :, here] = total.astype(BF16).reshape(PLANES, rows, 256)
         scaled = total * first[:, :, here].reshape(PLANES * rows, 256).astype(F32)
         gain_parts.append(jnp.sum(scaled, axis=0, keepdims=True))
-    gain_row = jnp.concatenate(gain_parts, axis=1) / gain_in[0:1, :]
-    gain_columns = jnp.transpose(jnp.broadcast_to(gain_row, (128, width)))
-    lane = lax.broadcasted_iota(jnp.int32, gain_columns.shape, 1)
-    misc = jnp.where(lane == 15, gain_columns, misc_in[...])
+    gain_one_row = jnp.concatenate(gain_parts, axis=1) / gain_one
+    kind = lax.broadcasted_iota(jnp.int32, (128, width), 0)
+    gain_rows = jnp.where(kind == 16, gain_one_row, jnp.where(kind == 17, gain_two_row, 0.0))
+    misc = jnp.transpose(gain_rows) + router_part
     dense[1 ^ core, 0, :, :, half - 128 :] = misc.astype(BF16).reshape(PLANES, plane_rows, 128)
     for step in steps:
         dense_swap(0, step).start()
 
-    keep_first = first_keep()
-    keep_first.start()
-    for step in (1, 2, 3):
-        first_ring(step).start()
-    grads_ring(2).start()
-    loop(1, 2, grads_next)
+    loop(0, 1, grads_next)
+    send_beyond(z, lambda step: grads_ring(step).start())
 
     def dense_ready(step):
         for kind in (0, 1):
@@ -1581,14 +1661,8 @@
         block = outs.at[step, 0]
         add_blocks(block, block, outs_one.at[step, 0], outs_two.at[step])
 
-        @pl.when(step > 0)
-        def _():
-            far(step).start()
-
     loop(0, 4, outs_finish)
-    grads_gather(0).end()
-    loop(3, 4, grads_next)
-    grads_gather(1).relay()
+    grads_gather(0).relay()
 
     def dense_cross_start(step):
         for kind in (0, 1):
@@ -1599,8 +1673,8 @@
             dense_cross(kind, step).start()
 
     loop(0, 4, dense_cross_start)
-    grads_gather(1).end()
-    grads_gather(3).relay()
+    loop(1, 3, grads_next)
+    loop(1, 4, lambda step: far(step).start())
 
     def dense_finish(step):
         for kind in (0, 1):
@@ -1615,12 +1689,14 @@
             dense_ring(1, step).start()
 
     loop(0, 4, dense_finish)
+    loop(1, 4, lambda step: first_ring(step).start())
     keep = dense_keep()
     keep.start()
+    grads_gather(3).end()
+    grads_gather(0).end()
+    grads_gather(1).relay()
     keep.wait()
     q_gather(0).begin()
-    loop(2, 3, grads_next)
-    grads_gather(3).end()
 
     def q_next(step):
         dense_ring(0, step).wait_recv()
@@ -1636,17 +1712,39 @@
     keep.wait()
     o_gather().begin()
     grads_gather(2).relay()
+    grads_gather(1).end()
     loop(0, 4, lambda step: q_gather(step).relay())
     o_gather().relay()
     loop(1, 4, lambda step: far(step).wait_recv())
-    add_blocks(sums_o, outs.at[0, 0], outs_far.at[0], outs_far.at[1], outs_far.at[2])
-    grads_gather(2).end()
+
+    def output_rows(i):
+        here = pl.ds(pl.multiple_of(i * 16, 16), 16)
+        total = middle_in[here, :] + outs[0, 0, here, :].astype(F32)
+        for step in range(3):
+            total = total + outs_far[step, here, :].astype(F32)
+        output_o[here, :] = total.astype(BF16)
+
+    loop(0, rows // 16, output_rows)
+    for step in (1, 2, 3):
+        first_ring(step).wait_recv()
+    grad_first = first_part[z].astype(F32)
+    for step in range(3):
+        grad_first = grad_first + first_got[step].astype(F32)
+    tokens = tok_in[...].astype(F32)
+    inverse = lax.rsqrt(jnp.mean(tokens * tokens, axis=1, keepdims=True) + epsilon)
+    normed = tokens * inverse
+    grad_normed = grad_first * gain_one
+    grad_o[...] = (
+        grad_middle[...]
+        + inverse
+        * (grad_normed - normed * jnp.mean(grad_normed * normed, axis=1, keepdims=True))
+    ).astype(BF16)
     loop(0, 4, lambda step: q_gather(step).end())
     o_gather().end()
-    loop(0, 4, lambda step: grads_gather(step).settle())
+    grads_gather(2).end()
+    loop(0, 4, lambda turn: grads_gather(turn).settle())
     loop(0, 4, lambda step: q_gather(step).settle())
     o_gather().settle()
-    keep_first.wait()
 
     def settle(step):
         grads_swap(step).wait_send()
@@ -1660,7 +1758,6 @@
     loop(0, 4, settle)
 
     def settle_rings(step):
-        first_ring(step).wait_recv()
         first_ring(step).wait_send()
         heads_ring(step).wait_send()
         grads_ring(step).wait_send()
@@ -1671,27 +1768,27 @@
     loop(1, 4, settle_rings)
 
 
-def finish(
-    outs, outs_one, grads, heads, exact, mixed, qkv, first, wq, tables, rows_attn, misc, gain, collective
-):
+def finish(outs, outs_one, grads, saved, tables, at_rows, collective):
+    exact, mixed, qkv, first, wq, wo = saved
     rows, width = first.shape[1:]
     seqlen = PLANES * rows
     size = WINDOW * HEAD_DIM
     plane_rows = width // PLANES
     block = (plane_rows // 4, width // 2)
+    heads = (PLANES, rows, size)
     any_spec = pl.BlockSpec(memory_space=pl.ANY)
     vmem_spec = pl.BlockSpec(memory_space=pltpu.VMEM)
     return pl.pallas_call(
         finish_kernel,
         out_shape=[
-            jax.ShapeDtypeStruct((rows, width), F32),
+            jax.ShapeDtypeStruct((rows, width), BF16),
+            jax.ShapeDtypeStruct((rows, width), BF16),
             jax.ShapeDtypeStruct((4, PLANES) + grads.shape[1:], BF16),
-            jax.ShapeDtypeStruct(first.shape, BF16),
             jax.ShapeDtypeStruct((PLANES, plane_rows, width), BF16),
             jax.ShapeDtypeStruct((plane_rows, width), BF16),
         ],
-        in_specs=[any_spec] * 9 + [vmem_spec] * 6,
-        out_specs=[vmem_spec] + [any_spec] * 4,
+        in_specs=[any_spec] * 9 + [vmem_spec] * 8,
+        out_specs=[vmem_spec] * 2 + [any_spec] * 3,
         scratch_shapes=[
             pltpu.VMEM((4, 2, rows, width), BF16),
             pltpu.VMEM((4, 2, rows, width), BF16),
@@ -1699,12 +1796,17 @@
             pltpu.VMEM((3, rows, width), BF16),
             pltpu.VMEM((4,) + grads.shape[2:], BF16),
             pltpu.VMEM((4,) + grads.shape[2:], BF16),
-            pltpu.VMEM(heads.shape, BF16),
+            pltpu.VMEM(heads, BF16),
             pltpu.VMEM(exact.shape, F32),
             pltpu.VMEM(mixed.shape, F32),
             pltpu.VMEM(qkv.shape, BF16),
             pltpu.VMEM(first.shape, BF16),
             pltpu.VMEM(wq.shape, BF16),
+            pltpu.VMEM(wo.shape, BF16),
+            pltpu.VMEM(heads, BF16),
+            pltpu.VMEM((rows, width), BF16),
+            pltpu.VMEM((rows, width), F32),
+            pltpu.VMEM((3, rows, width), BF16),
             pltpu.VMEM((seqlen, 3 * size), BF16),
             pltpu.VMEM(first.shape, BF16),
             pltpu.VMEM((2, 2, PLANES, plane_rows, width // 2), BF16),
@@ -1721,39 +1823,61 @@
             collective_id=collective, has_side_effects=True, vmem_limit_bytes=62 * 2**20
         ),
         name="finish",
-    )(outs, outs_one, grads, heads, exact, mixed, qkv, first, wq, *tables, *rows_attn, misc, gain)
-
-
-def widen_kernel(table, up_o, down_o):
+    )(outs, outs_one, grads, *saved, *tables, *at_rows)
+
+
+def widen_kernel(table, q, o, up_o, down_o, qkv_o, out_o, misc_o):
     columns = table.shape[2]
     split = up_o.shape[2]
+    size = WINDOW * HEAD_DIM
     for low in range(0, columns, 128):
         part = jnp.swapaxes(table[:, :, low : low + 128].astype(F32), 0, 1)
         if low < split:
             up_o[:, :, low : low + 128] = part
         else:
             down_o[:, :, low - split : low - split + 128] = part
-
-
-def widen(table):
+    out_o[...] = o[...].astype(F32)
+    column = 0
+    for kind in range(3):
+        for plane, (a, b) in enumerate(KEEP):
+            span = (b - a) * HEAD_DIM
+            begin = kind * size + a * HEAD_DIM
+            qkv_o[:, column : column + span] = q[plane, :, begin : begin + span].astype(F32)
+            column += span
+    total = q[0, :, 3 * size :].astype(F32)
+    for plane in range(1, PLANES):
+        total = total + q[plane, :, 3 * size :].astype(F32)
+    misc_o[...] = total
+
+
+def widen(table, q, o):
     experts, rows, columns = table.shape
+    width = o.shape[1]
     split = columns // 3 * 2
     step = rows // 4
+    shapes = [
+        (rows, experts, split),
+        (rows, experts, columns - split),
+        (rows, 3 * width),
+        (rows, width),
+        (rows, 128),
+    ]
     return pl.pallas_call(
         widen_kernel,
         grid=(rows // step,),
-        out_shape=[
-            jax.ShapeDtypeStruct((rows, experts, split), F32),
-            jax.ShapeDtypeStruct((rows, experts, columns - split), F32),
+        out_shape=[jax.ShapeDtypeStruct(shape, F32) for shape in shapes],
+        in_specs=[
+            pl.BlockSpec((experts, step, columns), lambda i: (0, i, 0)),
+            pl.BlockSpec((PLANES, step, width), lambda i: (0, i, 0)),
+            pl.BlockSpec((step, width), lambda i: (i, 0)),
         ],
-        in_specs=[pl.BlockSpec((experts, step, columns), lambda i: (0, i, 0))],
         out_specs=[
-            pl.BlockSpec((step, experts, split), lambda i: (i, 0, 0)),
-            pl.BlockSpec((step, experts, columns - split), lambda i: (i, 0, 0)),
+            pl.BlockSpec((step,) + shape[1:], lambda i, n=len(shape): (i,) + (0,) * (n - 1))
+            for shape in shapes
         ],
-        compiler_params=pltpu.CompilerParams(vmem_limit_bytes=60 * 2**20),
+        compiler_params=pltpu.CompilerParams(vmem_limit_bytes=62 * 2**20),
         name="widen",
-    )(table)
+    )(table, q, o)
 
 
 def windows(x):
@@ -1817,84 +1941,29 @@
     we_all, cot_all, wq_all, out_weight, first_in, qkv, weights_exact, mixed_exact, mixed, middle, second_in = start(
         tokens, ids_send, wq_send, w_out, we_send, cot_send, cosine[:, 0, :], sine_signed, 1
     )
-    misc_all = wq_all[:, 3 * size :]
-    router = misc_all[:, 1 : experts + 1]
-    gain_one = misc_all[:, experts + 1].astype(F32)
-    gain_two = misc_all[:, experts + 2].astype(F32)
-    inverse_two = rms_inverse(middle)
-    normed_two = middle * inverse_two
-
     weights = we_all.reshape(width, 3 * FF)
     grads, outs, outs_one, sums = run_experts(second_in, cot_all, weights, wq_all, 3)
 
-    hi = sums[:, width + 1 : width + 1 + experts]
-    lo = sums[:, width + 33 : width + 33 + experts]
-    grad_probs = hi + lo
-    probs = jax.nn.softmax(dot(second_in, router, ((1,), (0,))), axis=-1)
-    grad_logits = (
-        probs * (grad_probs - jnp.sum(probs * grad_probs, axis=1, keepdims=True))
-    ).astype(BF16)
-    grad_second = sums[:, :width] + dot(grad_logits, router, ((1,), (1,)))
-    grad_output = cotangent.astype(F32)
-    grad_normed_two = grad_second * gain_two
-    gain_two_part = jnp.sum(grad_second * normed_two, axis=0)
-    grad_middle = grad_output + inverse_two * (
-        grad_normed_two
-        - normed_two * jnp.mean(grad_normed_two * normed_two, axis=-1, keepdims=True)
-    )
-    router_part = dot(second_in, grad_logits, ((0,), (0,)))
-    grad_attention = grad_middle.astype(BF16)
-    grad_mixed = dot(grad_attention, out_weight, ((1,), (1,)), BF16)
-    misc_part = jnp.concatenate(
-        [
-            router_part,
-            jnp.zeros((width, 1), F32),
-            gain_two_part[:, None],
-            jnp.zeros((width, 128 - experts - 2), F32),
-        ],
-        axis=1,
-    )
-    sums, table, first_all, q_all, o_all = finish(
+    output, grad_tokens, table, q_all, o_all = finish(
         outs,
         outs_one,
         grads.reshape(PLANES, 2, width // PLANES // 2, 3 * FF),
-        windows(grad_mixed),
-        weights_exact,
-        mixed_exact,
-        qkv,
-        first_in,
-        wq_all,
+        (weights_exact, mixed_exact, qkv, first_in, wq_all, out_weight),
         (cosine[:, 0, :], sine_signed),
-        (mixed, grad_attention),
-        misc_part,
-        jnp.broadcast_to(gain_one[None, :], (8, width)),
+        (mixed, sums, second_in, middle, cotangent, tokens),
         6,
     )
-    output = (middle + sums).astype(BF16)
-    grad_first = jnp.sum(first_all.astype(F32), axis=0)
-    inputs = tokens.astype(F32)
-    inverse_one = rms_inverse(inputs)
-    normed_one = inputs * inverse_one
-    grad_normed_one = grad_first * gain_one
-    grad_tokens = grad_middle + inverse_one * (
-        grad_normed_one
-        - normed_one * jnp.mean(grad_normed_one * normed_one, axis=-1, keepdims=True)
-    )
-    out_sum = o_all.astype(F32)
-    qkv_sum = jnp.concatenate(
-        [from_windows(q_all[:, :, i * size : (i + 1) * size]) for i in range(3)], axis=1
-    ).astype(F32)
-    misc_sum = jnp.sum(q_all[:, :, 3 * size :].astype(F32), axis=0)
-
-    up_sum, down_sum = widen(table.reshape(experts + 1, width // PLANES, 3 * FF))
+    up_sum, down_sum, qkv_sum, out_sum, misc_sum = widen(
+        table.reshape(experts + 1, width // PLANES, 3 * FF), q_all, o_all
+    )
     return (
         output,
-        grad_tokens.astype(BF16),
-        misc_sum[:, experts],
+        grad_tokens,
+        misc_sum[:, experts + 1],
         qkv_sum,
         out_sum,
-        misc_sum[:, experts + 1],
-        misc_sum[:, :experts],
+        misc_sum[:, experts + 2],
+        misc_sum[:, 1 : experts + 1],
         up_sum,
         down_sum,
     )

time: 577 us -> 539 us (0.934)
  Pallas kernels: 534 us -> 515 us
  other arithmetic: 20.6 us -> 5.44 us
  matrix products: 5.94 us -> 0 us
    pallas_call x1, Pallas kernels: 210 us -> 200 us  [finish(): pl.pallas_call(finish_kernel, out_shape=[jax.ShapeDtypeStruct((rows, widt...]
    pallas_call x1, Pallas kernels: 167 us -> 158 us  [start(): pl.pallas_call(start_kernel, out_shape=[jax.ShapeDtypeStruct(shape, kind)...]
    convert_element_type x5 -> x0, other arithmetic: 6.85 us -> none  [the longest x1 2.57 us: expert_local(): qkv_sum = jnp.concatenate([from_windows(q_all[:, :, i * size:(i + 1) * si...]
    reduce_sum x7 -> x0, other arithmetic: 6.61 us -> none  [the longest x2 2.33 us: rms_inverse(): jnp.mean(values * values, axis=-1, keepdims=True) + epsilon]
    dot_general x4 -> x0, matrix products: 5.94 us -> none  [dot(): lax.dot_general(a, b, ((dims[0], dims[1]), ((), ())), preferred_element_t...]
where the time goes in v5:
time: 539 us; the launch traced here: 535 us
  Pallas kernels  515 us (96%)
  local copies, waits for them, and re-layouts  13.9 us (3%)
  other arithmetic  5.44 us (1%)
    pallas_call x1, Pallas kernels, finish(): pl.pallas_call(finish_kernel, out_shape=[jax.ShapeDtypeStruct((rows, widt...  200 us
    pallas_call x1, Pallas kernels, start(): pl.pallas_call(start_kernel, out_shape=[jax.ShapeDtypeStruct(shape, kind)...  158 us
    pallas_call x1, Pallas kernels, run_experts(): pl.pallas_call(experts_kernel, out_shape=[jax.ShapeDtypeStruct((width, 3...  128 us
    pallas_call x1, Pallas kernels, widen(): pl.pallas_call(widen_kernel, grid=(rows // step,), out_shape=[jax.ShapeDt...  29.1 us

profile of v5, /device:TPU:29, one launch (start us, length us, event | category | flops | bytes accessed | tf_op | source)
XLA Modules:
  0.0 535.0 jit_solution(8185376299695001905)
XLA Ops:
  0.6 0.0 copy-start.1
  0.7 0.0 copy-start
  0.7 0.8 convert_element_type.6
  1.5 0.9 fusion.2
  2.4 0.8 copy.34
  3.2 0.8 copy.35
  3.9 0.8 copy.33
  4.7 0.1 concatenate.22
  4.8 0.1 copy.39
  5.0 0.7 pad_maximum_fusion.3.ids_in
  5.7 0.6 broadcast_in_dim.56
  6.3 1.8 concatenate.25.cot_in
  8.1 1.0 slice_bitcast_fusion.11
  9.1 0.8 pad_maximum_fusion.1.wq_in
  9.9 1.0 fusion
  10.9 1.0 pad_maximum_fusion.2
  11.9 0.0 copy-done.1
  11.9 0.2 copy.37
  12.1 0.0 copy-done
  12.1 0.7 copy.36
  12.8 0.2 pad_maximum_fusion
  13.0 2.0 copy.42
  15.0 158.4 %start.1 = (bf16[8,4,40,2688]{3,2,1,0:T(8,128)(2,1)}, bf16[4,4,128,1408]{3,2,1,0:T(8,128)(2,1)}, bf16[1280,1280]{1,0:T(8,128)(2,1)}, bf16[1280,1280]{1,0:T(8,128...) custom-call(bf16[128,1280]{1,0:T(8,128)(2,1)} %tok_in.3, ...), custom_call_target="tpu_custom_call" | custom-call | tf_op jit(solution)/shard_map/start/pallas_call | solution.py:913
  173.4 127.5 %experts.1 = (bf16[1280,2688]{1,0:T(8,128)(2,1)}, bf16[4,4,128,1280]{3,2,1,0:T(8,128)(2,1)}, bf16[4,2,128,1280]{3,2,1,0:T(8,128)(2,1)}, f32[128,1408]{1,0:T(8,128)}) custom-call(bf16[128,1280]{1,0:T(8,128)(2,1)} %get-tuple-element.34.x_in.second_in, bf16[4,4,128,1408]{3,2,1,0:T(8,128)(2,1)} %get-tuple-element.35.cot_in, bf16[1280,2688]{1,0:T(8,128)(2,1)} %bitcast.36, ...), custom_call_target="tpu_custom_call" | custom-call | tf_op jit(solution)/shard_map/experts/pallas_call | solution.py:1306
  301.0 199.8 %finish.1 = (bf16[128,1280]{1,0:T(8,128)(2,1)}, bf16[128,1280]{1,0:T(8,128)(2,1)}, bf16[4,4,2,160,2688]{4,3,2,1,0:T(8,128)(2,1)}, bf16[4,320,1280]{2,1,0:T(8,128)(2,1)}, bf16[320,1280]{1,0:T(8,128)(2,1)}) custom-call(bf16[4,4,128,1280]{3,2,1,0:T(8,128)(2,1)} %get-tuple-element.38.outs_in, bf16[4,2,128,1280]{3,2,1,0:T(8,128)(2,1)} %get-tuple-element.39.outs_one_in, ...), custom_call_target="tpu_custom_call" | custom-call | tf_op jit(solution)/shard_map/finish/pallas_call | solution.py:1781
  500.8 0.0 copy-start.3
  500.8 0.0 copy-start.2
  500.8 29.1 %widen.1 = (f32[320,16,1792]{2,1,0:T(8,128)}, f32[320,16,896]{2,1,0:T(8,128)}, f32[320,3840]{1,0:T(8,128)}, f32[320,1280]{1,0:T(8,128)}, f32[320,128]{1,0:T(8,128)}) custom-call(bf16[16,320,2688]{2,1,0:T(8,128)(2,1)} %bitcast.33, bf16[4,320,1280]{2,1,0:T(8,128)(2,1)} %get-tuple-element.52.q, bf16[320,1280]{1,0:T(8,128)(2,1)} %get-tuple-element.53.o), custom_call_target="tpu_custom_call" | custom-call | tf_op jit(solution)/shard_map/widen/pallas_call | solution.py:1865
  529.9 1.9 slice_reduce_fusion
  531.8 1.0 slice.74
  532.8 0.7 copy.40
  533.5 0.0 copy-done.3
  533.5 0.7 copy.45
  534.2 0.0 copy-done.2
  534.2 0.7 copy.46
  (9 shorter events, 0.1 us)
Async XLA Ops:
  0.6 11.2 %copy-start.1 = (bf16[40,16,896]{2,1,0:T(8,128)(2,1)S(1)}, bf16[40,16,896]{2,1,0:T(8,128)(2,1)}, u32[]{:S(2)}) copy-start(bf16[40,16,896]{2,1,0:T(8,128)(2,1)} %param.21) | copy-start | bytes 3440644
  0.7 11.4 %copy-start = (bf16[40,16,1792]{2,1,0:T(8,128)(2,1)S(1)}, bf16[40,16,1792]{2,1,0:T(8,128)(2,1)}, u32[]{:S(2)}) copy-start(bf16[40,16,1792]{2,1,0:T(8,128)(2,1)} %param.20) | copy-start | bytes 6881284
  500.8 32.7 %copy-start.3 = (bf16[128,1280]{1,0:T(8,128)(2,1)S(1)}, bf16[128,1280]{1,0:T(8,128)(2,1)}, u32[]{:S(2)}) copy-start(bf16[128,1280]{1,0:T(8,128)(2,1)} %get-tuple-element.113) | copy-start | bytes 983044
  500.8 33.4 %copy-start.2 = (bf16[128,1280]{1,0:T(8,128)(2,1)S(1)}, bf16[128,1280]{1,0:T(8,128)(2,1)}, u32[]{:S(2)}) copy-start(bf16[128,1280]{1,0:T(8,128)(2,1)} %get-tuple-element.114) | copy-start | bytes 983044

commit v6 on v5

--- a/solution.py
+++ b/solution.py
@@ -1,5 +1,6 @@
 import jax
 import jax.numpy as jnp
+import numpy as np
 from jax import lax
 from jax.experimental import pallas as pl
 from jax.experimental.pallas import tpu as pltpu
@@ -612,10 +613,12 @@
 
 
 def start_kernel(
-    tok_in, ids_in, wq_in, wo_in, we_in, cot_in, cos_in, sin_in,
-    we_o, cot_o, wq_o, wo_o, first_o, qkv_o, exact_o, mixed_o, mixed_rows_o, middle_o, second_o, hop,
-    tok, ids, wq_blocks, wo_blocks, staged, mask, mixed_got, mixed_send,
-    load_sems, send_sems, recv_sems,
+    tok_in, wq_in, wo_in, seq_in, routes_in, misc_in, up_in, down_in, cot_in, cos_in, sin_in,
+    we_o, cot_o, wq_out, wo_out, first_out, qkv_out, exact_out, mixed_out, mixed_rows_o, middle_o,
+    second_o, hop,
+    tok, ids, wq_blocks, wo_blocks, staged, mask, mixed_got, mixed_send, ids_in, we_in, cot_full,
+    wq_o, wo_o, first_o, qkv_o, exact_o, mixed_o,
+    load_sems, out_sems, send_sems, recv_sems,
 ):
     links = Links(send_sems, recv_sems)
     w, z = links.w, links.z
@@ -629,25 +632,49 @@
         for i, (src, dst) in enumerate(
             (
                 (tok_in, tok.at[z]),
-                (ids_in, ids.at[z]),
-                (wq_in.at[z], wq_blocks.at[w, z]),
                 (wo_in, wo_blocks.at[w, z]),
-                (cot_in, cot_o.at[chip, z]),
+                (cot_full, cot_o.at[chip, z]),
             )
         )
     ]
-    for keep in keeps:
+    for keep in keeps[:2]:
         keep.start()
+    window_starts = [jnp.int32(0)] * 4
+    for plane, begin in enumerate(STARTS):
+        for step in range(4):
+            window_starts[step] = jnp.where(
+                lax.rem(z + step, PLANES) == plane, begin, window_starts[step]
+            )
+
+    def window(step, kind):
+        return wq_in.at[:, at(kind * width + window_starts[step] * HEAD_DIM, size)]
+
+    def wq_own(kind):
+        return pltpu.make_async_copy(
+            window(0, kind),
+            wq_blocks.at[w, z, :, pl.ds(kind * size, size)],
+            load_sems.at[3 + kind],
+        )
+
+    for kind in range(3):
+        wq_own(kind).start()
+    wq_blocks[w, z, :, 3 * size :] = misc_in[...]
+    row_ids = jnp.broadcast_to(seq_in[...].astype(F32), (rows, rows))
+    ids_in[:rows, :] = row_ids.astype(BF16)
+    ids_in[rows:, :] = jnp.transpose(row_ids).astype(BF16)
+    ids[z] = ids_in[...]
     greet(w, z)
 
     tok_chain = Chain(links, 0, tok_in, lambda p: tok.at[p])
     ids_chain = Chain(links, 2, ids_in, lambda p: ids.at[p])
     wo_chain = Chain(links, 4, wo_in, lambda p: wo_blocks.at[w, p])
-    cot_chain = Chain(links, 6, cot_in, lambda p: cot_o.at[chip, p])
-
-    def wq_ring(step):
+    cot_chain = Chain(links, 6, cot_full, lambda p: cot_o.at[chip, p])
+
+    def wq_ring(step, kind):
         to = links.plane(step, 1)
-        return links.copy(8, step, wq_in.at[to], wq_blocks.at[w, z], (w, to))
+        here = wq_blocks.at[w, z, :, pl.ds(kind * size, size if kind < 3 else 128)]
+        src = window(step, kind) if kind < 3 else misc_in
+        return links.copy(39 + kind if kind else 8, step, src, here, (w, to))
 
     def wq_gather(step):
         source = links.plane(step, -1)
@@ -723,19 +750,38 @@
     tok_chain.begin()
     ids_chain.begin()
     for step in (1, 2, 3):
-        wq_ring(step).start()
-    for keep in keeps:
+        for kind in range(4):
+            wq_ring(step, kind).start()
+    for kind in range(3):
+        wq_own(kind).wait()
+    wq_gather(0).begin()
+    for keep in keeps[:2]:
         keep.wait()
-    wq_gather(0).begin()
+
+    lane = lax.broadcasted_iota(jnp.int32, (rows, 128), 1)
+    member = lane == 0
+    for route in range(routes_in.shape[1]):
+        member = member | (lane == routes_in[:, route : route + 1] + 1)
+    cot_full[:, :width] = cot_in[...]
+    cot_full[:, width:] = member.astype(F32).astype(BF16)
+    keeps[2].start()
     tok_chain.arrive(0)
     ids_chain.arrive(0)
     for step in (1, 2, 3):
-        wq_ring(step).wait_recv()
+        for kind in range(4):
+            wq_ring(step, kind).wait_recv()
         wq_gather(step).begin()
     wo_chain.begin()
     tok_chain.arrive(1)
     ids_chain.arrive(1)
     cot_chain.begin()
+
+    def experts_first(source, low):
+        for i in range(0, source.shape[2], 128):
+            part = jnp.swapaxes(source[:, :, i : i + 128].astype(F32), 0, 1).astype(BF16)
+            for expert in range(source.shape[1]):
+                we_in[expert % PLANES, expert // PLANES, :, low + i : low + i + 128] = part[expert]
+
     end_plane = (z == 0) | (z == PLANES - 1)
 
     @pl.when(jnp.logical_not(end_plane))
@@ -744,6 +790,8 @@
         ids_chain.arrive(2)
 
     loop(0, 4, lambda step: wq_gather(step).relay())
+    experts_first(up_in, 0)
+    experts_first(down_in, up_in.shape[2])
 
     @pl.when(end_plane)
     def _():
@@ -754,6 +802,7 @@
     wo_chain.arrive(0)
     wo_gather(0).begin()
     wo_gather(3).begin()
+    keeps[2].wait()
     cot_gather(3).begin()
     weights_next(3)
     for i in range(PLANES):
@@ -783,7 +832,21 @@
 
     cot_chain.arrive(0)
     cot_gather(0).begin()
+    outputs = [
+        pltpu.make_async_copy(src, dst, out_sems.at[i])
+        for i, (src, dst) in enumerate(
+            (
+                (wq_o, wq_out),
+                (first_o, first_out),
+                (qkv_o, qkv_out),
+                (exact_o, exact_out),
+                (mixed_o, mixed_out),
+                (wo_o, wo_out),
+            )
+        )
+    ]
     assemble(wq_blocks, wq_o)
+    outputs[0].start()
     gains = jnp.transpose(wq_o[:, size * 3 :].astype(F32))
     gain_one = gains[16:17, :]
     gain_two = gains[17:18, :]
@@ -794,6 +857,7 @@
         first_o[p] = (block * inverse * gain_one).astype(BF16)
 
     loop(0, PLANES, normalise)
+    outputs[1].start()
     wo_chain.arrive(1)
     wo_gather(1).begin()
     cot_chain.arrive(1)
@@ -813,6 +877,7 @@
                 qkv_o[kind, head, span, :] = here.astype(BF16)
 
     loop(0, PLANES, project)
+    outputs[2].start()
     wo_chain.arrive(2)
     wo_gather(2).begin()
     cot_chain.arrive(2)
@@ -828,6 +893,8 @@
         mixed_o[head] = mul(exact.astype(BF16), qkv_o[2, head], 1, 0)
 
     loop(0, WINDOW, attend)
+    outputs[3].start()
+    outputs[4].start()
     for p in range(PLANES):
         for head in range(WINDOW):
             mixed_send[p, :, head * HEAD_DIM : (head + 1) * HEAD_DIM] = mixed_o[
@@ -845,6 +912,7 @@
     weights_end(0)
     loop(0, 4, lambda turn: wo_gather(turn).settle())
     assemble(wo_blocks, wo_o)
+    outputs[5].start()
     for step in (1, 2, 3):
         mixed_ring(step).wait_recv()
     column = 0
@@ -867,6 +935,8 @@
     weights_end(1)
     weights_end(2)
     loop(0, 4, lambda turn: cot_gather(turn).settle())
+    for output in outputs:
+        output.wait()
     for chain in (tok_chain, ids_chain, wo_chain, cot_chain):
         chain.settle()
     for step in (0, 1, 2, 3):
@@ -879,7 +949,8 @@
             weights_core(step, flip).wait_send()
             weights_core(step, flip).wait_recv()
         if step:
-            wq_ring(step).wait_send()
+            for kind in range(4):
+                wq_ring(step, kind).wait_send()
             mixed_ring(step).wait_send()
 
 
@@ -887,52 +958,61 @@
     return tok[z, :, here].astype(F32)
 
 
-def start(tok, ids, wq, wo, we, cot, cosine, sine, collective):
+def start(tok, wq, wo, seq, routes, misc, up, down, cot, tables, collective):
     rows, width = tok.shape
     own = wo.shape[0]
-    hidden3 = we.shape[-1]
+    experts = up.shape[1]
+    hidden3 = up.shape[2] + down.shape[2]
     seqlen = PLANES * rows
     size = WINDOW * HEAD_DIM
     blocks = (8, PLANES, own, width)
-    any_out = pl.BlockSpec(memory_space=pl.ANY)
-    vmem_out = pl.BlockSpec(memory_space=pltpu.VMEM)
+    any_spec = pl.BlockSpec(memory_space=pl.ANY)
+    vmem_spec = pl.BlockSpec(memory_space=pltpu.VMEM)
+    kept = [
+        ((width, width), BF16),
+        ((width, width), BF16),
+        ((PLANES, rows, width), BF16),
+        ((3, WINDOW, seqlen, HEAD_DIM), BF16),
+        ((WINDOW, seqlen, seqlen), F32),
+        ((WINDOW, seqlen, HEAD_DIM), F32),
+    ]
     shapes = [
-        ((8, PLANES, own, hidden3), BF16, any_out),
-        ((4, PLANES) + cot.shape, BF16, any_out),
-        ((width, width), BF16, vmem_out),
-        ((width, width), BF16, vmem_out),
-        ((PLANES, rows, width), BF16, vmem_out),
-        ((3, WINDOW, seqlen, HEAD_DIM), BF16, vmem_out),
-        ((WINDOW, seqlen, seqlen), F32, vmem_out),
-        ((WINDOW, seqlen, HEAD_DIM), F32, vmem_out),
-        ((rows, width), BF16, vmem_out),
-        ((rows, width), F32, vmem_out),
-        ((rows, width), BF16, vmem_out),
-        ((3, 4, own, hidden3), BF16, any_out),
+        ((8, PLANES, own, hidden3), BF16),
+        ((4, PLANES, rows, width + 128), BF16),
+        *kept,
+        ((rows, width), BF16),
+        ((rows, width), F32),
+        ((rows, width), BF16),
+        ((3, 4, own, hidden3), BF16),
     ]
     return pl.pallas_call(
         start_kernel,
-        out_shape=[jax.ShapeDtypeStruct(shape, kind) for shape, kind, _ in shapes],
-        in_specs=[any_out] * 6 + [vmem_out] * 2,
-        out_specs=[spec for _, _, spec in shapes],
+        out_shape=[jax.ShapeDtypeStruct(shape, kind) for shape, kind in shapes],
+        in_specs=[any_spec] * 3 + [vmem_spec] * 8,
+        out_specs=[any_spec] * 8 + [vmem_spec] * 3 + [any_spec],
         scratch_shapes=[
             pltpu.VMEM((PLANES, rows, width), BF16),
-            pltpu.VMEM((PLANES,) + ids.shape, BF16),
+            pltpu.VMEM((PLANES, 2 * rows, rows), BF16),
             pltpu.VMEM(blocks, BF16),
             pltpu.VMEM(blocks, BF16),
             pltpu.VMEM((PLANES * own, width), F32),
             pltpu.VMEM((seqlen, seqlen), F32),
             pltpu.VMEM((PLANES, rows, size), BF16),
             pltpu.VMEM((PLANES, rows, size), BF16),
+            pltpu.VMEM((2 * rows, rows), BF16),
+            pltpu.VMEM((PLANES, experts // PLANES, own, hidden3), BF16),
+            pltpu.VMEM((rows, width + 128), BF16),
+            *[pltpu.VMEM(shape, kind) for shape, kind in kept],
             pltpu.SemaphoreType.DMA((10,)),
-            pltpu.SemaphoreType.DMA((39, 4)),
-            pltpu.SemaphoreType.DMA((39, 4)),
+            pltpu.SemaphoreType.DMA((6,)),
+            pltpu.SemaphoreType.DMA((43, 4)),
+            pltpu.SemaphoreType.DMA((43, 4)),
         ],
         compiler_params=pltpu.CompilerParams(
-            collective_id=collective, has_side_effects=True, vmem_limit_bytes=56 * 2**20
+            collective_id=collective, has_side_effects=True, vmem_limit_bytes=60 * 2**20
         ),
         name="start",
-    )(tok, ids, wq, wo, we, cot, cosine, sine)[:-1]
+    )(tok, wq, wo, seq, routes, misc, up, down, cot, *tables)[:-1]
 
 
 def add_blocks(out, *terms):
@@ -1826,7 +1906,7 @@
     )(outs, outs_one, grads, *saved, *tables, *at_rows)
 
 
-def widen_kernel(table, q, o, up_o, down_o, qkv_o, out_o, misc_o):
+def widen_kernel(table, q, o, up_o, down_o, qkv_o, out_o, misc_o, router_o):
     columns = table.shape[2]
     split = up_o.shape[2]
     size = WINDOW * HEAD_DIM
@@ -1848,6 +1928,7 @@
     for plane in range(1, PLANES):
         total = total + q[plane, :, 3 * size :].astype(F32)
     misc_o[...] = total
+    router_o[...] = total[:, 1 : 1 + router_o.shape[1]]
 
 
 def widen(table, q, o):
@@ -1861,6 +1942,7 @@
         (rows, 3 * width),
         (rows, width),
         (rows, 128),
+        (rows, experts - 1),
     ]
     return pl.pallas_call(
         widen_kernel,
@@ -1895,6 +1977,17 @@
     return lax.dot_general(a, b, ((dims[0], dims[1]), ((), ())), preferred_element_type=F32).astype(out)
 
 
+def rotary_tables(seqlen):
+    half_dim = HEAD_DIM // 2
+    frequency = 10000.0 ** (-np.arange(half_dim, dtype=np.float32) / half_dim)
+    angles = np.arange(seqlen, dtype=np.float32)[:, None] * frequency[None, :].astype(np.float32)
+    cosine, sine = np.cos(angles), np.sin(angles)
+    return (
+        jnp.asarray(np.concatenate([cosine, cosine], axis=1), F32),
+        jnp.asarray(np.concatenate([-sine, sine], axis=1), F32),
+    )
+
+
 def expert_local(
     tokens, seq_ids, routes, cotangent, gain_attn, w_qkv, w_out, gain_ffn, w_router, w_up, w_down
 ):
@@ -1914,33 +2007,14 @@
         ],
         axis=1,
     )
-    wq_send = jnp.concatenate(
-        [windows(w_qkv[:, i * width : (i + 1) * width]) for i in range(3)]
-        + [jnp.broadcast_to(misc[None], (PLANES, own, 128))],
-        axis=2,
-    )
-    we_send = jnp.concatenate([w_up, w_down], axis=2).reshape(own, 4, PLANES, 3 * FF)
-    we_send = jnp.transpose(we_send, (2, 1, 0, 3))
-    choose = routes[:, :, None] == jnp.arange(experts, dtype=jnp.int32)[None, None, :]
-    member = jnp.any(choose, axis=1)
-    member_cols = jnp.concatenate(
-        [jnp.ones((rows, 1), BF16), member.astype(BF16), jnp.zeros((rows, 127 - experts), BF16)],
-        axis=1,
-    )
-    cot_send = jnp.concatenate([cotangent, member_cols], axis=1)
-    ids_f = seq_ids.astype(BF16)
-    ids_send = jnp.concatenate(
-        [
-            jnp.broadcast_to(ids_f[None, :], (rows, rows)),
-            jnp.broadcast_to(ids_f[:, None], (rows, rows)),
-        ]
-    )
-    half_dim = HEAD_DIM // 2
-    cosine, sine_table = rotary(jnp.arange(seqlen, dtype=F32), HEAD_DIM)
-    sine_signed = sine_table[:, 0, :] * jnp.where(jnp.arange(HEAD_DIM) < half_dim, -1.0, 1.0)
-    we_all, cot_all, wq_all, out_weight, first_in, qkv, weights_exact, mixed_exact, mixed, middle, second_in = start(
-        tokens, ids_send, wq_send, w_out, we_send, cot_send, cosine[:, 0, :], sine_signed, 1
-    )
+    tables = rotary_tables(seqlen)
+    (
+        we_all, cot_all, wq_all, out_weight, first_in, qkv, weights_exact, mixed_exact, mixed, middle,
+        second_in,
+    ) = start(
+        tokens, w_qkv, w_out, seq_ids[None, :], routes, misc, w_up, w_down, cotangent, tables, 1
+    )
+
     weights = we_all.reshape(width, 3 * FF)
     grads, outs, outs_one, sums = run_experts(second_in, cot_all, weights, wq_all, 3)
 
@@ -1949,11 +2023,11 @@
         outs_one,
         grads.reshape(PLANES, 2, width // PLANES // 2, 3 * FF),
         (weights_exact, mixed_exact, qkv, first_in, wq_all, out_weight),
-        (cosine[:, 0, :], sine_signed),
+        tables,
         (mixed, sums, second_in, middle, cotangent, tokens),
         6,
     )
-    up_sum, down_sum, qkv_sum, out_sum, misc_sum = widen(
+    up_sum, down_sum, qkv_sum, out_sum, misc_sum, router_sum = widen(
         table.reshape(experts + 1, width // PLANES, 3 * FF), q_all, o_all
     )
     return (
@@ -1963,7 +2037,7 @@
         qkv_sum,
         out_sum,
         misc_sum[:, experts + 2],
-        misc_sum[:, 1 : experts + 1],
+        router_sum,
         up_sum,
         down_sum,
     )

time: 539 us -> 529 us (0.981)
  other arithmetic: 5.44 us -> 0 us
where the time goes in v6:
time: 529 us; the launch traced here: 526 us
  Pallas kernels  516 us (98%)
  local copies, waits for them, and re-layouts  9.36 us (2%)
    pallas_call x1, Pallas kernels, finish(): pl.pallas_call(finish_kernel, out_shape=[jax.ShapeDtypeStruct((rows, widt...  200 us
    pallas_call x1, Pallas kernels, start(): pl.pallas_call(start_kernel, out_shape=[jax.ShapeDtypeStruct(shape, kind)...  156 us
    pallas_call x1, Pallas kernels, run_experts(): pl.pallas_call(experts_kernel, out_shape=[jax.ShapeDtypeStruct((width, 3...  130 us
    pallas_call x1, Pallas kernels, widen(): pl.pallas_call(widen_kernel, grid=(rows // step,), out_shape=[jax.ShapeDt...  30.1 us

profile of v6, /device:TPU:29, one launch (start us, length us, event | category | flops | bytes accessed | tf_op | source)
XLA Modules:
  0.0 525.9 jit_solution(15439031341508944038)
XLA Ops:
  0.6 0.8 copy.28
  1.4 0.8 copy.29
  2.1 0.8 copy.27
  2.9 0.7 concatenate.3.misc_in
  3.6 1.4 copy.30.routes_in
  5.1 156.1 %start.1 = (bf16[8,4,40,2688]{3,2,1,0:T(8,128)(2,1)}, bf16[4,4,128,1408]{3,2,1,0:T(8,128)(2,1)}, bf16[1280,1280]{1,0:T(8,128)(2,1)}, bf16[1280,1280]{1,0:T(8,128...) custom-call(bf16[128,1280]{1,0:T(8,128)(2,1)} %tok_in.3, ...), custom_call_target="tpu_custom_call" | custom-call | tf_op jit(solution)/shard_map/start/pallas_call | solution.py:988
  161.2 129.9 %experts.1 = (bf16[1280,2688]{1,0:T(8,128)(2,1)}, bf16[4,4,128,1280]{3,2,1,0:T(8,128)(2,1)}, bf16[4,2,128,1280]{3,2,1,0:T(8,128)(2,1)}, f32[128,1408]{1,0:T(8,128)}) custom-call(bf16[128,1280]{1,0:T(8,128)(2,1)} %get-tuple-element.35.x_in.second_in, bf16[4,4,128,1408]{3,2,1,0:T(8,128)(2,1)} %get-tuple-element.36.cot_in, bf16[1280,2688]{1,0:T(8,128)(2,1)} %bitcast.7, ...), custom_call_target="tpu_custom_call" | custom-call | tf_op jit(solution)/shard_map/experts/pallas_call | solution.py:1386
  291.1 199.8 %finish.1 = (bf16[128,1280]{1,0:T(8,128)(2,1)}, bf16[128,1280]{1,0:T(8,128)(2,1)}, bf16[4,4,2,160,2688]{4,3,2,1,0:T(8,128)(2,1)}, bf16[4,320,1280]{2,1,0:T(8,128)(2,1)}, bf16[320,1280]{1,0:T(8,128)(2,1)}) custom-call(bf16[4,4,128,1280]{3,2,1,0:T(8,128)(2,1)} %get-tuple-element.39.outs_in, bf16[4,2,128,1280]{3,2,1,0:T(8,128)(2,1)} %get-tuple-element.40.outs_one_in, ...), custom_call_target="tpu_custom_call" | custom-call | tf_op jit(solution)/shard_map/finish/pallas_call | solution.py:1861
  490.9 0.0 copy-start.1
  490.9 0.0 copy-start
  490.9 30.1 %widen.1 = (f32[320,16,1792]{2,1,0:T(8,128)}, f32[320,16,896]{2,1,0:T(8,128)}, f32[320,3840]{1,0:T(8,128)}, f32[320,1280]{1,0:T(8,128)}, f32[320,128]{1,0:T(8,128)}, /*index=5*/f32[320,15]{1,0:T(8,128)}) custom-call(bf16[16,320,2688]{2,1,0:T(8,128)(2,1)} %bitcast.6, bf16[4,320,1280]{2,1,0:T(8,128)(2,1)} %get-tuple-element.53.q, ...), custom_call_target="tpu_custom_call" | custom-call | tf_op jit(solution)/shard_map/widen/pallas_call | solution.py:1947
  521.0 1.9 slice_reduce_fusion
  522.8 1.6 copy.31
  524.5 0.0 copy-done.1
  524.5 0.7 copy.34
  525.2 0.0 copy-done
  525.2 0.7 copy.35
  (2 shorter events, 0.0 us)
Async XLA Ops:
  490.9 33.6 %copy-start.1 = (bf16[128,1280]{1,0:T(8,128)(2,1)S(1)}, bf16[128,1280]{1,0:T(8,128)(2,1)}, u32[]{:S(2)}) copy-start(bf16[128,1280]{1,0:T(8,128)(2,1)} %get-tuple-element.90) | copy-start | bytes 983044
  490.9 34.3 %copy-start = (bf16[128,1280]{1,0:T(8,128)(2,1)S(1)}, bf16[128,1280]{1,0:T(8,128)(2,1)}, u32[]{:S(2)}) copy-start(bf16[128,1280]{1,0:T(8,128)(2,1)} %get-tuple-element.91) | copy-start | bytes 983044

commit v7 on v6

--- a/solution.py
+++ b/solution.py
@@ -613,11 +613,11 @@
 
 
 def start_kernel(
-    tok_in, wq_in, wo_in, seq_in, routes_in, misc_in, up_in, down_in, cot_in, cos_in, sin_in,
+    tok_in, wq_in, wo_in, seq_in, routes_in, router_in, gains_in, up_in, down_in, cot_in, cos_in, sin_in,
     we_o, cot_o, wq_out, wo_out, first_out, qkv_out, exact_out, mixed_out, mixed_rows_o, middle_o,
     second_o, hop,
     tok, ids, wq_blocks, wo_blocks, staged, mask, mixed_got, mixed_send, ids_in, we_in, cot_full,
-    wq_o, wo_o, first_o, qkv_o, exact_o, mixed_o,
+    columns, misc_in, wq_o, wo_o, first_o, qkv_o, exact_o, mixed_o,
     load_sems, out_sems, send_sems, recv_sems,
 ):
     links = Links(send_sems, recv_sems)
@@ -658,6 +658,11 @@
 
     for kind in range(3):
         wq_own(kind).start()
+    routed = router_in.shape[0]
+    columns[...] = jnp.zeros(columns.shape, F32)
+    columns[1 : routed + 1, :own] = router_in[...].astype(F32)
+    columns[routed + 1 : routed + 3, :own] = gains_in[...].astype(F32)
+    misc_in[...] = jnp.transpose(columns[...])[:own, :].astype(BF16)
     wq_blocks[w, z, :, 3 * size :] = misc_in[...]
     row_ids = jnp.broadcast_to(seq_in[...].astype(F32), (rows, rows))
     ids_in[:rows, :] = row_ids.astype(BF16)
@@ -758,12 +763,12 @@
     for keep in keeps[:2]:
         keep.wait()
 
-    lane = lax.broadcasted_iota(jnp.int32, (rows, 128), 1)
-    member = lane == 0
-    for route in range(routes_in.shape[1]):
-        member = member | (lane == routes_in[:, route : route + 1] + 1)
+    expert = lax.broadcasted_iota(jnp.int32, (128, rows), 0)
+    member = expert == 0
+    for route in range(routes_in.shape[0]):
+        member = member | (expert == routes_in[route : route + 1, :] + 1)
     cot_full[:, :width] = cot_in[...]
-    cot_full[:, width:] = member.astype(F32).astype(BF16)
+    cot_full[:, width:] = jnp.transpose(member.astype(F32)).astype(BF16)
     keeps[2].start()
     tok_chain.arrive(0)
     ids_chain.arrive(0)
@@ -958,7 +963,7 @@
     return tok[z, :, here].astype(F32)
 
 
-def start(tok, wq, wo, seq, routes, misc, up, down, cot, tables, collective):
+def start(tok, wq, wo, seq, routes, router, gains, up, down, cot, tables, collective):
     rows, width = tok.shape
     own = wo.shape[0]
     experts = up.shape[1]
@@ -988,7 +993,7 @@
     return pl.pallas_call(
         start_kernel,
         out_shape=[jax.ShapeDtypeStruct(shape, kind) for shape, kind in shapes],
-        in_specs=[any_spec] * 3 + [vmem_spec] * 8,
+        in_specs=[any_spec] * 3 + [vmem_spec] * 9,
         out_specs=[any_spec] * 8 + [vmem_spec] * 3 + [any_spec],
         scratch_shapes=[
             pltpu.VMEM((PLANES, rows, width), BF16),
@@ -1002,6 +1007,8 @@
             pltpu.VMEM((2 * rows, rows), BF16),
             pltpu.VMEM((PLANES, experts // PLANES, own, hidden3), BF16),
             pltpu.VMEM((rows, width + 128), BF16),
+            pltpu.VMEM((128, 128), F32),
+            pltpu.VMEM((own, 128), BF16),
             *[pltpu.VMEM(shape, kind) for shape, kind in kept],
             pltpu.SemaphoreType.DMA((10,)),
             pltpu.SemaphoreType.DMA((6,)),
@@ -1012,7 +1019,7 @@
             collective_id=collective, has_side_effects=True, vmem_limit_bytes=60 * 2**20
         ),
         name="start",
-    )(tok, wq, wo, seq, routes, misc, up, down, cot, *tables)[:-1]
+    )(tok, wq, wo, seq, routes, router, gains, up, down, cot, *tables)[:-1]
 
 
 def add_blocks(out, *terms):
@@ -1182,6 +1189,7 @@
         direct(step, 2).wait_recv()
         across(turn).start()
 
+    begin(3)
     begin(0)
     begin(1)
     relay(0)
@@ -1270,10 +1278,6 @@
         step = step_at(turn)
         across(turn).wait_recv()
         first_half(step)
-
-        @pl.when(turn == 0)
-        def _():
-            begin(3)
 
         @pl.when(turn < 2)
         def _():
@@ -1589,13 +1593,13 @@
             )
         )
     ]
+    for step in range(4):
+        for load in outs_loads(step):
+            load.start()
     for load in loads[:2]:
         load.start()
     for step in steps:
         grads_load(step).start()
-    for step in steps:
-        for load in outs_loads(step):
-            load.start()
     for load in loads[2:]:
         load.start()
     greet(w, z)
@@ -1607,16 +1611,16 @@
         grads_swap(step).wait_recv()
         add_blocks(grads_own.at[step], grads_own.at[step], grads_got.at[step])
 
-    grads_ready(0)
-    keep = grads_keep()
-    keep.start()
-
     def outs_cross(step):
         for load in outs_loads(step):
             load.wait()
         add_blocks(outs.at[step, 1], outs.at[step, 1], outs_one.at[step, 1])
         cross(step).start()
 
+    loop(0, 4, outs_cross)
+    grads_ready(0)
+    keep = grads_keep()
+    keep.start()
     keep.wait()
     grads_gather(3).begin()
     for load in loads[:2]:
@@ -1654,7 +1658,6 @@
         heads_ring(step).start()
     heads[z] = heads_send[z]
     loop(1, 4, grads_ready)
-    loop(0, 4, outs_cross)
     for step in (1, 2, 3):
         heads_ring(step).wait_recv()
     send_next(z, lambda step: grads_ring(step).start())
@@ -1754,7 +1757,6 @@
 
     loop(0, 4, dense_cross_start)
     loop(1, 3, grads_next)
-    loop(1, 4, lambda step: far(step).start())
 
     def dense_finish(step):
         for kind in (0, 1):
@@ -1769,6 +1771,7 @@
             dense_ring(1, step).start()
 
     loop(0, 4, dense_finish)
+    loop(1, 4, lambda step: far(step).start())
     loop(1, 4, lambda step: first_ring(step).start())
     keep = dense_keep()
     keep.start()
@@ -1997,22 +2000,23 @@
     seqlen = PLANES * rows
     size = WINDOW * HEAD_DIM
 
-    misc = jnp.concatenate(
-        [
-            jnp.zeros((own, 1), BF16),
-            w_router,
-            gain_attn[:, None],
-            gain_ffn[:, None],
-            jnp.zeros((own, 128 - experts - 3), BF16),
-        ],
-        axis=1,
-    )
     tables = rotary_tables(seqlen)
     (
         we_all, cot_all, wq_all, out_weight, first_in, qkv, weights_exact, mixed_exact, mixed, middle,
         second_in,
     ) = start(
-        tokens, w_qkv, w_out, seq_ids[None, :], routes, misc, w_up, w_down, cotangent, tables, 1
+        tokens,
+        w_qkv,
+        w_out,
+        seq_ids[None, :],
+        routes.T,
+        w_router.T,
+        jnp.stack([gain_attn, gain_ffn]),
+        w_up,
+        w_down,
+        cotangent,
+        tables,
+        1,
     )
 
     weights = we_all.reshape(width, 3 * FF)

time: 529 us -> 522 us (0.987)
  no operation moved by 1% of the time
where the time goes in v7:
time: 522 us; the launch traced here: 519 us
  Pallas kernels  512 us (98%)
    pallas_call x1, Pallas kernels, finish(): pl.pallas_call(finish_kernel, out_shape=[jax.ShapeDtypeStruct((rows, widt...  196 us
    pallas_call x1, Pallas kernels, start(): pl.pallas_call(start_kernel, out_shape=[jax.ShapeDtypeStruct(shape, kind)...  156 us
    pallas_call x1, Pallas kernels, run_experts(): pl.pallas_call(experts_kernel, out_shape=[jax.ShapeDtypeStruct((width, 3...  130 us
    pallas_call x1, Pallas kernels, widen(): pl.pallas_call(widen_kernel, grid=(rows // step,), out_shape=[jax.ShapeDt...  30.1 us

profile of v7, /device:TPU:29, one launch (start us, length us, event | category | flops | bytes accessed | tf_op | source)
XLA Modules:
  0.0 518.8 jit_solution(4944419671862574901)
XLA Ops:
  0.6 1.2 pad_maximum_fusion.gains_in
  1.8 156.1 %start.1 = (bf16[8,4,40,2688]{3,2,1,0:T(8,128)(2,1)}, bf16[4,4,128,1408]{3,2,1,0:T(8,128)(2,1)}, bf16[1280,1280]{1,0:T(8,128)(2,1)}, bf16[1280,1280]{1,0:T(8,128...) custom-call(bf16[128,1280]{1,0:T(8,128)(2,1)} %tok_in.3, ...), custom_call_target="tpu_custom_call" | custom-call | tf_op jit(solution)/shard_map/start/pallas_call | solution.py:993
  158.0 129.9 %experts.1 = (bf16[1280,2688]{1,0:T(8,128)(2,1)}, bf16[4,4,128,1280]{3,2,1,0:T(8,128)(2,1)}, bf16[4,2,128,1280]{3,2,1,0:T(8,128)(2,1)}, f32[128,1408]{1,0:T(8,128)}) custom-call(bf16[128,1280]{1,0:T(8,128)(2,1)} %get-tuple-element.35.x_in.second_in, bf16[4,4,128,1408]{3,2,1,0:T(8,128)(2,1)} %get-tuple-element.36.cot_in, bf16[1280,2688]{1,0:T(8,128)(2,1)} %bitcast.9, ...), custom_call_target="tpu_custom_call" | custom-call | tf_op jit(solution)/shard_map/experts/pallas_call | solution.py:1390
  287.9 195.8 %finish.1 = (bf16[128,1280]{1,0:T(8,128)(2,1)}, bf16[128,1280]{1,0:T(8,128)(2,1)}, bf16[4,4,2,160,2688]{4,3,2,1,0:T(8,128)(2,1)}, bf16[4,320,1280]{2,1,0:T(8,128)(2,1)}, bf16[320,1280]{1,0:T(8,128)(2,1)}) custom-call(bf16[4,4,128,1280]{3,2,1,0:T(8,128)(2,1)} %get-tuple-element.39.outs_in, bf16[4,2,128,1280]{3,2,1,0:T(8,128)(2,1)} %get-tuple-element.40.outs_one_in, ...), custom_call_target="tpu_custom_call" | custom-call | tf_op jit(solution)/shard_map/finish/pallas_call | solution.py:1864
  483.7 0.0 copy-start.1
  483.7 0.0 copy-start
  483.7 30.1 %widen.1 = (f32[320,16,1792]{2,1,0:T(8,128)}, f32[320,16,896]{2,1,0:T(8,128)}, f32[320,3840]{1,0:T(8,128)}, f32[320,1280]{1,0:T(8,128)}, f32[320,128]{1,0:T(8,128)}, /*index=5*/f32[320,15]{1,0:T(8,128)}) custom-call(bf16[16,320,2688]{2,1,0:T(8,128)(2,1)} %bitcast.8, bf16[4,320,1280]{2,1,0:T(8,128)(2,1)} %get-tuple-element.53.q, ...), custom_call_target="tpu_custom_call" | custom-call | tf_op jit(solution)/shard_map/widen/pallas_call | solution.py:1950
  513.8 1.9 slice_reduce_fusion
  515.7 1.6 copy.23
  517.3 0.0 copy-done.1
  517.3 0.7 copy.26
  518.1 0.0 copy-done
  518.1 0.7 copy.27
Async XLA Ops:
  483.7 33.6 %copy-start.1 = (bf16[128,1280]{1,0:T(8,128)(2,1)S(1)}, bf16[128,1280]{1,0:T(8,128)(2,1)}, u32[]{:S(2)}) copy-start(bf16[128,1280]{1,0:T(8,128)(2,1)} %get-tuple-element.90) | copy-start | bytes 983044
  483.7 34.3 %copy-start = (bf16[128,1280]{1,0:T(8,128)(2,1)S(1)}, bf16[128,1280]{1,0:T(8,128)(2,1)}, u32[]{:S(2)}) copy-start(bf16[128,1280]{1,0:T(8,128)(2,1)} %get-tuple-element.91) | copy-start | bytes 983044

commit v8 on v7

--- a/solution.py
+++ b/solution.py
@@ -1290,11 +1290,12 @@
         second_half(turn, step)
         outs_out(turn).start()
 
+        near(turn, 1).start()
+
         @pl.when(turn > 0)
         def _():
             send_cross(turn - 1)
 
-        near(turn, 1).start()
         near(turn, 0).start()
 
         @pl.when(turn > 1)

time: 522 us -> 519 us (level)
  no operation moved by 1% of the time
where the time goes in v8:
time: 519 us; the launch traced here: 516 us
  Pallas kernels  509 us (98%)
    pallas_call x1, Pallas kernels, finish(): pl.pallas_call(finish_kernel, out_shape=[jax.ShapeDtypeStruct((rows, widt...  191 us
    pallas_call x1, Pallas kernels, start(): pl.pallas_call(start_kernel, out_shape=[jax.ShapeDtypeStruct(shape, kind)...  156 us
    pallas_call x1, Pallas kernels, run_experts(): pl.pallas_call(experts_kernel, out_shape=[jax.ShapeDtypeStruct((width, 3...  132 us
    pallas_call x1, Pallas kernels, widen(): pl.pallas_call(widen_kernel, grid=(rows // step,), out_shape=[jax.ShapeDt...  30.1 us

profile of v8, /device:TPU:29, one launch (start us, length us, event | category | flops | bytes accessed | tf_op | source)
XLA Modules:
  0.0 515.7 jit_solution(11038260200068711656)
XLA Ops:
  0.6 1.2 pad_maximum_fusion.gains_in
  1.8 156.1 %start.1 = (bf16[8,4,40,2688]{3,2,1,0:T(8,128)(2,1)}, bf16[4,4,128,1408]{3,2,1,0:T(8,128)(2,1)}, bf16[1280,1280]{1,0:T(8,128)(2,1)}, bf16[1280,1280]{1,0:T(8,128...) custom-call(bf16[128,1280]{1,0:T(8,128)(2,1)} %tok_in.3, ...), custom_call_target="tpu_custom_call" | custom-call | tf_op jit(solution)/shard_map/start/pallas_call | solution.py:993
  158.0 131.8 %experts.1 = (bf16[1280,2688]{1,0:T(8,128)(2,1)}, bf16[4,4,128,1280]{3,2,1,0:T(8,128)(2,1)}, bf16[4,2,128,1280]{3,2,1,0:T(8,128)(2,1)}, f32[128,1408]{1,0:T(8,128)}) custom-call(bf16[128,1280]{1,0:T(8,128)(2,1)} %get-tuple-element.35.x_in.second_in, bf16[4,4,128,1408]{3,2,1,0:T(8,128)(2,1)} %get-tuple-element.36.cot_in, bf16[1280,2688]{1,0:T(8,128)(2,1)} %bitcast.9, ...), custom_call_target="tpu_custom_call" | custom-call | tf_op jit(solution)/shard_map/experts/pallas_call | solution.py:1391
  289.7 190.9 %finish.1 = (bf16[128,1280]{1,0:T(8,128)(2,1)}, bf16[128,1280]{1,0:T(8,128)(2,1)}, bf16[4,4,2,160,2688]{4,3,2,1,0:T(8,128)(2,1)}, bf16[4,320,1280]{2,1,0:T(8,128)(2,1)}, bf16[320,1280]{1,0:T(8,128)(2,1)}) custom-call(bf16[4,4,128,1280]{3,2,1,0:T(8,128)(2,1)} %get-tuple-element.39.outs_in, bf16[4,2,128,1280]{3,2,1,0:T(8,128)(2,1)} %get-tuple-element.40.outs_one_in, ...), custom_call_target="tpu_custom_call" | custom-call | tf_op jit(solution)/shard_map/finish/pallas_call | solution.py:1865
  480.6 0.0 copy-start.1
  480.6 0.0 copy-start
  480.7 30.1 %widen.1 = (f32[320,16,1792]{2,1,0:T(8,128)}, f32[320,16,896]{2,1,0:T(8,128)}, f32[320,3840]{1,0:T(8,128)}, f32[320,1280]{1,0:T(8,128)}, f32[320,128]{1,0:T(8,128)}, /*index=5*/f32[320,15]{1,0:T(8,128)}) custom-call(bf16[16,320,2688]{2,1,0:T(8,128)(2,1)} %bitcast.8, bf16[4,320,1280]{2,1,0:T(8,128)(2,1)} %get-tuple-element.53.q, ...), custom_call_target="tpu_custom_call" | custom-call | tf_op jit(solution)/shard_map/widen/pallas_call | solution.py:1951
  510.7 1.9 slice_reduce_fusion
  512.6 1.6 copy.23
  514.2 0.0 copy-done.1
  514.2 0.7 copy.26
  515.0 0.0 copy-done
  515.0 0.7 copy.27
Async XLA Ops:
  480.6 33.6 %copy-start.1 = (bf16[128,1280]{1,0:T(8,128)(2,1)S(1)}, bf16[128,1280]{1,0:T(8,128)(2,1)}, u32[]{:S(2)}) copy-start(bf16[128,1280]{1,0:T(8,128)(2,1)} %get-tuple-element.90) | copy-start | bytes 983044
  480.6 34.3 %copy-start = (bf16[128,1280]{1,0:T(8,128)(2,1)S(1)}, bf16[128,1280]{1,0:T(8,128)(2,1)}, u32[]{:S(2)}) copy-start(bf16[128,1280]{1,0:T(8,128)(2,1)} %get-tuple-element.91) | copy-start | bytes 983044
